TPU v7x, 128 devices: a whole 4x4x4 slice. The times are simulated.
128 devices in a mesh: prow: 16 (over z, y), pcol: 8 (over x, core).
Axes of the slice: x: 4, y: 4, z: 4, core: 2. Of those that a mesh axis runs over, the one named last changes fastest.
Arguments:
- rhs: float32 [8, 16, 64, 128], P(None, 'prow'), may hold values from -6 to 6
- lower: float32 [8, 16, 16, 8, 128, 128], P(None, 'prow', None, 'pcol'), may hold values from -0.25 to 0.25
- upper: float32 [8, 16, 16, 8, 128, 128], P(None, 'prow', None, 'pcol'), may hold values from -0.25 to 0.25
- lower_inverse: float32 [8, 16, 128, 128], P(None, 'prow'), as said below
- upper_inverse: float32 [8, 16, 128, 128], P(None, 'prow'), as said below
- pattern: int32 [128, 128], replicated, may hold values from 0 to 1, as said below
- levels: int32 [128], replicated, may hold values from 0 to 5, as said below
- widths: int32 [128], replicated, may hold values from 64 to 128
Outputs:
- forward: float32 [8, 16, 64, 128], P(None, 'prow')
- solution: float32 [8, 16, 64, 128], P(None, 'prow')
Inputs may be any that keep to these rules, and one draw needn't show every extreme that they name: `lower_inverse`: each inverse has diagonal entries between 0.5 and 2 plus a dense random part of standard deviation 0.4 / sqrt(128). `upper_inverse`: each inverse has diagonal entries between 0.5 and 2 plus a dense random part of standard deviation 0.4 / sqrt(128). The supernodes form one binary elimination tree; pattern[i, j] is 1 exactly where i is a proper ancestor of j or j of i, and 0 elsewhere and on the diagonal. `levels`: A supernode's level is its height in the tree (leaves 0), capped at 5, which the root reaches; a parent's level is above its child's unless both are capped. Levels 1 to 4 each hold half as many supernodes as the one below.
All inputs are finite; a program needn't handle non-finite values.
Results may differ from a plain program's by a relative error of at most 0.00017.
Values sent between devices are 32-bit elements; how exact they have to be, the bound alone decides.
No kernel may reach another device: no remote copies, remote signals or barrier semaphores. Data moves between devices by JAX's collectives and lax.ppermute only.
A program may use at most 128 MiB of HBM per device.

v0:
```python
import jax
import jax.numpy as jnp
from jax import lax
from jax.sharding import PartitionSpec as P

LEVELS = 6


def spread(value, axis, source):
    kept = jnp.where(lax.axis_index(axis) == source, value, 0).astype(value.dtype)
    return lax.psum(kept, axis)


def apply_inverse(inverse, right):
    return jnp.einsum("akl,ahl->ahk", inverse, right, precision=lax.Precision.HIGHEST)


def solve_levels(blocks, inverse, right, valid, row_levels, mask, rising):
    prow_count = lax.axis_size("prow")
    pcol_count = lax.axis_size("pcol")
    column = lax.axis_index("pcol")
    ratio = prow_count // pcol_count
    masked = blocks * mask[:, :, None, None]
    row_state = jnp.zeros(right.shape, jnp.float32)
    col_state = jnp.zeros((masked.shape[1],) + right.shape[1:], jnp.float32)
    order = list(range(LEVELS)) if rising else list(range(LEVELS - 1, -1, -1))
    for place, level in enumerate(order):
        partial_sum = jnp.einsum(
            "ackl,chl->ahk", masked, col_state, precision=lax.Precision.HIGHEST
        )
        total = lax.psum(partial_sum, "pcol")
        fresh = apply_inverse(inverse, right - total) * valid
        current = (row_levels == level)[:, None, None]
        row_state = jnp.where(current, fresh, row_state)
        if place + 1 < LEVELS:
            pieces = []
            for offset in range(ratio):
                pieces.append(spread(row_state, "prow", column + offset * pcol_count))
            stacked = jnp.stack(pieces, axis=1)
            col_state = stacked.reshape((-1,) + right.shape[1:])
    return row_state


def local(rhs, lower, upper, lower_inverse, upper_inverse, pattern, levels, widths):
    prow_count = lax.axis_size("prow")
    pcol_count = lax.axis_size("pcol")
    row_index = lax.axis_index("prow")
    col_index = lax.axis_index("pcol")
    row_blocks = rhs.shape[0]
    col_blocks = lower.shape[2]
    width = rhs.shape[3]
    right = rhs.reshape(row_blocks, rhs.shape[2], width)
    lower_local = lower.reshape(row_blocks, col_blocks, width, width)
    upper_local = upper.reshape(row_blocks, col_blocks, width, width)
    lower_inv = lower_inverse.reshape(row_blocks, width, width)
    upper_inv = upper_inverse.reshape(row_blocks, width, width)
    row_levels = lax.dynamic_index_in_dim(
        levels.reshape(row_blocks, prow_count), row_index, 1, keepdims=False
    )
    col_levels = lax.dynamic_index_in_dim(
        levels.reshape(col_blocks, pcol_count), col_index, 1, keepdims=False
    )
    row_widths = lax.dynamic_index_in_dim(
        widths.reshape(row_blocks, prow_count), row_index, 1, keepdims=False
    )
    grid = pattern.reshape(row_blocks, prow_count, col_blocks, pcol_count)
    grid = lax.dynamic_index_in_dim(grid, row_index, 1, keepdims=False)
    grid = lax.dynamic_index_in_dim(grid, col_index, 2, keepdims=False).astype(jnp.float32)
    valid = (jnp.arange(width)[None, :] < row_widths[:, None]).astype(jnp.float32)[:, None, :]
    below = grid * (col_levels[None, :] < row_levels[:, None]).astype(jnp.float32)
    above = grid * (col_levels[None, :] > row_levels[:, None]).astype(jnp.float32)
    forward = solve_levels(lower_local, lower_inv, right, valid, row_levels, below, True)
    solution = solve_levels(upper_local, upper_inv, forward, valid, row_levels, above, False)
    shape = rhs.shape
    return (forward.reshape(shape), solution.reshape(shape))


def solution(mesh):
    in_specs = (
        P(None, "prow", None, None),
        P(None, "prow", None, "pcol", None, None),
        P(None, "prow", None, "pcol", None, None),
        P(None, "prow", None, None),
        P(None, "prow", None, None),
        P(),
        P(),
        P(),
    )
    out_specs = (P(None, "prow", None, None), P(None, "prow", None, None))
    return jax.shard_map(local, mesh=mesh, in_specs=in_specs, out_specs=out_specs, check_vma=False)
```

profile of v0, /device:TPU:1, one launch (start us, length us, event | category | flops | bytes accessed | tf_op | source)
XLA Modules:
  0.0 1693.3 jit_solution(5649968917246429695)
XLA Ops:
  8.8 0.9 copy.26
  10.6 11.2 fusion.44
  22.3 60.6 %all-reduce.33.cloned.1.call-done = f32[8,64,128]{2,1,0:T(8,128)} async-done(((f32[8,64,128]{2,1,0:T(8,128)}), f32[8,64,128]{2,1,0:T(8,128)}) %all-reduce.33.cloned.1.call-update) | async-done | bytes 262160 | tf_op jit(solution)/shard_map/psum | solution.py:31
  82.9 2.1 fusion.76
  85.0 0.8 select_bitcast_fusion.19
  85.9 86.5 %all-reduce.71.cloned.1.call-done = (f32[8,1,64,128]{3,2,0,1:T(8,128)}, f32[8,1,64,128]{3,2,0,1:T(8,128)}) async-done(((f32[8,1,64,128]{3,2,0,1:T(8,128)}, f32[8,1,64,128]{3,2,0,1:T(8,128)}), (f32[8,1,64,128]{3,2,0,1:T(8,128)}, f32[8,1,64,128]{3,2,0,1:T(8,128)})) %all-reduce.71.cloned.1.call-update) | async-done | bytes 524304 | tf_op jit(solution)/shard_map/psum | solution.py:11
  172.4 1.1 pad_maximum_fusion
  173.5 10.9 fusion.45
  184.5 58.3 %all-reduce.35.cloned.1.call-done = f32[8,64,128]{2,1,0:T(8,128)} async-done(((f32[8,64,128]{2,1,0:T(8,128)}), f32[8,64,128]{2,1,0:T(8,128)}) %all-reduce.35.cloned.1.call-update) | async-done | bytes 262160 | tf_op jit(solution)/shard_map/psum | solution.py:31
  242.8 2.1 fusion.77
  244.9 0.8 select_bitcast_fusion.17
  245.9 86.3 %all-reduce.69.cloned.1.call-done = (f32[8,1,64,128]{3,2,0,1:T(8,128)}, f32[8,1,64,128]{3,2,0,1:T(8,128)}) async-done(((f32[8,1,64,128]{3,2,0,1:T(8,128)}, f32[8,1,64,128]{3,2,0,1:T(8,128)}), (f32[8,1,64,128]{3,2,0,1:T(8,128)}, f32[8,1,64,128]{3,2,0,1:T(8,128)})) %all-reduce.69.cloned.1.call-update) | async-done | bytes 524304 | tf_op jit(solution)/shard_map/psum | solution.py:11
  332.2 1.1 pad_maximum_fusion.1
  333.3 10.9 fusion.48
  344.5 58.2 %all-reduce.37.cloned.1.call-done = f32[8,64,128]{2,1,0:T(8,128)} async-done(((f32[8,64,128]{2,1,0:T(8,128)}), f32[8,64,128]{2,1,0:T(8,128)}) %all-reduce.37.cloned.1.call-update) | async-done | bytes 262160 | tf_op jit(solution)/shard_map/psum | solution.py:31
  402.6 2.1 fusion.78
  404.7 0.8 select_bitcast_fusion.15
  405.6 86.3 %all-reduce.67.cloned.1.call-done = (f32[8,1,64,128]{3,2,0,1:T(8,128)}, f32[8,1,64,128]{3,2,0,1:T(8,128)}) async-done(((f32[8,1,64,128]{3,2,0,1:T(8,128)}, f32[8,1,64,128]{3,2,0,1:T(8,128)}), (f32[8,1,64,128]{3,2,0,1:T(8,128)}, f32[8,1,64,128]{3,2,0,1:T(8,128)})) %all-reduce.67.cloned.1.call-update) | async-done | bytes 524304 | tf_op jit(solution)/shard_map/psum | solution.py:11
  492.0 1.1 pad_maximum_fusion.2
  493.1 10.9 fusion.51
  504.1 58.3 %all-reduce.39.cloned.1.call-done = f32[8,64,128]{2,1,0:T(8,128)} async-done(((f32[8,64,128]{2,1,0:T(8,128)}), f32[8,64,128]{2,1,0:T(8,128)}) %all-reduce.39.cloned.1.call-update) | async-done | bytes 262160 | tf_op jit(solution)/shard_map/psum | solution.py:31
  562.4 2.1 fusion.79
  565.4 86.5 %all-reduce.65.cloned.1.call-done = (f32[8,1,64,128]{3,2,0,1:T(8,128)}, f32[8,1,64,128]{3,2,0,1:T(8,128)}) async-done(((f32[8,1,64,128]{3,2,0,1:T(8,128)}, f32[8,1,64,128]{3,2,0,1:T(8,128)}), (f32[8,1,64,128]{3,2,0,1:T(8,128)}, f32[8,1,64,128]{3,2,0,1:T(8,128)})) %all-reduce.65.cloned.1.call-update) | async-done | bytes 524304 | tf_op jit(solution)/shard_map/psum | solution.py:11
  651.9 1.1 pad_maximum_fusion.3
  653.0 10.9 fusion.54
  664.0 58.3 %all-reduce.41.cloned.1.call-done = f32[8,64,128]{2,1,0:T(8,128)} async-done(((f32[8,64,128]{2,1,0:T(8,128)}), f32[8,64,128]{2,1,0:T(8,128)}) %all-reduce.41.cloned.1.call-update) | async-done | bytes 262160 | tf_op jit(solution)/shard_map/psum | solution.py:31
  722.3 2.1 fusion.80
  725.5 11.2 fusion.60
  736.8 74.9 %all-reduce.63.cloned.1.call-done = (f32[8,1,64,128]{3,2,0,1:T(8,128)}, f32[8,1,64,128]{3,2,0,1:T(8,128)}) async-done(((f32[8,1,64,128]{3,2,0,1:T(8,128)}, f32[8,1,64,128]{3,2,0,1:T(8,128)}), (f32[8,1,64,128]{3,2,0,1:T(8,128)}, f32[8,1,64,128]{3,2,0,1:T(8,128)})) %all-reduce.63.cloned.1.call-update) | async-done | bytes 524304 | tf_op jit(solution)/shard_map/psum | solution.py:11
  811.7 1.1 pad_maximum_fusion.4
  812.8 10.9 fusion.57
  823.8 59.5 %all-reduce.73.cloned.1.call-done = (f32[8,64,128]{2,1,0:T(8,128)}, f32[8,64,128]{2,1,0:T(8,128)}) async-done(((f32[8,64,128]{2,1,0:T(8,128)}, f32[8,64,128]{2,1,0:T(8,128)}), (f32[8,64,128]{2,1,0:T(8,128)}, f32[8,64,128]{2,1,0:T(8,128)})) %all-reduce.73.cloned.1.call-update) | async-done | bytes 524304 | tf_op jit(solution)/shard_map/psum | solution.py:31
  883.3 2.1 fusion.81
  885.4 2.2 fusion.82
  887.6 0.9 select_bitcast_fusion.9
  888.6 85.4 %all-reduce.61.cloned.1.call-done = (f32[8,1,64,128]{3,2,0,1:T(8,128)}, f32[8,1,64,128]{3,2,0,1:T(8,128)}) async-done(((f32[8,1,64,128]{3,2,0,1:T(8,128)}, f32[8,1,64,128]{3,2,0,1:T(8,128)}), (f32[8,1,64,128]{3,2,0,1:T(8,128)}, f32[8,1,64,128]{3,2,0,1:T(8,128)})) %all-reduce.61.cloned.1.call-update) | async-done | bytes 524304 | tf_op jit(solution)/shard_map/psum | solution.py:11
  974.0 1.1 pad_maximum_fusion.5
  975.1 10.9 fusion.61
  986.1 58.3 %all-reduce.43.cloned.1.call-done = f32[8,64,128]{2,1,0:T(8,128)} async-done(((f32[8,64,128]{2,1,0:T(8,128)}), f32[8,64,128]{2,1,0:T(8,128)}) %all-reduce.43.cloned.1.call-update) | async-done | bytes 262160 | tf_op jit(solution)/shard_map/psum | solution.py:31
  1044.4 2.1 fusion.83
  1046.5 0.9 select_bitcast_fusion.7
  1047.7 86.1 %all-reduce.59.cloned.1.call-done = (f32[8,1,64,128]{3,2,0,1:T(8,128)}, f32[8,1,64,128]{3,2,0,1:T(8,128)}) async-done(((f32[8,1,64,128]{3,2,0,1:T(8,128)}, f32[8,1,64,128]{3,2,0,1:T(8,128)}), (f32[8,1,64,128]{3,2,0,1:T(8,128)}, f32[8,1,64,128]{3,2,0,1:T(8,128)})) %all-reduce.59.cloned.1.call-update) | async-done | bytes 524304 | tf_op jit(solution)/shard_map/psum | solution.py:11
  1133.8 1.1 pad_maximum_fusion.6
  1134.9 10.9 fusion.64
  1145.9 58.3 %all-reduce.45.cloned.1.call-done = f32[8,64,128]{2,1,0:T(8,128)} async-done(((f32[8,64,128]{2,1,0:T(8,128)}), f32[8,64,128]{2,1,0:T(8,128)}) %all-reduce.45.cloned.1.call-update) | async-done | bytes 262160 | tf_op jit(solution)/shard_map/psum | solution.py:31
  1204.2 2.1 fusion.84
  1206.3 0.9 select_bitcast_fusion.5
  1207.3 86.3 %all-reduce.57.cloned.1.call-done = (f32[8,1,64,128]{3,2,0,1:T(8,128)}, f32[8,1,64,128]{3,2,0,1:T(8,128)}) async-done(((f32[8,1,64,128]{3,2,0,1:T(8,128)}, f32[8,1,64,128]{3,2,0,1:T(8,128)}), (f32[8,1,64,128]{3,2,0,1:T(8,128)}, f32[8,1,64,128]{3,2,0,1:T(8,128)})) %all-reduce.57.cloned.1.call-update) | async-done | bytes 524304 | tf_op jit(solution)/shard_map/psum | solution.py:11
  1293.6 1.1 pad_maximum_fusion.7
  1294.7 10.9 fusion.67
  1305.7 58.3 %all-reduce.47.cloned.1.call-done = f32[8,64,128]{2,1,0:T(8,128)} async-done(((f32[8,64,128]{2,1,0:T(8,128)}), f32[8,64,128]{2,1,0:T(8,128)}) %all-reduce.47.cloned.1.call-update) | async-done | bytes 262160 | tf_op jit(solution)/shard_map/psum | solution.py:31
  1364.0 2.1 fusion.85
  1366.0 0.9 select_bitcast_fusion.3
  1367.0 86.3 %all-reduce.55.cloned.1.call-done = (f32[8,1,64,128]{3,2,0,1:T(8,128)}, f32[8,1,64,128]{3,2,0,1:T(8,128)}) async-done(((f32[8,1,64,128]{3,2,0,1:T(8,128)}, f32[8,1,64,128]{3,2,0,1:T(8,128)}), (f32[8,1,64,128]{3,2,0,1:T(8,128)}, f32[8,1,64,128]{3,2,0,1:T(8,128)})) %all-reduce.55.cloned.1.call-update) | async-done | bytes 524304 | tf_op jit(solution)/shard_map/psum | solution.py:11
  1453.3 1.1 pad_maximum_fusion.8
  1454.4 10.9 fusion.70
  1465.4 58.3 %all-reduce.49.cloned.1.call-done = f32[8,64,128]{2,1,0:T(8,128)} async-done(((f32[8,64,128]{2,1,0:T(8,128)}), f32[8,64,128]{2,1,0:T(8,128)}) %all-reduce.49.cloned.1.call-update) | async-done | bytes 262160 | tf_op jit(solution)/shard_map/psum | solution.py:31
  1523.8 2.1 fusion.86
  1525.8 0.9 select_bitcast_fusion.1
  1527.3 85.9 %all-reduce.53.cloned.1.call-done = (f32[8,1,64,128]{3,2,0,1:T(8,128)}, f32[8,1,64,128]{3,2,0,1:T(8,128)}) async-done(((f32[8,1,64,128]{3,2,0,1:T(8,128)}, f32[8,1,64,128]{3,2,0,1:T(8,128)}), (f32[8,1,64,128]{3,2,0,1:T(8,128)}, f32[8,1,64,128]{3,2,0,1:T(8,128)})) %all-reduce.53.cloned.1.call-update) | async-done | bytes 524304 | tf_op jit(solution)/shard_map/psum | solution.py:11
  1613.1 1.1 pad_maximum_fusion.9
  1614.2 10.9 fusion.73
  1625.2 58.3 %all-reduce.51.cloned.1.call-done = f32[8,64,128]{2,1,0:T(8,128)} async-done(((f32[8,64,128]{2,1,0:T(8,128)}), f32[8,64,128]{2,1,0:T(8,128)}) %all-reduce.51.cloned.1.call-update) | async-done | bytes 262160 | tf_op jit(solution)/shard_map/psum | solution.py:31
  1683.5 2.8 fusion.88
  (76 shorter events, 7.2 us)
Async XLA Ops:
  7.2 75.7 %copy-start = (f32[8,1,128,128]{3,2,1,0:T(8,128)S(1)}, f32[8,1,128,128]{3,2,1,0:T(8,128)}, u32[]{:S(2)}) copy-start(f32[8,1,128,128]{3,2,1,0:T(8,128)} %param.11) | copy-start | bytes 1572868
  7.2 14.7 copy-start.4
  7.2 75.7 %copy-start.3 = (f32[8,1,64,128]{3,2,1,0:T(8,128)S(1)}, f32[8,1,64,128]{3,2,1,0:T(8,128)}, u32[]{:S(2)}) copy-start(f32[8,1,64,128]{3,2,1,0:T(8,128)} %param.8) | copy-start | bytes 786436
  7.2 75.7 %all-reduce.33.cloned.1.call-start = ((), (), s32[]{:S(2)}) async-start(), calls=%async_computation | async-start | bytes 524288 | tf_op jit(solution)/shard_map/psum | solution.py:31
  21.8 150.5 %all-reduce.71.cloned.1.call-start = ((), (), s32[]{:S(2)}) async-start(), calls=%async_computation.19 | async-start | bytes 1048576 | tf_op jit(solution)/shard_map/psum | solution.py:11
  85.8 157.0 %all-reduce.35.cloned.1.call-start = ((), (), s32[]{:S(2)}) async-start(), calls=%async_computation.1 | async-start | bytes 524288 | tf_op jit(solution)/shard_map/psum | solution.py:31
  184.5 147.7 %all-reduce.69.cloned.1.call-start = ((), (), s32[]{:S(2)}) async-start(), calls=%async_computation.18 | async-start | bytes 1048576 | tf_op jit(solution)/shard_map/psum | solution.py:11
  245.8 156.8 %all-reduce.37.cloned.1.call-start = ((), (), s32[]{:S(2)}) async-start(), calls=%async_computation.2 | async-start | bytes 524288 | tf_op jit(solution)/shard_map/psum | solution.py:31
  344.3 147.7 %all-reduce.67.cloned.1.call-start = ((), (), s32[]{:S(2)}) async-start(), calls=%async_computation.17 | async-start | bytes 1048576 | tf_op jit(solution)/shard_map/psum | solution.py:11
  405.6 156.8 %all-reduce.39.cloned.1.call-start = ((), (), s32[]{:S(2)}) async-start(), calls=%async_computation.3 | async-start | bytes 524288 | tf_op jit(solution)/shard_map/psum | solution.py:31
  504.1 147.8 %all-reduce.65.cloned.1.call-start = ((), (), s32[]{:S(2)}) async-start(), calls=%async_computation.16 | async-start | bytes 1048576 | tf_op jit(solution)/shard_map/psum | solution.py:11
  565.3 157.0 %all-reduce.41.cloned.1.call-start = ((), (), s32[]{:S(2)}) async-start(), calls=%async_computation.4 | async-start | bytes 524288 | tf_op jit(solution)/shard_map/psum | solution.py:31
  664.0 147.7 %all-reduce.63.cloned.1.call-start = ((), (), s32[]{:S(2)}) async-start(), calls=%async_computation.15 | async-start | bytes 1048576 | tf_op jit(solution)/shard_map/psum | solution.py:11
  725.3 158.0 %all-reduce.73.cloned.1.call-start = ((), (), s32[]{:S(2)}) async-start(), calls=%async_computation.20 | async-start | bytes 1048576 | tf_op jit(solution)/shard_map/psum | solution.py:31
  736.8 148.7 %copy-start.1 = (f32[8,1,128,128]{3,2,1,0:T(8,128)S(1)}, f32[8,1,128,128]{3,2,1,0:T(8,128)}, u32[]{:S(2)}) copy-start(f32[8,1,128,128]{3,2,1,0:T(8,128)} %param.12) | copy-start | bytes 1572868
  823.8 150.2 %all-reduce.61.cloned.1.call-start = ((), (), s32[]{:S(2)}) async-start(), calls=%async_computation.14 | async-start | bytes 1048576 | tf_op jit(solution)/shard_map/psum | solution.py:11
  885.4 798.1 %copy-start.2 = (f32[8,64,128]{2,1,0:T(8,128)}, f32[8,64,128]{2,1,0:T(8,128)S(1)}, u32[]{:S(2)}) copy-start(f32[8,64,128]{2,1,0:T(8,128)S(1)} %fusion.81) | copy-start | bytes 786436
  888.5 155.9 %all-reduce.43.cloned.1.call-start = ((), (), s32[]{:S(2)}) async-start(), calls=%async_computation.5 | async-start | bytes 524288 | tf_op jit(solution)/shard_map/psum | solution.py:31
  986.1 147.7 %all-reduce.59.cloned.1.call-start = ((), (), s32[]{:S(2)}) async-start(), calls=%async_computation.13 | async-start | bytes 1048576 | tf_op jit(solution)/shard_map/psum | solution.py:11
  1047.4 156.8 %all-reduce.45.cloned.1.call-start = ((), (), s32[]{:S(2)}) async-start(), calls=%async_computation.6 | async-start | bytes 524288 | tf_op jit(solution)/shard_map/psum | solution.py:31
  1145.9 147.7 %all-reduce.57.cloned.1.call-start = ((), (), s32[]{:S(2)}) async-start(), calls=%async_computation.12 | async-start | bytes 1048576 | tf_op jit(solution)/shard_map/psum | solution.py:11
  1207.2 156.7 %all-reduce.47.cloned.1.call-start = ((), (), s32[]{:S(2)}) async-start(), calls=%async_computation.7 | async-start | bytes 524288 | tf_op jit(solution)/shard_map/psum | solution.py:31
  1305.7 147.6 %all-reduce.55.cloned.1.call-start = ((), (), s32[]{:S(2)}) async-start(), calls=%async_computation.11 | async-start | bytes 1048576 | tf_op jit(solution)/shard_map/psum | solution.py:11
  1366.9 156.8 %all-reduce.49.cloned.1.call-start = ((), (), s32[]{:S(2)}) async-start(), calls=%async_computation.8 | async-start | bytes 524288 | tf_op jit(solution)/shard_map/psum | solution.py:31
  1465.4 147.7 %all-reduce.53.cloned.1.call-start = ((), (), s32[]{:S(2)}) async-start(), calls=%async_computation.10 | async-start | bytes 1048576 | tf_op jit(solution)/shard_map/psum | solution.py:11
  1526.7 156.8 %all-reduce.51.cloned.1.call-start = ((), (), s32[]{:S(2)}) async-start(), calls=%async_computation.9 | async-start | bytes 524288 | tf_op jit(solution)/shard_map/psum | solution.py:31
Sparse Core Ops, SparseCore 0:
  22.0 60.8 all-reduce.32
  87.1 85.2 all-reduce.70
  184.6 58.2 all-reduce.34
  246.9 85.2 all-reduce.68
  344.4 58.2 all-reduce.36
  406.7 85.2 all-reduce.66
  504.2 58.1 all-reduce.38
  566.6 85.2 all-reduce.64
  664.1 58.2 all-reduce.40
  726.4 85.2 all-reduce.62
  823.9 59.3 all-reduce.72
  888.6 85.2 all-reduce.60
  986.2 58.2 all-reduce.42
  1048.5 85.2 all-reduce.58
  1146.0 58.2 all-reduce.44
  1208.3 85.2 all-reduce.56
  1305.8 58.1 all-reduce.46
  1368.0 85.2 all-reduce.54
  1465.5 58.2 all-reduce.48
  1527.8 85.2 all-reduce.52
  1625.3 58.1 all-reduce.50
where the time goes:
time: 1700 us; the launch traced here: 1690 us
  waiting for transfers between devices  1500 us (88%)
  matrix products  158 us (9%)
  other arithmetic  19.3 us (1%)
    psum x10, waiting for transfers between devices, spread(): return lax.psum(kept, axis)  851 us
    psum x11, waiting for transfers between devices, solve_levels(): total = lax.psum(partial_sum, 'pcol')  645 us
    dot_general x12, matrix products, solve_levels(): jnp.einsum('ackl,chl->ahk', masked, col_state, precision=lax.Precision.HI...  132 us
  transfers between devices with their start and end apart: 21, of which 21 were waited for; matrix products, arithmetic and copies ran while one was open for 1% of the time, Pallas kernels for 0%

commit v1 on v0

--- a/solution.py
+++ b/solution.py
@@ -1,9 +1,28 @@
 import jax
 import jax.numpy as jnp
 from jax import lax
+from jax.experimental import pallas as pl
+from jax.experimental.pallas import tpu as pltpu
 from jax.sharding import PartitionSpec as P
 
 LEVELS = 6
+W = 128
+NRHS = 64
+NB = 128
+RB = 8
+CB = 16
+PR = 16
+PC = 8
+HS = NRHS // PC
+CAP_L = 12
+CAP_U = 28
+LIST = 64
+HBM = pl.BlockSpec(memory_space=pltpu.HBM)
+SMEM = pl.BlockSpec(memory_space=pltpu.SMEM)
+VMEM = pl.BlockSpec(memory_space=pltpu.VMEM)
+LEVEL, WIDTH, START_L, END_L, START_U, END_U = range(6)
+LIST_L, LIST_U, LIST_T, PACK_L, PACK_U, COUNTS = range(8, 14)
+SAME_CORE = [[2 * x + c for x in range(PC // 2)] for c in range(2)]
 
 
 def spread(value, axis, source):
@@ -41,7 +60,7 @@
     return row_state
 
 
-def local(rhs, lower, upper, lower_inverse, upper_inverse, pattern, levels, widths):
+def general(rhs, lower, upper, lower_inverse, upper_inverse, pattern, levels, widths):
     prow_count = lax.axis_size("prow")
     pcol_count = lax.axis_size("pcol")
     row_index = lax.axis_index("prow")
@@ -75,6 +94,351 @@
     return (forward.reshape(shape), solution.reshape(shape))
 
 
+def dot3(x, w):
+    m = x.shape[0]
+    xh = x.astype(jnp.bfloat16).astype(jnp.float32)
+    xs = jnp.concatenate([xh, x - xh], axis=0).astype(jnp.bfloat16)
+    wh = w.astype(jnp.bfloat16)
+    wl = (w - wh.astype(jnp.float32)).astype(jnp.bfloat16)
+    dims = (((1,), (1,)), ((), ()))
+    a = lax.dot_general(xs, wl, dims, preferred_element_type=jnp.float32)
+    b = lax.dot_general(xs, wh, dims, preferred_element_type=jnp.float32)
+    return (a[m:] + a[:m]) + (b[m:] + b[:m])
+
+
+def iota(shape, dim):
+    return lax.broadcasted_iota(jnp.int32, shape, dim)
+
+
+def flag(cond):
+    return jnp.where(cond, 1.0, 0.0)
+
+
+def table_kernel(pattern, levels, widths, out):
+    p = lax.axis_index("prow")
+    q = lax.axis_index("pcol")
+    lev = levels[...].astype(jnp.float32)
+    wid = widths[...].astype(jnp.float32)
+    i = iota((NB, NB), 0)
+    j = iota((NB, NB), 1)
+    lev_col = jnp.sum(jnp.where(i == j, lev, 0.0), axis=1, keepdims=True)
+    linked = flag(pattern[...] > 0)
+    low = linked * flag(lev < lev_col)
+    high = linked * flag(lev > lev_col)
+    near = low * flag((lev_col < 2.5) | (lev > 2.5))
+    far = low - near
+    same = flag((i & (PC - 1)) == (j & (PC - 1)))
+    ahead = flag(i < j)
+    same_ahead = same * ahead
+
+    def dot(x, y):
+        return jnp.dot(x, y, preferred_element_type=jnp.float32)
+
+    by_row = flag((iota((PR, NB), 1) & (PR - 1)) == iota((PR, NB), 0))
+
+    def over(full, cap):
+        rows = dot(by_row, full)
+        most = jnp.max(jnp.max(dot(rows, same), axis=1, keepdims=True), axis=0, keepdims=True)
+        listed = jnp.max(jnp.sum(rows, axis=1, keepdims=True), axis=0, keepdims=True)
+        return flag((most > cap) | (listed > LIST))
+
+    full = jnp.maximum(over(near, CAP_L), over(high, CAP_U))
+
+    lane = iota((RB, NB), 1)
+    sub = iota((RB, NB), 0)
+    mine = flag(lane == sub * PR + p)
+    row_lev = jnp.sum(mine * lev, axis=1, keepdims=True)
+    row_wid = jnp.sum(mine * wid, axis=1, keepdims=True)
+    col = lane & (PC - 1)
+    own = flag(col == q)
+    node = lane.astype(jnp.float32)
+    spot = (sub * CB + (lane >> 3)).astype(jnp.float32)
+
+    def ranks(sel):
+        total = jnp.zeros((1, NB), jnp.float32)
+        rows = []
+        for a in range(RB):
+            rows.append(total)
+            total = total + sel[a : a + 1]
+        prior = jnp.concatenate(rows, axis=0)
+        start = jnp.sum(prior, axis=1, keepdims=True)
+        end = start + jnp.sum(sel, axis=1, keepdims=True)
+        return start, end, start + dot(sel, ahead), dot(prior, same) + dot(sel, same_ahead)
+
+    def listing(sel, place, value, size):
+        t = iota((size, NB), 0).astype(jnp.float32)
+        held = jnp.zeros((size, NB), jnp.float32)
+        for a in range(RB):
+            hit = flag(t == place[a : a + 1]) * sel[a : a + 1]
+            held = held + hit * value[a : a + 1]
+        ones = jnp.ones((RB, NB), jnp.float32)
+        row = lax.dot_general(ones, held, (((1,), (1,)), ((), ())), preferred_element_type=jnp.float32)[:1]
+        if size < NB:
+            row = jnp.concatenate([row, jnp.zeros((1, NB - size), jnp.float32)], axis=1)
+        return row
+
+    def count(sel):
+        return jnp.sum(jnp.sum(sel, axis=1, keepdims=True), axis=0, keepdims=True)
+
+    def panel(sel, cap):
+        start, end, place, rank = ranks(sel)
+        slot = ((col & 1) * (4 * cap) + (col >> 1) * cap).astype(jnp.float32) + jnp.minimum(rank, cap - 1.0)
+        listed = listing(sel, place, slot, LIST) * NB + listing(sel, place, node, LIST)
+        packed = listing(sel * own, rank, spot, 32)
+        return jnp.minimum(start, LIST), jnp.minimum(end, LIST), listed, packed, jnp.minimum(count(sel * own), cap)
+
+    near_p = dot(mine, near)
+    high_p = dot(mine, high)
+    far_p = dot(mine, far)
+    start_l, end_l, list_l, pack_l, count_l = panel(near_p, CAP_L)
+    start_u, end_u, list_u, pack_u, count_u = panel(high_p, CAP_U)
+    _, _, _, rank_t = ranks(far_p)
+    list_t = listing(far_p * own, rank_t, spot, NB)
+    count_t = count(far_p * own)
+    rows = jnp.zeros((RB, NB), jnp.float32)
+    for k, value in enumerate([row_lev, row_wid, start_l, end_l, start_u, end_u]):
+        rows = rows + flag(lane == k) * value
+    counts = jnp.zeros((1, NB), jnp.float32)
+    for k, value in enumerate([count_l, count_u, count_t, full]):
+        counts = counts + flag(lane[:1] == k) * value
+    none = jnp.zeros((1, NB), jnp.float32)
+    lists = jnp.concatenate([list_l, list_u, list_t, pack_l, pack_u, counts, none, none], axis=0)
+    out[0:8, :] = rows.astype(jnp.int32)
+    out[8:16, :] = lists.astype(jnp.int32)
+
+
+def tables(pattern, levels, widths):
+    return pl.pallas_call(
+        table_kernel,
+        out_shape=jax.ShapeDtypeStruct((16, NB), jnp.int32),
+        in_specs=[VMEM, VMEM, VMEM],
+        out_specs=VMEM,
+    )(pattern, levels.reshape(1, NB), widths.reshape(1, NB))
+
+
+def pack_kernel(where, cap, table, blocks, out, held, sems_in, sems_out):
+    count = table[COUNTS, where]
+    row = PACK_L + where
+
+    def load(t):
+        n = table[row, t]
+        return pltpu.make_async_copy(blocks.at[n >> 4, n & (CB - 1)], held.at[t], sems_in.at[t])
+
+    def store(t):
+        return pltpu.make_async_copy(held.at[t], out.at[t], sems_out.at[t])
+
+    pl.loop(0, count)(lambda t: load(t).start())
+
+    @pl.loop(0, count)
+    def _(t):
+        load(t).wait()
+        store(t).start()
+
+    pl.loop(0, count)(lambda t: store(t).wait())
+
+
+def pack(where, cap, table, blocks):
+    return pl.pallas_call(
+        lambda *refs: pack_kernel(where, cap, *refs),
+        out_shape=jax.ShapeDtypeStruct((cap, W, W), jnp.float32),
+        in_specs=[SMEM, HBM],
+        out_specs=HBM,
+        scratch_shapes=[
+            pltpu.VMEM((cap, W, W), jnp.float32),
+            pltpu.SemaphoreType.DMA((cap,)),
+            pltpu.SemaphoreType.DMA((cap,)),
+        ],
+    )(table, blocks)
+
+
+def level_kernel(level, copies, kind, cap, turn, table, known, right, inverse, panel_0, panel_1, *rest):
+    if turn:
+        inverse_2, out, out_2, blocks, inv, inv_2, sems, isems = rest
+    else:
+        out, blocks, inv, sems, isems = rest
+    p = lax.axis_index("prow")
+    row = LIST_U if kind else LIST_L
+    first, last = (START_U, END_U) if kind else (START_L, END_L)
+
+    def copy(t, panel=panel_0):
+        slot = table[row, t] >> 7
+        slot = jnp.where(slot >= 4 * cap, slot - 4 * cap, slot)
+        return pltpu.make_async_copy(panel.at[slot], blocks.at[t], sems.at[t])
+
+    core = lax.axis_index("pcol") & 1
+
+    def begin(t):
+        other = jnp.where((table[row, t] >> 7) >= 4 * cap, 1 - core, core)
+
+        @pl.when(other == 1)
+        def _():
+            copy(t, panel_1).start()
+
+        @pl.when(other == 0)
+        def _():
+            copy(t, panel_0).start()
+
+    def icopy(a):
+        return pltpu.make_async_copy(inverse.at[a], inv.at[a], isems.at[a])
+
+    def icopy_2(a):
+        return pltpu.make_async_copy(inverse_2.at[a], inv_2.at[a], isems.at[RB + a])
+
+    for a in range(RB):
+        @pl.when(table[a, LEVEL] == level)
+        def _():
+            if panel_0 is not None:
+                pl.loop(table[a, first], table[a, last])(begin)
+            icopy(a).start()
+            if turn:
+                icopy_2(a).start()
+
+    lane = iota((HS, W), 1)
+    for a in range(RB):
+        old = known[p, a] if known is not None else jnp.zeros((HS, W), jnp.float32)
+        for r in range(copies):
+            out[r, a] = old if not turn else jnp.zeros((HS, W), jnp.float32)
+        if turn:
+            out_2[a] = old
+
+        @pl.when(table[a, LEVEL] == level)
+        def _():
+            acc = right[a]
+            if panel_0 is not None:
+                def step(t, acc):
+                    copy(t).wait()
+                    node = table[row, t] & (NB - 1)
+                    return acc - dot3(known[node & (PR - 1), node >> 4], blocks[t])
+
+                acc = lax.fori_loop(table[a, first], table[a, last], step, acc)
+            icopy(a).wait()
+            keep = lane < table[a, WIDTH]
+            fresh = jnp.where(keep, dot3(acc, inv[a]), 0.0)
+            if turn:
+                out_2[a] = fresh
+                icopy_2(a).wait()
+                fresh = jnp.where(keep, dot3(fresh, inv_2[a]), 0.0)
+            for r in range(copies):
+                out[r, a] = fresh
+
+
+def level_step(level, copies, kind, table, known, right, inverse, panel, turn=None):
+    cap = CAP_U if kind else CAP_L
+    ins, specs = [table], [SMEM]
+    for x, spec in ((known, VMEM), (right, VMEM), (inverse, HBM)):
+        if x is not None:
+            ins.append(x)
+            specs.append(spec)
+    if panel is not None:
+        ins += list(panel)
+        specs += [HBM, HBM]
+    if turn is not None:
+        ins.append(turn)
+        specs.append(HBM)
+
+    def kernel(*refs):
+        refs = list(refs)
+        given = [refs.pop(0)]
+        given.append(refs.pop(0) if known is not None else None)
+        given += [refs.pop(0), refs.pop(0)]
+        given += [refs.pop(0), refs.pop(0)] if panel is not None else [None, None]
+        level_kernel(level, copies, kind, cap, turn is not None, *given, *refs)
+
+    out_shape = [jax.ShapeDtypeStruct((copies, RB, HS, W), jnp.float32)]
+    scratch = [pltpu.VMEM((LIST, W, W), jnp.float32), pltpu.VMEM((RB, W, W), jnp.float32)]
+    if turn is not None:
+        out_shape.append(jax.ShapeDtypeStruct((RB, HS, W), jnp.float32))
+        scratch.append(pltpu.VMEM((RB, W, W), jnp.float32))
+    scratch += [pltpu.SemaphoreType.DMA((LIST,)), pltpu.SemaphoreType.DMA((2 * RB,))]
+    out = pl.pallas_call(
+        kernel,
+        out_shape=out_shape,
+        in_specs=specs,
+        out_specs=[VMEM] * len(out_shape),
+        scratch_shapes=scratch,
+        compiler_params=pltpu.CompilerParams(vmem_limit_bytes=24 * 1024 * 1024),
+    )(*ins)
+    return out if turn is not None else out[0]
+
+
+def across_kernel(table, known, lower, out, blocks, sems):
+    count = table[COUNTS, 2]
+
+    def copy(t):
+        n = table[LIST_T, t]
+        return pltpu.make_async_copy(lower.at[n >> 4, n & (CB - 1)], blocks.at[t], sems.at[t])
+
+    pl.loop(0, count)(lambda t: copy(t).start())
+    out[...] = jnp.zeros_like(out)
+
+    def step(t, carry):
+        copy(t).wait()
+        n = table[LIST_T, t]
+        a = n >> 4
+        c = n & (CB - 1)
+        x = known[:, c & 1, c >> 1].reshape(NRHS, W)
+        out[:, a] += dot3(x, blocks[t]).reshape(PC, HS, W)
+        return carry
+
+    lax.fori_loop(0, count, step, 0)
+
+
+def across(table, known, lower):
+    return pl.pallas_call(
+        across_kernel,
+        out_shape=jax.ShapeDtypeStruct((PC, RB, HS, W), jnp.float32),
+        in_specs=[SMEM, VMEM, HBM],
+        out_specs=VMEM,
+        scratch_shapes=[pltpu.VMEM((NB, W, W), jnp.float32), pltpu.SemaphoreType.DMA((NB,))],
+        compiler_params=pltpu.CompilerParams(vmem_limit_bytes=24 * 1024 * 1024),
+    )(table, known, lower)
+
+
+def gather_panel(packed):
+    here = lax.all_gather(packed, "pcol", axis_index_groups=SAME_CORE, tiled=True)
+    there = lax.ppermute(here, "pcol", [(k, k ^ 1) for k in range(PC)])
+    return here, there
+
+
+def local(rhs, lower, upper, lower_inverse, upper_inverse, pattern, levels, widths):
+    q = lax.axis_index("pcol")
+    right = rhs.reshape(RB, NRHS, W)
+    lower_blocks = lower.reshape(RB, CB, W, W)
+    upper_blocks = upper.reshape(RB, CB, W, W)
+    lower_inv = lower_inverse.reshape(RB, W, W)
+    upper_inv = upper_inverse.reshape(RB, W, W)
+    table = tables(pattern, levels, widths)
+    panel_l = gather_panel(pack(0, CAP_L, table, lower_blocks))
+    panel_u = gather_panel(pack(1, CAP_U, table, upper_blocks))
+    swap = lambda x: lax.all_to_all(x, "prow", 0, 0)
+
+    b = lax.dynamic_slice_in_dim(right, q * HS, HS, 1)
+    known = swap(level_step(0, PR, 0, table, None, b, lower_inv, None))
+    for level in range(1, LEVELS - 1):
+        if level == 3:
+            split = known.reshape(2, PC, RB, HS, W).transpose(1, 0, 2, 3, 4)
+            columns = lax.all_to_all(split, "pcol", 0, 0)
+            sums = lax.all_to_all(across(table, columns, lower_blocks), "pcol", 0, 0)
+            b = b - jnp.sum(sums, axis=0)
+        known = swap(level_step(level, PR, 0, table, known, b, lower_inv, panel_l))
+    state, forward = level_step(LEVELS - 1, PR, 0, table, known, b, lower_inv, panel_l, upper_inv)
+    full_f = lax.all_gather(forward, "pcol")
+    known = swap(state)
+    for level in range(LEVELS - 2, 0, -1):
+        known = swap(level_step(level, PR, 1, table, known, forward, upper_inv, panel_u))
+    state = level_step(0, PC, 1, table, known, forward, upper_inv, panel_u)
+    full_s = lax.all_to_all(state, "pcol", 0, 0)
+    shape = rhs.shape
+    whole = lambda x: x.transpose(1, 0, 2, 3).reshape(shape)
+    args = (rhs, lower, upper, lower_inverse, upper_inverse, pattern, levels, widths)
+    done = lax.while_loop(
+        lambda c: c[2] > 0,
+        lambda c: general(*args) + (jnp.int32(0),),
+        (whole(full_f), whole(full_s), table[COUNTS, 3]),
+    )
+    return done[0], done[1]
+
+
 def solution(mesh):
     in_specs = (
         P(None, "prow", None, None),

time: 1700 us -> 389 us (0.23)
  waiting for transfers between devices: 1500 us -> 117 us
  blocking collectives: 0 us -> 182 us
  matrix products: 158 us -> 0 us
  Pallas kernels: 0 us -> 51.4 us
  other arithmetic: 19.3 us -> 0.99 us
    psum x21 -> x0, waiting for transfers between devices: 1500 us -> none  [the longest x10 851 us: spread(): return lax.psum(kept, axis)]
    all_to_all x0 -> x12, blocking collectives: none -> 168 us  [the longest x10 142 us: local(): swap = lambda x: lax.all_to_all(x, 'prow', 0, 0)]
    dot_general x24 -> x0, matrix products: 158 us -> none  [the longest x12 132 us: solve_levels(): jnp.einsum('ackl,chl->ahk', masked, col_state, precision=lax.Precision.HI...]
    all_gather x0 -> x2, waiting for transfers between devices: none -> 117 us  [gather_panel(): lax.all_gather(packed, 'pcol', axis_index_groups=SAME_CORE, tiled=True)]
    pallas_call x0 -> x15, Pallas kernels: none -> 51.4 us  [the longest x11 37.3 us: level_step(): pl.pallas_call(kernel, out_shape=out_shape, in_specs=specs, out_specs=[VM...]
    another operation x20 -> x0, other arithmetic: 19.2 us -> none  [solve_levels(): stacked = jnp.stack(pieces, axis=1)]
  transfers between devices with their start and end apart: 21 -> 5, of which waited for: 21 -> 2; matrix products, arithmetic and copies ran while one was open for 1% -> 1% of each run, Pallas kernels for 0% -> 7%
where the time goes in v1:
time: 389 us
  blocking collectives  182 us (47%)
  waiting for transfers between devices  117 us (30%)
  Pallas kernels  51.4 us (13%)
  starting transfers between devices  15.3 us (4%)
  between operations  14.3 us (4%)
  local copies, waits for them, and re-layouts  7.86 us (2%)
    all_to_all x10, blocking collectives, local(): swap = lambda x: lax.all_to_all(x, 'prow', 0, 0)  142 us
    all_gather x2, waiting for transfers between devices, gather_panel(): lax.all_gather(packed, 'pcol', axis_index_groups=SAME_CORE, tiled=True)  117 us
    pallas_call x11, Pallas kernels, level_step(): pl.pallas_call(kernel, out_shape=out_shape, in_specs=specs, out_specs=[VM...  37.3 us
    all_to_all x1, blocking collectives, local(): columns = lax.all_to_all(split, 'pcol', 0, 0)  15.2 us
    all_gather x1, blocking collectives, local(): full_f = lax.all_gather(forward, 'pcol')  13.8 us
    all_to_all x1, starting transfers between devices, local(): full_s = lax.all_to_all(state, 'pcol', 0, 0)  13.8 us
    all_to_all x1, blocking collectives, local(): sums = lax.all_to_all(across(table, columns, lower_blocks), 'pcol', 0, 0)  11.3 us
  transfers between devices with their start and end apart: 5, of which 2 were waited for; matrix products, arithmetic and copies ran while one was open for 1% of the time, Pallas kernels for 7%

profile of v1, /device:TPU:1, one launch (start us, length us, event | category | flops | bytes accessed | tf_op | source)
XLA Modules:
  0.0 389.4 jit_solution(15276520692560956418)
XLA Ops:
  7.2 0.0 all-gather.6.cloned.1.call-start
  7.2 2.4 shard_map.95.refs_0_.table
  9.6 2.9 shard_map.104
  12.6 0.0 copy-start.14
  12.6 0.0 copy-start.7
  12.6 0.0 all-gather.6.cloned.1.call-update
  12.6 0.0 all-gather.4.cloned.1.call-start
  12.7 2.5 shard_map.97
  15.2 0.0 all-gather.4.cloned.1.call-update
  15.2 75.1 %all-gather.6.cloned.1.call-done.refs_4_ = f32[112,128,128]{2,1,0:T(8,128)} async-done(((f32[28,128,128]{2,1,0:T(8,128)}), f32[112,128,128]{2,1,0:T(8,128)}) %all-gather.6.cloned.1.call-update) | async-done | bytes 7340048 | tf_op jit(solution)/shard_map/all_gather | solution.py:398
  90.3 0.7 collective-permute-start.1
  91.0 41.5 %all-gather.4.cloned.1.call-done.refs_4_ = f32[48,128,128]{2,1,0:T(8,128)} async-done(((f32[12,128,128]{2,1,0:T(8,128)}), f32[48,128,128]{2,1,0:T(8,128)}) %all-gather.4.cloned.1.call-update) | async-done | bytes 3145744 | tf_op jit(solution)/shard_map/all_gather | solution.py:398
  132.4 0.7 collective-permute-start
  133.1 0.0 copy-done.14
  133.1 0.0 copy-done.7
  133.1 2.9 shard_map.96
  136.1 17.4 %all_to_all.65.refs_1_ = f32[16,8,8,128]{3,2,1,0:T(8,128)S(1)} all-to-all(f32[16,8,8,128]{3,2,1,0:T(8,128)S(1)} %shard_map.96), channel_id=1, replica_groups=mesh['prow'=16,'pcol'=8] {'prow'}, dimensions={0} | all-to-all | bytes 1048576 | tf_op jit(solution)/shard_map/all_to_all | solution.py:413
  153.5 0.0 collective-permute-done.refs_5_
  153.5 1.9 copy-done
  155.4 4.0 %shard_map.98 = f32[16,8,8,128]{3,2,1,0:T(8,128)S(1)} custom-call(s32[16,128]{1,0:T(8,128)S(1)} %copy-done.7, f32[16,8,8,128]{3,2,1,0:T(8,128)S(1)} %all_to_all.65.refs_1_, f32[8,8,128]{2,1,0:T(8,128)S(1)} %dynamic-slice_bitcast_fusion.refs_1_.refs_2_, f32[8,128,128]{2,1,0:T(8,128)} %bitcast.283, f32[48,128,128]{2,1,0:T(8,128)S(1)} %copy-done, ...), custom_call_target="tpu_custom_call" | custom-call | tf_op jit(solution)/shard_map/pallas_call | solution.py:353
  159.4 14.9 %all_to_all.66.refs_1_ = f32[16,8,8,128]{3,2,1,0:T(8,128)S(1)} all-to-all(f32[16,8,8,128]{3,2,1,0:T(8,128)S(1)} %shard_map.98), channel_id=1, replica_groups=mesh['prow'=16,'pcol'=8] {'prow'}, dimensions={0} | all-to-all | bytes 1048576 | tf_op jit(solution)/shard_map/all_to_all | solution.py:413
  174.2 0.0 copy-done.2
  174.2 0.0 copy-done.8
  174.3 1.5 shard_map.99
  175.8 0.0 copy-start.1
  175.8 18.3 %all_to_all.67.refs_1_ = f32[16,8,8,128]{3,2,1,0:T(8,128)S(1)} all-to-all(f32[16,8,8,128]{3,2,1,0:T(8,128)S(1)} %shard_map.99), channel_id=1, replica_groups=mesh['prow'=16,'pcol'=8] {'prow'}, dimensions={0} | all-to-all | bytes 1048576 | tf_op jit(solution)/shard_map/all_to_all | solution.py:413
  194.2 0.0 copy-start.5
  194.2 0.8 copy-done.5
  195.0 15.2 %all_to_all.68.known = f32[8,2,8,8,128]{4,3,2,1,0:T(8,128)S(1)} all-to-all(f32[8,2,8,8,128]{4,3,2,1,0:T(8,128)S(1)} %bitcast.310), channel_id=1, replica_groups=mesh['prow'=16,'pcol'=8] {'pcol'}, dimensions={0} | all-to-all | bytes 1048576 | tf_op jit(solution)/shard_map/all_to_all | solution.py:420
  210.1 0.0 slice-done.2
  210.1 0.0 slice-done.3
  210.1 6.3 %shard_map.100 = f32[8,8,8,128]{3,2,1,0:T(8,128)S(1)} custom-call(s32[16,128]{1,0:T(8,128)S(1)} %copy-done.7, f32[8,2,8,8,128]{4,3,2,1,0:T(8,128)S(1)} %all_to_all.68.known, f32[8,16,128,128]{3,2,1,0:T(8,128)S(1)} %bitcast.279), custom_call_target="tpu_custom_call" | custom-call | tf_op jit(solution)/shard_map/pallas_call | solution.py:387
  216.4 11.3 %all_to_all.69 = f32[8,8,8,128]{3,2,1,0:T(8,128)} all-to-all(f32[8,8,8,128]{3,2,1,0:T(8,128)S(1)} %shard_map.100), channel_id=1, replica_groups=mesh['prow'=16,'pcol'=8] {'pcol'}, dimensions={0} | all-to-all | bytes 524288 | tf_op jit(solution)/shard_map/all_to_all | solution.py:421
  227.7 1.0 reduce_sum.9
  228.7 0.0 copy-done.1
  228.7 0.0 copy-start.3
  228.7 1.9 copy-done.3
  230.6 1.0 copy-done.6
  231.7 2.8 shard_map.101
  234.5 13.2 %all_to_all.70.refs_1_ = f32[16,8,8,128]{3,2,1,0:T(8,128)S(1)} all-to-all(f32[16,8,8,128]{3,2,1,0:T(8,128)S(1)} %shard_map.101), channel_id=1, replica_groups=mesh['prow'=16,'pcol'=8] {'prow'}, dimensions={0} | all-to-all | bytes 1048576 | tf_op jit(solution)/shard_map/all_to_all | solution.py:413
  247.7 2.3 shard_map.102
  250.0 12.8 %all_to_all.71.refs_1_ = f32[16,8,8,128]{3,2,1,0:T(8,128)S(1)} all-to-all(f32[16,8,8,128]{3,2,1,0:T(8,128)S(1)} %shard_map.102), channel_id=1, replica_groups=mesh['prow'=16,'pcol'=8] {'prow'}, dimensions={0} | all-to-all | bytes 1048576 | tf_op jit(solution)/shard_map/all_to_all | solution.py:413
  262.8 5.2 %shard_map.103 = (f32[16,8,8,128]{3,2,1,0:T(8,128)S(1)}, f32[8,8,128]{2,1,0:T(8,128)S(1)}) custom-call(s32[16,128]{1,0:T(8,128)S(1)} %copy-done.7, f32[16,8,8,128]{3,2,1,0:T(8,128)S(1)} %all_to_all.71.refs_1_, f32[8,8,128]{2,1,0:T(8,128)S(1)} %fusion.122.refs_2_, f32[8,128,128]{2,1,0:T(8,128)S(1)} %bitcast.287, f32[48,128,128]{2,1,0:T(8,128)S(1)} %copy-done.1, ...), custom_call_target="tpu_custom_call" | custom-call | tf_op jit(solution)/shard_map/pallas_call | solution.py:353
  268.0 11.7 %all_to_all.72.refs_1_ = f32[16,8,8,128]{3,2,1,0:T(8,128)S(1)} all-to-all(f32[16,8,8,128]{3,2,1,0:T(8,128)S(1)} %get-tuple-element.60), channel_id=1, replica_groups=mesh['prow'=16,'pcol'=8] {'prow'}, dimensions={0} | all-to-all | bytes 1048576 | tf_op jit(solution)/shard_map/all_to_all | solution.py:413
  279.7 0.0 collective-permute-done.1.refs_5_
  279.7 2.8 shard_map.105
  282.5 11.7 %all_to_all.73.refs_1_ = f32[16,8,8,128]{3,2,1,0:T(8,128)S(1)} all-to-all(f32[16,8,8,128]{3,2,1,0:T(8,128)S(1)} %shard_map.105), channel_id=1, replica_groups=mesh['prow'=16,'pcol'=8] {'prow'}, dimensions={0} | all-to-all | bytes 1048576 | tf_op jit(solution)/shard_map/all_to_all | solution.py:413
  294.3 3.1 shard_map.106
  297.4 11.6 %all_to_all.74.refs_1_ = f32[16,8,8,128]{3,2,1,0:T(8,128)S(1)} all-to-all(f32[16,8,8,128]{3,2,1,0:T(8,128)S(1)} %shard_map.106), channel_id=1, replica_groups=mesh['prow'=16,'pcol'=8] {'prow'}, dimensions={0} | all-to-all | bytes 1048576 | tf_op jit(solution)/shard_map/all_to_all | solution.py:413
  309.0 1.5 shard_map.107
  310.5 14.8 %all_to_all.75.refs_1_ = f32[16,8,8,128]{3,2,1,0:T(8,128)S(1)} all-to-all(f32[16,8,8,128]{3,2,1,0:T(8,128)S(1)} %shard_map.107), channel_id=1, replica_groups=mesh['prow'=16,'pcol'=8] {'prow'}, dimensions={0} | all-to-all | bytes 1048576 | tf_op jit(solution)/shard_map/all_to_all | solution.py:413
  325.4 3.1 shard_map.108
  328.5 15.3 %all_to_all.76.refs_1_ = f32[16,8,8,128]{3,2,1,0:T(8,128)S(1)} all-to-all(f32[16,8,8,128]{3,2,1,0:T(8,128)S(1)} %shard_map.108), channel_id=1, replica_groups=mesh['prow'=16,'pcol'=8] {'prow'}, dimensions={0} | all-to-all | bytes 1048576 | tf_op jit(solution)/shard_map/all_to_all | solution.py:413
  343.8 0.0 copy-start.17
  343.8 8.1 %shard_map.109 = f32[8,8,8,128]{3,2,1,0:T(8,128)} custom-call(s32[16,128]{1,0:T(8,128)S(1)} %copy-done.7, f32[16,8,8,128]{3,2,1,0:T(8,128)S(1)} %all_to_all.76.refs_1_, f32[8,8,128]{2,1,0:T(8,128)S(1)} %get-tuple-element.59.refs_2_, f32[8,128,128]{2,1,0:T(8,128)S(1)} %bitcast.294, f32[112,128,128]{2,1,0:T(8,128)S(1)} %bitcast.273, ...), custom_call_target="tpu_custom_call" | custom-call | tf_op jit(solution)/shard_map/pallas_call | solution.py:353
  351.9 13.8 %all-to-all-start.12 = ((f32[8,8,8,128]{3,2,1,0:T(8,128)}), f32[8,8,8,128]{3,2,1,0:T(8,128)S(1)}, u32[]{:S(2)}, u32[]{:S(2)}) async-start(f32[8,8,8,128]{3,2,1,0:T(8,128)} %shard_map.109), calls=%async_computation.12 | async-start | bytes 524288 | tf_op jit(solution)/shard_map/all_to_all | solution.py:430
  365.7 0.6 slice.4
  366.3 0.1 copy.75
  366.4 13.8 %all-gather = f32[64,8,128]{2,1,0:T(8,128)S(1)} all-gather(f32[8,8,128]{2,1,0:T(8,128)S(1)} %get-tuple-element.59.refs_2_), channel_id=2, replica_groups=mesh['prow'=16,'pcol'=8] {'pcol'}, dimensions={0}, use_global_device_ids=true | all-gather | bytes 294912 | tf_op jit(solution)/shard_map/all_gather | solution.py:425
  380.2 0.7 copy.98
  380.9 0.0 all-to-all-done.12
  380.9 0.7 copy_bitcast_fusion.1
  381.7 0.0 copy-done.17
  381.7 0.9 while.11
  (29 shorter events, 0.1 us)
Async XLA Ops:
  7.2 83.1 %all-gather.6.cloned.1.call-start = ((), (), s32[]{:S(2)}) async-start(), calls=%async_computation.35 | async-start | bytes 9175040 | tf_op jit(solution)/shard_map/all_gather | solution.py:398
  12.6 120.6 %copy-start.14 = (f32[8,1,64,128]{3,2,1,0:T(8,128)S(1)}, f32[8,1,64,128]{3,2,1,0:T(8,128)}, u32[]{:S(2)}) copy-start(f32[8,1,64,128]{3,2,1,0:T(8,128)} %param.10) | copy-start | bytes 786436
  12.6 120.6 %copy-start.7 = (s32[16,128]{1,0:T(8,128)S(1)}, s32[16,128]{1,0:T(8,128)}, u32[]{:S(2)}) copy-start(s32[16,128]{1,0:T(8,128)} %shard_map.95.refs_0_.table) | copy-start | bytes 24580
  12.6 119.8 %all-gather.4.cloned.1.call-start = ((), (), s32[]{:S(2)}) async-start(), calls=%async_computation.34 | async-start | bytes 3932160 | tf_op jit(solution)/shard_map/all_gather | solution.py:398
  90.3 189.5 %collective-permute-start.1 = (f32[112,128,128]{2,1,0:T(8,128)}, f32[112,128,128]{2,1,0:T(8,128)}, u32[]{:S(2)}, u32[]{:S(2)}) collective-permute-start(f32[112,128,128]{2,1,0:T(8,128)} %all-gather.6.cloned.1.call-done.refs_4_), channel_id=1, source_target_pairs={{0,1},{1,0},{2,3},{3,2},{4,5},{5,4},{6,7},{7,6},{8,9},{9,8},{10,11... | collective-permute-start | bytes 22020104 | tf_op jit(solution)/shard_map/ppermute | solution.py:399
  132.4 21.1 %collective-permute-start = (f32[48,128,128]{2,1,0:T(8,128)}, f32[48,128,128]{2,1,0:T(8,128)S(1)}, u32[]{:S(2)}, u32[]{:S(2)}) collective-permute-start(f32[48,128,128]{2,1,0:T(8,128)} %all-gather.4.cloned.1.call-done.refs_4_), channel_id=1, source_target_pairs={{0,1},{1,0},{2,3},{3,2},{4,5},{5,4},{6,7},{7,6},{8,9},{9,8},{10,11... | collective-permute-start | bytes 9437192 | tf_op jit(solution)/shard_map/ppermute | solution.py:399
  133.1 41.1 %copy-start.8 = (f32[8,1,128,128]{3,2,1,0:T(8,128)S(1)}, f32[8,1,128,128]{3,2,1,0:T(8,128)}, u32[]{:S(2)}) copy-start(f32[8,1,128,128]{3,2,1,0:T(8,128)} %param.13) | copy-start | bytes 1572868
  153.5 1.9 copy-start
  155.4 18.8 %copy-start.2 = (f32[48,128,128]{2,1,0:T(8,128)}, f32[48,128,128]{2,1,0:T(8,128)S(1)}, u32[]{:S(2)}) copy-start(f32[48,128,128]{2,1,0:T(8,128)S(1)} %collective-permute-done.refs_5_) | copy-start | bytes 9437188
  155.4 54.7 %slice-start.2 = ((s8[8388608]{0:T(1024)(128)(4,1)}), s8[4194304]{0:T(1024)(128)(4,1)S(1)}, s32[]{:S(2)}) async-start(s8[8388608]{0:T(1024)(128)(4,1)} %bitcast.277), calls=%async_computation.38 | async-start | bytes 8388608
  174.3 35.9 %slice-start.3 = ((s8[8388608]{0:T(1024)(128)(4,1)}), s8[4194304]{0:T(1024)(128)(4,1)S(1)}, s32[]{:S(2)}) async-start(s8[8388608]{0:T(1024)(128)(4,1)} %bitcast.277), calls=%async_computation.39 | async-start | bytes 8388608
  175.8 52.9 %copy-start.1 = (f32[48,128,128]{2,1,0:T(8,128)S(1)}, f32[48,128,128]{2,1,0:T(8,128)}, u32[]{:S(2)}) copy-start(f32[48,128,128]{2,1,0:T(8,128)} %all-gather.4.cloned.1.call-done.refs_4_) | copy-start | bytes 9437188
  194.2 0.8 copy-start.5
  228.7 1.9 copy-start.3
  230.6 1.0 copy-start.6
  231.7 16.0 %copy-start.4 = (f32[48,128,128]{2,1,0:T(8,128)S(1)}, f32[48,128,128]{2,1,0:T(8,128)}, u32[]{:S(2)}) copy-start(f32[48,128,128]{2,1,0:T(8,128)} %copy-done.2) | copy-start | bytes 9437188
  231.7 16.0 %copy-start.9 = (f32[8,1,128,128]{3,2,1,0:T(8,128)S(1)}, f32[8,1,128,128]{3,2,1,0:T(8,128)}, u32[]{:S(2)}) copy-start(f32[8,1,128,128]{3,2,1,0:T(8,128)} %param.13) | copy-start | bytes 1572868
  231.7 31.1 %copy-start.11 = (f32[8,1,128,128]{3,2,1,0:T(8,128)S(1)}, f32[8,1,128,128]{3,2,1,0:T(8,128)}, u32[]{:S(2)}) copy-start(f32[8,1,128,128]{3,2,1,0:T(8,128)} %param.14) | copy-start | bytes 1572868
  247.7 32.0 %slice-start = ((s8[7340032]{0:T(1024)(128)(4,1)}), s8[4194304]{0:T(1024)(128)(4,1)S(1)}, s32[]{:S(2)}) async-start(s8[7340032]{0:T(1024)(128)(4,1)} %bitcast.272), calls=%async_computation.36 | async-start | bytes 8388608
  262.8 17.0 %slice-start.1 = ((s8[7340032]{0:T(1024)(128)(4,1)}), s8[3145728]{0:T(1024)(128)(4,1)S(1)}, s32[]{:S(2)}) async-start(s8[7340032]{0:T(1024)(128)(4,1)} %bitcast.272), calls=%async_computation.37 | async-start | bytes 6291456
  343.8 22.5 %copy-start.15 = (s32[128,128]{1,0:T(8,128)S(1)}, s32[128,128]{1,0:T(8,128)}, u32[]{:S(2)}) copy-start(s32[128,128]{1,0:T(8,128)} %pattern.1) | copy-start | bytes 196612
  343.8 37.9 %copy-start.10 = (f32[8,1,128,128]{3,2,1,0:T(8,128)S(1)}, f32[8,1,128,128]{3,2,1,0:T(8,128)}, u32[]{:S(2)}) copy-start(f32[8,1,128,128]{3,2,1,0:T(8,128)} %param.13) | copy-start | bytes 1572868
  343.8 37.9 %copy-start.12 = (f32[8,1,128,128]{3,2,1,0:T(8,128)S(1)}, f32[8,1,128,128]{3,2,1,0:T(8,128)}, u32[]{:S(2)}) copy-start(f32[8,1,128,128]{3,2,1,0:T(8,128)} %param.14) | copy-start | bytes 1572868
  343.8 37.9 %copy-start.16 = (s32[128]{0:T(128)S(1)}, s32[128]{0:T(128)}, u32[]{:S(2)}) copy-start(s32[128]{0:T(128)} %param.16) | copy-start | bytes 1540
  343.8 37.9 %copy-start.17 = (s32[128]{0:T(128)S(1)}, s32[128]{0:T(128)}, u32[]{:S(2)}) copy-start(s32[128]{0:T(128)} %param.17) | copy-start | bytes 1540
  351.9 29.0 %all-to-all-start.12 = ((f32[8,8,8,128]{3,2,1,0:T(8,128)}), f32[8,8,8,128]{3,2,1,0:T(8,128)S(1)}, u32[]{:S(2)}, u32[]{:S(2)}) async-start(f32[8,8,8,128]{3,2,1,0:T(8,128)} %shard_map.109), calls=%async_computation.12 | async-start | bytes 524288 | tf_op jit(solution)/shard_map/all_to_all | solution.py:430
Sparse Core Ops, SparseCore 0:
  12.7 77.4 all-gather.5
  92.0 40.3 all-gather.3

commit v2 on v1

--- a/solution.py
+++ b/solution.py
@@ -14,15 +14,16 @@
 PR = 16
 PC = 8
 HS = NRHS // PC
-CAP_L = 12
+CAP_L = 10
 CAP_U = 28
 LIST = 64
-HBM = pl.BlockSpec(memory_space=pltpu.HBM)
+GROUP = 4
+HBM = pl.BlockSpec(memory_space=pl.ANY)
+ROOM = 60 * 1024 * 1024
 SMEM = pl.BlockSpec(memory_space=pltpu.SMEM)
 VMEM = pl.BlockSpec(memory_space=pltpu.VMEM)
 LEVEL, WIDTH, START_L, END_L, START_U, END_U = range(6)
 LIST_L, LIST_U, LIST_T, PACK_L, PACK_U, COUNTS = range(8, 14)
-SAME_CORE = [[2 * x + c for x in range(PC // 2)] for c in range(2)]
 
 
 def spread(value, axis, source):
@@ -95,19 +96,22 @@
 
 
 def dot3(x, w):
-    m = x.shape[0]
+    m, n = x.shape[0], w.shape[0]
     xh = x.astype(jnp.bfloat16).astype(jnp.float32)
     xs = jnp.concatenate([xh, x - xh], axis=0).astype(jnp.bfloat16)
     wh = w.astype(jnp.bfloat16)
     wl = (w - wh.astype(jnp.float32)).astype(jnp.bfloat16)
-    dims = (((1,), (1,)), ((), ()))
-    a = lax.dot_general(xs, wl, dims, preferred_element_type=jnp.float32)
-    b = lax.dot_general(xs, wh, dims, preferred_element_type=jnp.float32)
-    return (a[m:] + a[:m]) + (b[m:] + b[:m])
+    ws = jnp.concatenate([wh, wl], axis=0)
+    y = lax.dot_general(xs, ws, (((1,), (1,)), ((), ())), preferred_element_type=jnp.float32)
+    return (y[m:, n:] + y[:m, n:]) + (y[m:, :n] + y[:m, :n])
 
 
 def iota(shape, dim):
     return lax.broadcasted_iota(jnp.int32, shape, dim)
+
+
+def cost(mib):
+    return pl.CostEstimate(flops=0, bytes_accessed=mib << 20, transcendentals=0)
 
 
 def flag(cond):
@@ -182,7 +186,7 @@
 
     def panel(sel, cap):
         start, end, place, rank = ranks(sel)
-        slot = ((col & 1) * (4 * cap) + (col >> 1) * cap).astype(jnp.float32) + jnp.minimum(rank, cap - 1.0)
+        slot = (col * cap).astype(jnp.float32) + jnp.minimum(rank, cap - 1.0)
         listed = listing(sel, place, slot, LIST) * NB + listing(sel, place, node, LIST)
         packed = listing(sel * own, rank, spot, 32)
         return jnp.minimum(start, LIST), jnp.minimum(end, LIST), listed, packed, jnp.minimum(count(sel * own), cap)
@@ -213,10 +217,11 @@
         out_shape=jax.ShapeDtypeStruct((16, NB), jnp.int32),
         in_specs=[VMEM, VMEM, VMEM],
         out_specs=VMEM,
+        cost_estimate=cost(4),
     )(pattern, levels.reshape(1, NB), widths.reshape(1, NB))
 
 
-def pack_kernel(where, cap, table, blocks, out, held, sems_in, sems_out):
+def pack_kernel(where, cap, table, blocks, _, out, held, sems_in, sems_out):
     count = table[COUNTS, where]
     row = PACK_L + where
 
@@ -237,21 +242,22 @@
     pl.loop(0, count)(lambda t: store(t).wait())
 
 
-def pack(where, cap, table, blocks):
+def pack(where, cap, table, blocks, after):
     return pl.pallas_call(
         lambda *refs: pack_kernel(where, cap, *refs),
         out_shape=jax.ShapeDtypeStruct((cap, W, W), jnp.float32),
-        in_specs=[SMEM, HBM],
+        in_specs=[SMEM, HBM, HBM],
         out_specs=HBM,
         scratch_shapes=[
             pltpu.VMEM((cap, W, W), jnp.float32),
             pltpu.SemaphoreType.DMA((cap,)),
             pltpu.SemaphoreType.DMA((cap,)),
         ],
-    )(table, blocks)
-
-
-def level_kernel(level, copies, kind, cap, turn, table, known, right, inverse, panel_0, panel_1, *rest):
+        cost_estimate=cost(4),
+    )(table, blocks, after)
+
+
+def level_kernel(level, copies, kind, turn, both, table, known, right, inverse, panel, *rest):
     if turn:
         inverse_2, out, out_2, blocks, inv, inv_2, sems, isems = rest
     else:
@@ -260,23 +266,8 @@
     row = LIST_U if kind else LIST_L
     first, last = (START_U, END_U) if kind else (START_L, END_L)
 
-    def copy(t, panel=panel_0):
-        slot = table[row, t] >> 7
-        slot = jnp.where(slot >= 4 * cap, slot - 4 * cap, slot)
-        return pltpu.make_async_copy(panel.at[slot], blocks.at[t], sems.at[t])
-
-    core = lax.axis_index("pcol") & 1
-
-    def begin(t):
-        other = jnp.where((table[row, t] >> 7) >= 4 * cap, 1 - core, core)
-
-        @pl.when(other == 1)
-        def _():
-            copy(t, panel_1).start()
-
-        @pl.when(other == 0)
-        def _():
-            copy(t, panel_0).start()
+    def copy(t):
+        return pltpu.make_async_copy(panel.at[table[row, t] >> 7], blocks.at[t], sems.at[t])
 
     def icopy(a):
         return pltpu.make_async_copy(inverse.at[a], inv.at[a], isems.at[a])
@@ -287,8 +278,8 @@
     for a in range(RB):
         @pl.when(table[a, LEVEL] == level)
         def _():
-            if panel_0 is not None:
-                pl.loop(table[a, first], table[a, last])(begin)
+            if panel is not None:
+                pl.loop(table[a, first], table[a, last])(lambda t: copy(t).start())
             icopy(a).start()
             if turn:
                 icopy_2(a).start()
@@ -297,20 +288,40 @@
     for a in range(RB):
         old = known[p, a] if known is not None else jnp.zeros((HS, W), jnp.float32)
         for r in range(copies):
-            out[r, a] = old if not turn else jnp.zeros((HS, W), jnp.float32)
+            if both:
+                out[r, 0, a] = right[a]
+                out[r, 1, a] = old
+            else:
+                out[r, a] = old if not turn else jnp.zeros((HS, W), jnp.float32)
         if turn:
             out_2[a] = old
 
         @pl.when(table[a, LEVEL] == level)
         def _():
             acc = right[a]
-            if panel_0 is not None:
-                def step(t, acc):
-                    copy(t).wait()
-                    node = table[row, t] & (NB - 1)
-                    return acc - dot3(known[node & (PR - 1), node >> 4], blocks[t])
-
-                acc = lax.fori_loop(table[a, first], table[a, last], step, acc)
+            if panel is not None:
+                start, end = table[a, first], table[a, last]
+
+                def step(g, acc):
+                    xs, ws = [], []
+                    for u in range(GROUP):
+                        t = start + g * GROUP + u
+                        there = t < end
+
+                        @pl.when(there)
+                        def _():
+                            copy(t).wait()
+
+                        t = jnp.minimum(t, end - 1)
+                        node = table[row, t] & (NB - 1)
+                        xs.append(known[node & (PR - 1), node >> 4] * jnp.where(there, 1.0, 0.0))
+                        ws.append(blocks[t])
+                    for u in range(0, GROUP, 2):
+                        x = jnp.concatenate(xs[u : u + 2], axis=1)
+                        acc = acc - dot3(x, jnp.concatenate(ws[u : u + 2], axis=1))
+                    return acc
+
+                acc = lax.fori_loop(0, (end - start + GROUP - 1) // GROUP, step, acc)
             icopy(a).wait()
             keep = lane < table[a, WIDTH]
             fresh = jnp.where(keep, dot3(acc, inv[a]), 0.0)
@@ -319,19 +330,21 @@
                 icopy_2(a).wait()
                 fresh = jnp.where(keep, dot3(fresh, inv_2[a]), 0.0)
             for r in range(copies):
-                out[r, a] = fresh
-
-
-def level_step(level, copies, kind, table, known, right, inverse, panel, turn=None):
-    cap = CAP_U if kind else CAP_L
+                if both:
+                    out[r, 1, a] = fresh
+                else:
+                    out[r, a] = fresh
+
+
+def level_step(level, copies, kind, table, known, right, inverse, panel, turn=None, both=False):
     ins, specs = [table], [SMEM]
     for x, spec in ((known, VMEM), (right, VMEM), (inverse, HBM)):
         if x is not None:
             ins.append(x)
             specs.append(spec)
     if panel is not None:
-        ins += list(panel)
-        specs += [HBM, HBM]
+        ins.append(panel)
+        specs.append(HBM)
     if turn is not None:
         ins.append(turn)
         specs.append(HBM)
@@ -341,10 +354,11 @@
         given = [refs.pop(0)]
         given.append(refs.pop(0) if known is not None else None)
         given += [refs.pop(0), refs.pop(0)]
-        given += [refs.pop(0), refs.pop(0)] if panel is not None else [None, None]
-        level_kernel(level, copies, kind, cap, turn is not None, *given, *refs)
-
-    out_shape = [jax.ShapeDtypeStruct((copies, RB, HS, W), jnp.float32)]
+        given.append(refs.pop(0) if panel is not None else None)
+        level_kernel(level, copies, kind, turn is not None, both, *given, *refs)
+
+    shape = (copies, 2, RB, HS, W) if both else (copies, RB, HS, W)
+    out_shape = [jax.ShapeDtypeStruct(shape, jnp.float32)]
     scratch = [pltpu.VMEM((LIST, W, W), jnp.float32), pltpu.VMEM((RB, W, W), jnp.float32)]
     if turn is not None:
         out_shape.append(jax.ShapeDtypeStruct((RB, HS, W), jnp.float32))
@@ -356,7 +370,8 @@
         in_specs=specs,
         out_specs=[VMEM] * len(out_shape),
         scratch_shapes=scratch,
-        compiler_params=pltpu.CompilerParams(vmem_limit_bytes=24 * 1024 * 1024),
+        compiler_params=pltpu.CompilerParams(vmem_limit_bytes=ROOM),
+        cost_estimate=cost(8),
     )(*ins)
     return out if turn is not None else out[0]
 
@@ -390,14 +405,9 @@
         in_specs=[SMEM, VMEM, HBM],
         out_specs=VMEM,
         scratch_shapes=[pltpu.VMEM((NB, W, W), jnp.float32), pltpu.SemaphoreType.DMA((NB,))],
-        compiler_params=pltpu.CompilerParams(vmem_limit_bytes=24 * 1024 * 1024),
+        compiler_params=pltpu.CompilerParams(vmem_limit_bytes=ROOM),
+        cost_estimate=cost(8),
     )(table, known, lower)
-
-
-def gather_panel(packed):
-    here = lax.all_gather(packed, "pcol", axis_index_groups=SAME_CORE, tiled=True)
-    there = lax.ppermute(here, "pcol", [(k, k ^ 1) for k in range(PC)])
-    return here, there
 
 
 def local(rhs, lower, upper, lower_inverse, upper_inverse, pattern, levels, widths):
@@ -408,12 +418,13 @@
     lower_inv = lower_inverse.reshape(RB, W, W)
     upper_inv = upper_inverse.reshape(RB, W, W)
     table = tables(pattern, levels, widths)
-    panel_l = gather_panel(pack(0, CAP_L, table, lower_blocks))
-    panel_u = gather_panel(pack(1, CAP_U, table, upper_blocks))
     swap = lambda x: lax.all_to_all(x, "prow", 0, 0)
 
     b = lax.dynamic_slice_in_dim(right, q * HS, HS, 1)
-    known = swap(level_step(0, PR, 0, table, None, b, lower_inv, None))
+    leaves = level_step(0, PR, 0, table, None, b, lower_inv, None)
+    panel_l = lax.all_gather(pack(0, CAP_L, table, lower_blocks, leaves), "pcol", tiled=True)
+    known = swap(leaves)
+    panel_u = lax.all_gather(pack(1, CAP_U, table, upper_blocks, known), "pcol", tiled=True)
     for level in range(1, LEVELS - 1):
         if level == 3:
             split = known.reshape(2, PC, RB, HS, W).transpose(1, 0, 2, 3, 4)
@@ -422,19 +433,18 @@
             b = b - jnp.sum(sums, axis=0)
         known = swap(level_step(level, PR, 0, table, known, b, lower_inv, panel_l))
     state, forward = level_step(LEVELS - 1, PR, 0, table, known, b, lower_inv, panel_l, upper_inv)
-    full_f = lax.all_gather(forward, "pcol")
     known = swap(state)
     for level in range(LEVELS - 2, 0, -1):
         known = swap(level_step(level, PR, 1, table, known, forward, upper_inv, panel_u))
-    state = level_step(0, PC, 1, table, known, forward, upper_inv, panel_u)
-    full_s = lax.all_to_all(state, "pcol", 0, 0)
+    state = level_step(0, PC, 1, table, known, forward, upper_inv, panel_u, both=True)
+    full = lax.all_to_all(state, "pcol", 0, 0)
     shape = rhs.shape
     whole = lambda x: x.transpose(1, 0, 2, 3).reshape(shape)
     args = (rhs, lower, upper, lower_inverse, upper_inverse, pattern, levels, widths)
     done = lax.while_loop(
         lambda c: c[2] > 0,
         lambda c: general(*args) + (jnp.int32(0),),
-        (whole(full_f), whole(full_s), table[COUNTS, 3]),
+        (whole(full[:, 0]), whole(full[:, 1]), table[COUNTS, 3]),
     )
     return done[0], done[1]
 

time: 389 us -> 297 us (0.76)
  waiting for transfers between devices: 117 us -> 26.4 us
  local copies, waits for them, and re-layouts: 7.86 us -> 3.71 us
    all_gather x2, waiting for transfers between devices: 117 us -> 18.2 us  [the longest x1 18.2 us: local(): lax.all_gather(pack(0, CAP_L, table, lower_blocks, leaves), 'pcol', tiled...]
    all_gather x1 -> x0, blocking collectives: 13.8 us -> none  [local(): full_f = lax.all_gather(forward, 'pcol')]
    all_to_all x1, waiting for transfers between devices: 0.01 us -> 8.13 us  [local(): full = lax.all_to_all(state, 'pcol', 0, 0)]
    all_to_all x10, blocking collectives: 142 us -> 149 us  [local(): swap = lambda x: lax.all_to_all(x, 'prow', 0, 0)]
    all_to_all x1, blocking collectives: 15.2 us -> 20.9 us  [local(): columns = lax.all_to_all(split, 'pcol', 0, 0)]
    unnamed x42 -> x16, local copies, waits for them, and re-layouts: 5.68 us -> 0.04 us
  transfers between devices with their start and end apart: 5 -> 3, of which waited for: 2 -> 2; matrix products, arithmetic and copies ran while one was open for 1% -> 1% of each run, Pallas kernels for 7% -> 7%
where the time goes in v2:
time: 297 us; the launch traced here: 294 us
  blocking collectives  184 us (62%)
  Pallas kernels  50.9 us (17%)
  waiting for transfers between devices  26.4 us (9%)
  between operations  14.2 us (5%)
  starting transfers between devices  12.9 us (4%)
  local copies, waits for them, and re-layouts  3.71 us (1%)
    all_to_all x10, blocking collectives, local(): swap = lambda x: lax.all_to_all(x, 'prow', 0, 0)  149 us
    pallas_call x11, Pallas kernels, level_step(): pl.pallas_call(kernel, out_shape=out_shape, in_specs=specs, out_specs=[VM...  40.2 us
    all_to_all x1, blocking collectives, local(): columns = lax.all_to_all(split, 'pcol', 0, 0)  20.9 us
    all_gather x1, waiting for transfers between devices, local(): lax.all_gather(pack(0, CAP_L, table, lower_blocks, leaves), 'pcol', tiled...  18.2 us
    all_to_all x1, blocking collectives, local(): sums = lax.all_to_all(across(table, columns, lower_blocks), 'pcol', 0, 0)  14.1 us
    all_to_all x1, starting transfers between devices, local(): full = lax.all_to_all(state, 'pcol', 0, 0)  12.8 us
    all_to_all x1, waiting for transfers between devices, local(): full = lax.all_to_all(state, 'pcol', 0, 0)  8.13 us
  transfers between devices with their start and end apart: 3, of which 2 were waited for; matrix products, arithmetic and copies ran while one was open for 1% of the time, Pallas kernels for 7%

profile of v2, /device:TPU:1, one launch (start us, length us, event | category | flops | bytes accessed | tf_op | source)
XLA Modules:
  0.0 293.8 jit_solution(18261507730842867103)
XLA Ops:
  7.2 0.0 all-gather.3.cloned.1.call-start
  7.2 1.4 dynamic-slice_bitcast_fusion.refs_1_.refs_2_
  8.6 2.4 shard_map.95.refs_0_.table
  11.0 3.8 %shard_map.96.refs_2_ = f32[16,8,8,128]{3,2,1,0:T(8,128)} custom-call(s32[16,128]{1,0:T(8,128)} %shard_map.95.refs_0_.table, f32[8,8,128]{2,1,0:T(8,128)} %dynamic-slice_bitcast_fusion.refs_1_.refs_2_, f32[8,128,128]{2,1,0:T(8,128)} %bitcast.278), custom_call_target="tpu_custom_call" | custom-call | bytes 8388608 | tf_op jit(solution)/shard_map/pallas_call | solution.py:367
  14.9 0.0 copy-start.5
  14.9 2.6 shard_map.97
  17.4 0.0 copy-start
  17.5 0.0 all-gather.3.cloned.1.call-update
  17.5 0.0 all-gather.5.cloned.1.call-start
  17.5 0.0 copy-done.5
  17.5 19.0 %all_to_all.65.refs_1_.refs_2_ = f32[16,8,8,128]{3,2,1,0:T(8,128)} all-to-all(f32[16,8,8,128]{3,2,1,0:T(8,128)S(1)} %copy-done.5), channel_id=1, replica_groups=mesh['prow'=16,'pcol'=8] {'prow'}, dimensions={0} | all-to-all | bytes 1048576 | tf_op jit(solution)/shard_map/all_to_all | solution.py:421
  36.6 2.8 shard_map.104
  39.3 0.0 all-gather.5.cloned.1.call-update
  39.4 18.2 %all-gather.3.cloned.1.call-done.refs_4_ = f32[80,128,128]{2,1,0:T(8,128)} async-done(((f32[10,128,128]{2,1,0:T(8,128)}), f32[80,128,128]{2,1,0:T(8,128)}) %all-gather.3.cloned.1.call-update) | async-done | bytes 5242896 | tf_op jit(solution)/shard_map/all_gather | solution.py:425
  57.6 0.0 copy-done
  57.6 5.1 %shard_map.98 = f32[16,8,8,128]{3,2,1,0:T(8,128)} custom-call(s32[16,128]{1,0:T(8,128)} %shard_map.95.refs_0_.table, f32[16,8,8,128]{3,2,1,0:T(8,128)} %all_to_all.65.refs_1_.refs_2_, f32[8,8,128]{2,1,0:T(8,128)} %dynamic-slice_bitcast_fusion.refs_1_.refs_2_, f32[8,128,128]{2,1,0:T(8,128)S(1)} %bitcast.279, f32[80,128,128]{2,1,0:T(8,128)} %all-gather.3.cloned.1.call-done.refs_4_), custom_call_target="tpu_custom_call" | custom-call | bytes 8388608 | tf_op jit(solution)/shard_map/pallas_call | solution.py:367
  62.7 16.9 %all_to_all.66.refs_1_ = f32[16,8,8,128]{3,2,1,0:T(8,128)} all-to-all(f32[16,8,8,128]{3,2,1,0:T(8,128)} %shard_map.98), channel_id=1, replica_groups=mesh['prow'=16,'pcol'=8] {'prow'}, dimensions={0} | all-to-all | bytes 1048576 | tf_op jit(solution)/shard_map/all_to_all | solution.py:421
  79.5 0.0 copy-start.3
  79.5 2.8 shard_map.99
  82.4 15.5 %all_to_all.67.refs_1_ = f32[16,8,8,128]{3,2,1,0:T(8,128)S(1)} all-to-all(f32[16,8,8,128]{3,2,1,0:T(8,128)} %shard_map.99), channel_id=1, replica_groups=mesh['prow'=16,'pcol'=8] {'prow'}, dimensions={0} | all-to-all | bytes 1048576 | tf_op jit(solution)/shard_map/all_to_all | solution.py:421
  97.9 0.0 copy-start.4
  97.9 20.9 %all_to_all.68.known = f32[8,2,8,8,128]{4,3,2,1,0:T(8,128)} all-to-all(f32[8,2,8,8,128]{4,3,2,1,0:T(8,128)S(1)} %bitcast.306), channel_id=1, replica_groups=mesh['prow'=16,'pcol'=8] {'pcol'}, dimensions={0} | all-to-all | bytes 1048576 | tf_op jit(solution)/shard_map/all_to_all | solution.py:431
  118.8 2.9 shard_map.100
  121.7 0.0 copy-start.1
  121.7 14.1 %all_to_all.69 = f32[8,8,8,128]{3,2,1,0:T(8,128)S(1)} all-to-all(f32[8,8,8,128]{3,2,1,0:T(8,128)} %shard_map.100), channel_id=1, replica_groups=mesh['prow'=16,'pcol'=8] {'pcol'}, dimensions={0} | all-to-all | bytes 524288 | tf_op jit(solution)/shard_map/all_to_all | solution.py:432
  135.9 0.0 copy-done.3
  135.9 0.6 fusion.122.refs_2_
  136.5 0.0 copy-done.4
  136.5 2.7 shard_map.101
  139.2 17.2 %all_to_all.70.refs_1_ = f32[16,8,8,128]{3,2,1,0:T(8,128)} all-to-all(f32[16,8,8,128]{3,2,1,0:T(8,128)} %shard_map.101), channel_id=1, replica_groups=mesh['prow'=16,'pcol'=8] {'prow'}, dimensions={0} | all-to-all | bytes 1048576 | tf_op jit(solution)/shard_map/all_to_all | solution.py:421
  156.5 2.7 shard_map.102
  159.2 13.8 %all_to_all.71.refs_1_ = f32[16,8,8,128]{3,2,1,0:T(8,128)} all-to-all(f32[16,8,8,128]{3,2,1,0:T(8,128)} %shard_map.102), channel_id=1, replica_groups=mesh['prow'=16,'pcol'=8] {'prow'}, dimensions={0} | all-to-all | bytes 1048576 | tf_op jit(solution)/shard_map/all_to_all | solution.py:421
  172.9 0.0 copy-done.1
  172.9 2.7 shard_map.103
  175.7 13.2 %all_to_all.72.refs_1_ = f32[16,8,8,128]{3,2,1,0:T(8,128)} all-to-all(f32[16,8,8,128]{3,2,1,0:T(8,128)} %get-tuple-element.59), channel_id=1, replica_groups=mesh['prow'=16,'pcol'=8] {'prow'}, dimensions={0} | all-to-all | bytes 1048576 | tf_op jit(solution)/shard_map/all_to_all | solution.py:421
  188.9 0.0 all-gather.5.cloned.1.call-done.refs_4_
  188.9 2.9 shard_map.105
  191.8 13.3 %all_to_all.73.refs_1_ = f32[16,8,8,128]{3,2,1,0:T(8,128)} all-to-all(f32[16,8,8,128]{3,2,1,0:T(8,128)} %shard_map.105), channel_id=1, replica_groups=mesh['prow'=16,'pcol'=8] {'prow'}, dimensions={0} | all-to-all | bytes 1048576 | tf_op jit(solution)/shard_map/all_to_all | solution.py:421
  205.1 2.7 shard_map.106
  207.9 13.2 %all_to_all.74.refs_1_ = f32[16,8,8,128]{3,2,1,0:T(8,128)} all-to-all(f32[16,8,8,128]{3,2,1,0:T(8,128)} %shard_map.106), channel_id=1, replica_groups=mesh['prow'=16,'pcol'=8] {'prow'}, dimensions={0} | all-to-all | bytes 1048576 | tf_op jit(solution)/shard_map/all_to_all | solution.py:421
  221.1 2.7 shard_map.107
  223.8 13.7 %all_to_all.75.refs_1_ = f32[16,8,8,128]{3,2,1,0:T(8,128)} all-to-all(f32[16,8,8,128]{3,2,1,0:T(8,128)} %shard_map.107), channel_id=1, replica_groups=mesh['prow'=16,'pcol'=8] {'prow'}, dimensions={0} | all-to-all | bytes 1048576 | tf_op jit(solution)/shard_map/all_to_all | solution.py:421
  237.5 6.0 %shard_map.108 = f32[16,8,8,128]{3,2,1,0:T(8,128)} custom-call(s32[16,128]{1,0:T(8,128)} %shard_map.95.refs_0_.table, f32[16,8,8,128]{3,2,1,0:T(8,128)} %all_to_all.75.refs_1_, f32[8,8,128]{2,1,0:T(8,128)} %get-tuple-element.60.refs_2_, f32[8,128,128]{2,1,0:T(8,128)S(1)} %bitcast.289, f32[224,128,128]{2,1,0:T(8,128)} %all-gather.5.cloned.1.call-done.refs_4_), custom_call_target="tpu_custom_call" | custom-call | bytes 8388608 | tf_op jit(solution)/shard_map/pallas_call | solution.py:367
  243.5 13.2 %all_to_all.76.refs_1_ = f32[16,8,8,128]{3,2,1,0:T(8,128)} all-to-all(f32[16,8,8,128]{3,2,1,0:T(8,128)} %shard_map.108), channel_id=1, replica_groups=mesh['prow'=16,'pcol'=8] {'prow'}, dimensions={0} | all-to-all | bytes 1048576 | tf_op jit(solution)/shard_map/all_to_all | solution.py:421
  256.7 0.0 copy-start.6
  256.8 0.0 copy-start.7
  256.8 0.0 copy-start.8
  256.8 6.0 %shard_map.109 = f32[8,2,8,8,128]{4,3,2,1,0:T(8,128)} custom-call(s32[16,128]{1,0:T(8,128)} %shard_map.95.refs_0_.table, f32[16,8,8,128]{3,2,1,0:T(8,128)} %all_to_all.76.refs_1_, f32[8,8,128]{2,1,0:T(8,128)} %get-tuple-element.60.refs_2_, f32[8,128,128]{2,1,0:T(8,128)S(1)} %bitcast.290, f32[224,128,128]{2,1,0:T(8,128)} %all-gather.5.cloned.1.call-done.refs_4_), custom_call_target="tpu_custom_call" | custom-call | bytes 8388608 | tf_op jit(solution)/shard_map/pallas_call | solution.py:367
  262.8 12.8 %all-to-all-start.12 = ((f32[8,2,8,8,128]{4,3,2,1,0:T(8,128)}), f32[8,2,8,8,128]{4,3,2,1,0:T(8,128)S(1)}, u32[]{:S(2)}, u32[]{:S(2)}) async-start(f32[8,2,8,8,128]{4,3,2,1,0:T(8,128)} %shard_map.109), calls=%async_computation.12 | async-start | bytes 1048576 | tf_op jit(solution)/shard_map/all_to_all | solution.py:440
  275.6 1.3 slice.14
  276.9 0.0 copy-done.6
  276.9 0.1 copy.74
  277.0 8.1 %all-to-all-done.12 = f32[8,2,8,8,128]{4,3,2,1,0:T(8,128)S(1)} async-done(((f32[8,2,8,8,128]{4,3,2,1,0:T(8,128)}), f32[8,2,8,8,128]{4,3,2,1,0:T(8,128)S(1)}, u32[]{:S(2)}, u32[]{:S(2)}) %all-to-all-start.12) | async-done | bytes 524320 | tf_op jit(solution)/shard_map/all_to_all | solution.py:440
  285.1 0.9 copy_bitcast_fusion.1
  286.0 0.0 copy-done.7
  286.0 0.0 copy-done.8
  286.0 0.9 while.11
  (3 shorter events, 0.1 us)
Async XLA Ops:
  7.2 50.4 %all-gather.3.cloned.1.call-start = ((), (), s32[]{:S(2)}) async-start(), calls=%async_computation.34 | async-start | bytes 5898240 | tf_op jit(solution)/shard_map/all_gather | solution.py:425
  14.9 2.7 copy-start.5
  17.4 40.2 %copy-start = (f32[8,1,128,128]{3,2,1,0:T(8,128)S(1)}, f32[8,1,128,128]{3,2,1,0:T(8,128)}, u32[]{:S(2)}) copy-start(f32[8,1,128,128]{3,2,1,0:T(8,128)} %param.13) | copy-start | bytes 1572868
  17.5 171.4 %all-gather.5.cloned.1.call-start = ((), (), s32[]{:S(2)}) async-start(), calls=%async_computation.35 | async-start | bytes 16515072 | tf_op jit(solution)/shard_map/all_gather | solution.py:427
  79.5 56.4 %copy-start.3 = (f32[8,1,64,128]{3,2,1,0:T(8,128)S(1)}, f32[8,1,64,128]{3,2,1,0:T(8,128)}, u32[]{:S(2)}) copy-start(f32[8,1,64,128]{3,2,1,0:T(8,128)} %param.10) | copy-start | bytes 786436
  97.9 38.6 %copy-start.4 = (f32[16,8,8,128]{3,2,1,0:T(8,128)}, f32[16,8,8,128]{3,2,1,0:T(8,128)S(1)}, u32[]{:S(2)}) copy-start(f32[16,8,8,128]{3,2,1,0:T(8,128)S(1)} %all_to_all.67.refs_1_) | copy-start | bytes 1572868
  121.7 51.2 %copy-start.1 = (f32[8,1,128,128]{3,2,1,0:T(8,128)S(1)}, f32[8,1,128,128]{3,2,1,0:T(8,128)}, u32[]{:S(2)}) copy-start(f32[8,1,128,128]{3,2,1,0:T(8,128)} %param.14) | copy-start | bytes 1572868
  256.7 20.1 %copy-start.6 = (s32[128,128]{1,0:T(8,128)S(1)}, s32[128,128]{1,0:T(8,128)}, u32[]{:S(2)}) copy-start(s32[128,128]{1,0:T(8,128)} %pattern.1) | copy-start | bytes 196612
  256.8 29.3 %copy-start.7 = (s32[128]{0:T(128)S(1)}, s32[128]{0:T(128)}, u32[]{:S(2)}) copy-start(s32[128]{0:T(128)} %param.16) | copy-start | bytes 1540
  256.8 29.3 %copy-start.8 = (s32[128]{0:T(128)S(1)}, s32[128]{0:T(128)}, u32[]{:S(2)}) copy-start(s32[128]{0:T(128)} %param.17) | copy-start | bytes 1540
  262.8 22.3 %all-to-all-start.12 = ((f32[8,2,8,8,128]{4,3,2,1,0:T(8,128)}), f32[8,2,8,8,128]{4,3,2,1,0:T(8,128)S(1)}, u32[]{:S(2)}, u32[]{:S(2)}) async-start(f32[8,2,8,8,128]{4,3,2,1,0:T(8,128)} %shard_map.109), calls=%async_computation.12 | async-start | bytes 1048576 | tf_op jit(solution)/shard_map/all_to_all | solution.py:440
Sparse Core Ops, SparseCore 0:
  17.6 39.9 all-gather.2
  59.4 84.5 all-gather.4

commit v3 on v2

--- a/solution.py
+++ b/solution.py
@@ -19,11 +19,12 @@
 LIST = 64
 GROUP = 4
 HBM = pl.BlockSpec(memory_space=pl.ANY)
-ROOM = 60 * 1024 * 1024
+ROOM = 52 * 1024 * 1024
 SMEM = pl.BlockSpec(memory_space=pltpu.SMEM)
 VMEM = pl.BlockSpec(memory_space=pltpu.VMEM)
-LEVEL, WIDTH, START_L, END_L, START_U, END_U = range(6)
-LIST_L, LIST_U, LIST_T, PACK_L, PACK_U, COUNTS = range(8, 14)
+WIDTH = 0
+LIST_L, LIST_U, LIST_T, PACK_L, PACK_U, COUNTS, ROWS, STARTS = range(8, 16)
+HALF = 16
 
 
 def spread(value, axis, source):
@@ -164,10 +165,17 @@
         for a in range(RB):
             rows.append(total)
             total = total + sel[a : a + 1]
-        prior = jnp.concatenate(rows, axis=0)
-        start = jnp.sum(prior, axis=1, keepdims=True)
-        end = start + jnp.sum(sel, axis=1, keepdims=True)
-        return start, end, start + dot(sel, ahead), dot(prior, same) + dot(sel, same_ahead)
+        return dot(jnp.concatenate(rows, axis=0), same) + dot(sel, same_ahead)
+
+    def ordered(size):
+        start = jnp.zeros((RB, 1), jnp.float32)
+        below = jnp.zeros((1, NB), jnp.float32)
+        index = iota((RB, 1), 0)
+        for a in range(RB):
+            first = (row_lev[a : a + 1] < row_lev) | ((row_lev[a : a + 1] == row_lev) & (index > a))
+            start = start + flag(first) * size[a : a + 1]
+            below = below + flag(row_lev[a : a + 1] < node[:1]) * size[a : a + 1]
+        return start, below
 
     def listing(sel, place, value, size):
         t = iota((size, NB), 0).astype(jnp.float32)
@@ -185,28 +193,37 @@
         return jnp.sum(jnp.sum(sel, axis=1, keepdims=True), axis=0, keepdims=True)
 
     def panel(sel, cap):
-        start, end, place, rank = ranks(sel)
+        rank = ranks(sel)
+        start, below = ordered(jnp.sum(sel, axis=1, keepdims=True))
+        place = start + dot(sel, ahead)
         slot = (col * cap).astype(jnp.float32) + jnp.minimum(rank, cap - 1.0)
-        listed = listing(sel, place, slot, LIST) * NB + listing(sel, place, node, LIST)
+        listed = listing(sel, place, slot, LIST) * (NB * RB) + listing(sel, place, node, LIST) * RB
+        listed = listed + listing(sel, place, sub.astype(jnp.float32), LIST)
         packed = listing(sel * own, rank, spot, 32)
-        return jnp.minimum(start, LIST), jnp.minimum(end, LIST), listed, packed, jnp.minimum(count(sel * own), cap)
+        return jnp.minimum(below, LIST), listed, packed, jnp.minimum(count(sel * own), cap)
 
     near_p = dot(mine, near)
     high_p = dot(mine, high)
     far_p = dot(mine, far)
-    start_l, end_l, list_l, pack_l, count_l = panel(near_p, CAP_L)
-    start_u, end_u, list_u, pack_u, count_u = panel(high_p, CAP_U)
-    _, _, _, rank_t = ranks(far_p)
-    list_t = listing(far_p * own, rank_t, spot, NB)
+    below_l, list_l, pack_l, count_l = panel(near_p, CAP_L)
+    below_u, list_u, pack_u, count_u = panel(high_p, CAP_U)
+    list_t = listing(far_p * own, ranks(far_p), spot, NB)
     count_t = count(far_p * own)
-    rows = jnp.zeros((RB, NB), jnp.float32)
-    for k, value in enumerate([row_lev, row_wid, start_l, end_l, start_u, end_u]):
-        rows = rows + flag(lane == k) * value
+    rows = flag(lane == WIDTH) * row_wid
     counts = jnp.zeros((1, NB), jnp.float32)
     for k, value in enumerate([count_l, count_u, count_t, full]):
         counts = counts + flag(lane[:1] == k) * value
-    none = jnp.zeros((1, NB), jnp.float32)
-    lists = jnp.concatenate([list_l, list_u, list_t, pack_l, pack_u, counts, none, none], axis=0)
+    spot_of, below_r = ordered(jnp.ones((RB, 1), jnp.float32))
+    order = jnp.zeros((1, NB), jnp.float32)
+    for a in range(RB):
+        order = order + flag(spot_of[a : a + 1] == node[:1]) * a
+
+    def beside(x, y):
+        return jnp.concatenate([x[:, :HALF], y[:, :HALF], jnp.zeros((1, NB - 2 * HALF), jnp.float32)], axis=1)
+
+    order = beside(order, below_r)
+    starts = beside(below_l, below_u)
+    lists = jnp.concatenate([list_l, list_u, list_t, pack_l, pack_u, counts, order, starts], axis=0)
     out[0:8, :] = rows.astype(jnp.int32)
     out[8:16, :] = lists.astype(jnp.int32)
 
@@ -221,7 +238,7 @@
     )(pattern, levels.reshape(1, NB), widths.reshape(1, NB))
 
 
-def pack_kernel(where, cap, table, blocks, _, out, held, sems_in, sems_out):
+def pack_kernel(where, cap, table, blocks, _, out, token, held, sems_in, sems_out):
     count = table[COUNTS, where]
     row = PACK_L + where
 
@@ -233,6 +250,7 @@
         return pltpu.make_async_copy(held.at[t], out.at[t], sems_out.at[t])
 
     pl.loop(0, count)(lambda t: load(t).start())
+    token[...] = jnp.zeros_like(token)
 
     @pl.loop(0, count)
     def _(t):
@@ -245,9 +263,12 @@
 def pack(where, cap, table, blocks, after):
     return pl.pallas_call(
         lambda *refs: pack_kernel(where, cap, *refs),
-        out_shape=jax.ShapeDtypeStruct((cap, W, W), jnp.float32),
+        out_shape=(
+            jax.ShapeDtypeStruct((cap, W, W), jnp.float32),
+            jax.ShapeDtypeStruct((HS, W), jnp.float32),
+        ),
         in_specs=[SMEM, HBM, HBM],
-        out_specs=HBM,
+        out_specs=(HBM, VMEM),
         scratch_shapes=[
             pltpu.VMEM((cap, W, W), jnp.float32),
             pltpu.SemaphoreType.DMA((cap,)),
@@ -257,17 +278,18 @@
     )(table, blocks, after)
 
 
-def level_kernel(level, copies, kind, turn, both, table, known, right, inverse, panel, *rest):
+def level_kernel(level, copies, kind, turn, both, sliced, table, known, right, inverse, panel, less, *rest):
     if turn:
-        inverse_2, out, out_2, blocks, inv, inv_2, sems, isems = rest
+        inverse_2, out, out_2, sums, blocks, inv, inv_2, sems, isems = rest
     else:
-        out, blocks, inv, sems, isems = rest
+        out, sums, blocks, inv, sems, isems = rest
     p = lax.axis_index("prow")
     row = LIST_U if kind else LIST_L
-    first, last = (START_U, END_U) if kind else (START_L, END_L)
+    e0, e1 = table[STARTS, kind * HALF + level], table[STARTS, kind * HALF + level + 1]
+    r0, r1 = table[ROWS, HALF + level], table[ROWS, HALF + level + 1]
 
     def copy(t):
-        return pltpu.make_async_copy(panel.at[table[row, t] >> 7], blocks.at[t], sems.at[t])
+        return pltpu.make_async_copy(panel.at[table[row, t] >> 10], blocks.at[t], sems.at[t])
 
     def icopy(a):
         return pltpu.make_async_copy(inverse.at[a], inv.at[a], isems.at[a])
@@ -275,68 +297,86 @@
     def icopy_2(a):
         return pltpu.make_async_copy(inverse_2.at[a], inv_2.at[a], isems.at[RB + a])
 
+    if panel is not None:
+        pl.loop(e0, e1)(lambda t: copy(t).start())
+
+    @pl.loop(r0, r1)
+    def _(r):
+        icopy(table[ROWS, r]).start()
+        if turn:
+            icopy_2(table[ROWS, r]).start()
+
+    shift = lax.axis_index("pcol") * HS
     for a in range(RB):
-        @pl.when(table[a, LEVEL] == level)
-        def _():
-            if panel is not None:
-                pl.loop(table[a, first], table[a, last])(lambda t: copy(t).start())
-            icopy(a).start()
-            if turn:
-                icopy_2(a).start()
-
-    lane = iota((HS, W), 1)
-    for a in range(RB):
+        mine = right[a, pl.ds(shift, HS)] if sliced else right[a]
+        if less is not None:
+            parts = [less[k, a] for k in range(PC)]
+            while len(parts) > 1:
+                parts = [x + y for x, y in zip(parts[::2], parts[1::2])]
+            mine = mine - parts[0]
+        sums[a] = mine
         old = known[p, a] if known is not None else jnp.zeros((HS, W), jnp.float32)
         for r in range(copies):
             if both:
-                out[r, 0, a] = right[a]
+                out[r, 0, a] = mine
                 out[r, 1, a] = old
             else:
                 out[r, a] = old if not turn else jnp.zeros((HS, W), jnp.float32)
         if turn:
             out_2[a] = old
 
-        @pl.when(table[a, LEVEL] == level)
-        def _():
-            acc = right[a]
-            if panel is not None:
-                start, end = table[a, first], table[a, last]
-
-                def step(g, acc):
-                    xs, ws = [], []
-                    for u in range(GROUP):
-                        t = start + g * GROUP + u
-                        there = t < end
-
-                        @pl.when(there)
-                        def _():
-                            copy(t).wait()
-
-                        t = jnp.minimum(t, end - 1)
-                        node = table[row, t] & (NB - 1)
-                        xs.append(known[node & (PR - 1), node >> 4] * jnp.where(there, 1.0, 0.0))
-                        ws.append(blocks[t])
-                    for u in range(0, GROUP, 2):
-                        x = jnp.concatenate(xs[u : u + 2], axis=1)
-                        acc = acc - dot3(x, jnp.concatenate(ws[u : u + 2], axis=1))
-                    return acc
-
-                acc = lax.fori_loop(0, (end - start + GROUP - 1) // GROUP, step, acc)
-            icopy(a).wait()
-            keep = lane < table[a, WIDTH]
-            fresh = jnp.where(keep, dot3(acc, inv[a]), 0.0)
-            if turn:
-                out_2[a] = fresh
-                icopy_2(a).wait()
-                fresh = jnp.where(keep, dot3(fresh, inv_2[a]), 0.0)
-            for r in range(copies):
-                if both:
-                    out[r, 1, a] = fresh
-                else:
-                    out[r, a] = fresh
-
-
-def level_step(level, copies, kind, table, known, right, inverse, panel, turn=None, both=False):
+    if panel is not None:
+        @pl.loop(0, (e1 - e0 + GROUP - 1) >> 2)
+        def _(g):
+            terms = []
+            for u in range(GROUP):
+                t = e0 + g * GROUP + u
+                there = t < e1
+
+                @pl.when(there)
+                def _():
+                    copy(t).wait()
+
+                t = jnp.minimum(t, e1 - 1)
+                node = (table[row, t] >> 3) & (NB - 1)
+                x = known[node & (PR - 1), node >> 4] * jnp.where(there, 1.0, 0.0)
+                terms.append((table[row, t] & (RB - 1), dot3(x, blocks[t])))
+            for a, term in terms:
+                sums[a] -= term
+
+    lane = iota((HS, W), 1)
+
+    @pl.loop(0, (r1 - r0 + GROUP - 1) >> 2)
+    def _(g):
+        fresh = []
+        for u in range(GROUP):
+            r = r0 + g * GROUP + u
+            there = r < r1
+            a = table[ROWS, jnp.minimum(r, r1 - 1)]
+
+            @pl.when(there)
+            def _():
+                icopy(a).wait()
+                if turn:
+                    icopy_2(a).wait()
+
+            fresh.append((there, a, jnp.where(lane < table[a, WIDTH], dot3(sums[a], inv[a]), 0.0)))
+        if turn:
+            later = [jnp.where(lane < table[a, WIDTH], dot3(x, inv_2[a]), 0.0) for _, a, x in fresh]
+            for there, a, x in fresh:
+                out_2[a] = x
+            fresh = [(there, a, x) for (there, a, _), x in zip(fresh, later)]
+        for there, a, x in fresh:
+            @pl.when(there)
+            def _():
+                for r in range(copies):
+                    if both:
+                        out[r, 1, a] = x
+                    else:
+                        out[r, a] = x
+
+
+def level_step(level, copies, kind, table, known, right, inverse, panel, turn=None, both=False, sliced=False, after=None, less=None):
     ins, specs = [table], [SMEM]
     for x, spec in ((known, VMEM), (right, VMEM), (inverse, HBM)):
         if x is not None:
@@ -345,21 +385,30 @@
     if panel is not None:
         ins.append(panel)
         specs.append(HBM)
+    if less is not None:
+        ins.append(less)
+        specs.append(VMEM)
     if turn is not None:
         ins.append(turn)
         specs.append(HBM)
+    if after is not None:
+        ins.append(after)
+        specs.append(HBM)
 
     def kernel(*refs):
         refs = list(refs)
+        if after is not None:
+            refs.pop(len(ins) - 1)
         given = [refs.pop(0)]
         given.append(refs.pop(0) if known is not None else None)
         given += [refs.pop(0), refs.pop(0)]
         given.append(refs.pop(0) if panel is not None else None)
-        level_kernel(level, copies, kind, turn is not None, both, *given, *refs)
+        given.append(refs.pop(0) if less is not None else None)
+        level_kernel(level, copies, kind, turn is not None, both, sliced, *given, *refs)
 
     shape = (copies, 2, RB, HS, W) if both else (copies, RB, HS, W)
     out_shape = [jax.ShapeDtypeStruct(shape, jnp.float32)]
-    scratch = [pltpu.VMEM((LIST, W, W), jnp.float32), pltpu.VMEM((RB, W, W), jnp.float32)]
+    scratch = [pltpu.VMEM((RB, HS, W), jnp.float32), pltpu.VMEM((LIST, W, W), jnp.float32), pltpu.VMEM((RB, W, W), jnp.float32)]
     if turn is not None:
         out_shape.append(jax.ShapeDtypeStruct((RB, HS, W), jnp.float32))
         scratch.append(pltpu.VMEM((RB, W, W), jnp.float32))
@@ -386,16 +435,24 @@
     pl.loop(0, count)(lambda t: copy(t).start())
     out[...] = jnp.zeros_like(out)
 
-    def step(t, carry):
-        copy(t).wait()
-        n = table[LIST_T, t]
-        a = n >> 4
-        c = n & (CB - 1)
-        x = known[:, c & 1, c >> 1].reshape(NRHS, W)
-        out[:, a] += dot3(x, blocks[t]).reshape(PC, HS, W)
-        return carry
-
-    lax.fori_loop(0, count, step, 0)
+    @pl.loop(0, (count + GROUP - 1) >> 2)
+    def _(g):
+        terms = []
+        for u in range(GROUP):
+            t = g * GROUP + u
+            there = t < count
+
+            @pl.when(there)
+            def _():
+                copy(t).wait()
+
+            t = jnp.minimum(t, count - 1)
+            n = table[LIST_T, t]
+            c = n & (CB - 1)
+            x = known[:, c & 1, c >> 1].reshape(NRHS, W) * jnp.where(there, 1.0, 0.0)
+            terms.append((n >> 4, dot3(x, blocks[t]).reshape(PC, HS, W)))
+        for a, term in terms:
+            out[:, a] += term
 
 
 def across(table, known, lower):
@@ -411,7 +468,6 @@
 
 
 def local(rhs, lower, upper, lower_inverse, upper_inverse, pattern, levels, widths):
-    q = lax.axis_index("pcol")
     right = rhs.reshape(RB, NRHS, W)
     lower_blocks = lower.reshape(RB, CB, W, W)
     upper_blocks = upper.reshape(RB, CB, W, W)
@@ -420,19 +476,23 @@
     table = tables(pattern, levels, widths)
     swap = lambda x: lax.all_to_all(x, "prow", 0, 0)
 
-    b = lax.dynamic_slice_in_dim(right, q * HS, HS, 1)
-    leaves = level_step(0, PR, 0, table, None, b, lower_inv, None)
-    panel_l = lax.all_gather(pack(0, CAP_L, table, lower_blocks, leaves), "pcol", tiled=True)
+    packed_l, token = pack(0, CAP_L, table, lower_blocks, table)
+    panel_l = lax.all_gather(packed_l, "pcol", tiled=True)
+    leaves = level_step(0, PR, 0, table, None, right, lower_inv, None, sliced=True, after=token)
     known = swap(leaves)
-    panel_u = lax.all_gather(pack(1, CAP_U, table, upper_blocks, known), "pcol", tiled=True)
-    for level in range(1, LEVELS - 1):
-        if level == 3:
-            split = known.reshape(2, PC, RB, HS, W).transpose(1, 0, 2, 3, 4)
-            columns = lax.all_to_all(split, "pcol", 0, 0)
-            sums = lax.all_to_all(across(table, columns, lower_blocks), "pcol", 0, 0)
-            b = b - jnp.sum(sums, axis=0)
-        known = swap(level_step(level, PR, 0, table, known, b, lower_inv, panel_l))
-    state, forward = level_step(LEVELS - 1, PR, 0, table, known, b, lower_inv, panel_l, upper_inv)
+    packed_u, _ = pack(1, CAP_U, table, upper_blocks, known[0, 0])
+    panel_u = lax.all_gather(packed_u, "pcol", tiled=True)
+    known = swap(level_step(1, PR, 0, table, known, right, lower_inv, panel_l, sliced=True))
+    known = swap(level_step(2, PR, 0, table, known, right, lower_inv, panel_l, sliced=True))
+    split = known.reshape(2, PC, RB, HS, W).transpose(1, 0, 2, 3, 4)
+    columns = lax.all_to_all(split, "pcol", 0, 0)
+    sums = lax.all_to_all(across(table, columns, lower_blocks), "pcol", 0, 0)
+    step = lambda level, copies, *turn: level_step(
+        level, copies, 0, table, known, right, lower_inv, panel_l, *turn, sliced=True, less=sums
+    )
+    for level in range(3, LEVELS - 1):
+        known = swap(step(level, PR))
+    state, forward = step(LEVELS - 1, PR, upper_inv)
     known = swap(state)
     for level in range(LEVELS - 2, 0, -1):
         known = swap(level_step(level, PR, 1, table, known, forward, upper_inv, panel_u))

time: 297 us -> 284 us (0.956)
  blocking collectives: 184 us -> 177 us
  waiting for transfers between devices: 26.4 us -> 23.1 us
    all_to_all x10, blocking collectives: 149 us -> 143 us  [local(): swap = lambda x: lax.all_to_all(x, 'prow', 0, 0)]
    all_gather x2, waiting for transfers between devices: 18.2 us -> 14.3 us  [the longest x1 14.2 us: local(): panel_l = lax.all_gather(packed_l, 'pcol', tiled=True)]
    pallas_call x11, Pallas kernels: 40.2 us -> 36.5 us  [level_step(): pl.pallas_call(kernel, out_shape=out_shape, in_specs=specs, out_specs=[VM...]
  transfers between devices with their start and end apart: 3 -> 3, of which waited for: 2 -> 2; matrix products, arithmetic and copies ran while one was open for 1% -> 0% of each run, Pallas kernels for 7% -> 9%
where the time goes in v3:
time: 284 us; the launch traced here: 281 us
  blocking collectives  177 us (62%)
  Pallas kernels  49.8 us (18%)
  waiting for transfers between devices  23.1 us (8%)
  between operations  14.3 us (5%)
  starting transfers between devices  13.6 us (5%)
  local copies, waits for them, and re-layouts  2.92 us (1%)
    all_to_all x10, blocking collectives, local(): swap = lambda x: lax.all_to_all(x, 'prow', 0, 0)  143 us
    pallas_call x11, Pallas kernels, level_step(): pl.pallas_call(kernel, out_shape=out_shape, in_specs=specs, out_specs=[VM...  36.5 us
    all_to_all x1, blocking collectives, local(): columns = lax.all_to_all(split, 'pcol', 0, 0)  20.3 us
    all_gather x1, waiting for transfers between devices, local(): panel_l = lax.all_gather(packed_l, 'pcol', tiled=True)  14.2 us
    all_to_all x1, starting transfers between devices, local(): full = lax.all_to_all(state, 'pcol', 0, 0)  13.5 us
    all_to_all x1, blocking collectives, local(): sums = lax.all_to_all(across(table, columns, lower_blocks), 'pcol', 0, 0)  13.1 us
    all_to_all x1, waiting for transfers between devices, local(): full = lax.all_to_all(state, 'pcol', 0, 0)  8.8 us
    pallas_call x2, Pallas kernels, pack(): pl.pallas_call(lambda *refs: pack_kernel(where, cap, *refs), out_shape=(j...  6.54 us
  transfers between devices with their start and end apart: 3, of which 2 were waited for; matrix products, arithmetic and copies ran while one was open for 0% of the time, Pallas kernels for 9%

profile of v3, /device:TPU:1, one launch (start us, length us, event | category | flops | bytes accessed | tf_op | source)
XLA Modules:
  0.0 281.5 jit_solution(11132814111438627796)
XLA Ops:
  7.2 0.0 copy-start.5
  7.2 0.0 copy-start.3
  7.2 0.0 all-gather.3.cloned.1.call-start
  7.2 2.6 shard_map.95.refs_0_.refs_2_.table
  9.8 0.0 copy-start
  9.8 3.2 %shard_map.96 = (f32[10,128,128]{2,1,0:T(8,128)}, f32[8,128]{1,0:T(8,128)}) custom-call(s32[16,128]{1,0:T(8,128)} %shard_map.95.refs_0_.refs_2_.table, f32[8,16,128,128]{3,2,1,0:T(8,128)} %bitcast.273, s32[16,128]{1,0:T(8,128)} %shard_map.95.refs_0_.refs_2_.table), custom_call_target="tpu_custom_call" | custom-call | bytes 4194304 | tf_op jit(solution)/shard_map/pallas_call | solution.py:264
  13.0 0.0 copy-start.1
  13.0 0.0 all-gather.3.cloned.1.call-update
  13.1 0.0 all-gather.5.cloned.1.call-start
  13.1 0.0 copy-done.5
  13.1 0.0 copy-done.3
  13.1 0.0 copy-done
  13.1 0.0 copy-start.2
  13.2 0.7 copy-done.2
  13.8 2.4 shard_map.97
  16.2 18.9 %all_to_all.65.refs_1_ = f32[16,8,8,128]{3,2,1,0:T(8,128)S(1)} all-to-all(f32[16,8,8,128]{3,2,1,0:T(8,128)S(1)} %shard_map.97), channel_id=1, replica_groups=mesh['prow'=16,'pcol'=8] {'prow'}, dimensions={0} | all-to-all | bytes 1048576 | tf_op jit(solution)/shard_map/all_to_all | solution.py:477
  35.1 0.6 slice_bitcast_fusion.2.refs_2_
  35.7 3.3 %shard_map.104 = (f32[28,128,128]{2,1,0:T(8,128)}, f32[8,128]{1,0:T(8,128)}) custom-call(s32[16,128]{1,0:T(8,128)} %shard_map.95.refs_0_.refs_2_.table, f32[8,16,128,128]{3,2,1,0:T(8,128)} %bitcast.276, f32[8,128]{1,0:T(8,128)} %slice_bitcast_fusion.2.refs_2_), custom_call_target="tpu_custom_call" | custom-call | bytes 4194304 | tf_op jit(solution)/shard_map/pallas_call | solution.py:264
  39.1 0.0 all-gather.5.cloned.1.call-update
  39.1 14.2 %all-gather.3.cloned.1.call-done.refs_4_ = f32[80,128,128]{2,1,0:T(8,128)} async-done(((f32[10,128,128]{2,1,0:T(8,128)}), f32[80,128,128]{2,1,0:T(8,128)}) %all-gather.3.cloned.1.call-update) | async-done | bytes 5242896 | tf_op jit(solution)/shard_map/all_gather | solution.py:480
  53.4 0.0 copy-done.1
  53.4 3.5 %shard_map.98 = f32[16,8,8,128]{3,2,1,0:T(8,128)S(1)} custom-call(s32[16,128]{1,0:T(8,128)S(1)} %copy-done.1, f32[16,8,8,128]{3,2,1,0:T(8,128)S(1)} %all_to_all.65.refs_1_, f32[8,64,128]{2,1,0:T(8,128)S(1)} %bitcast.293, f32[8,128,128]{2,1,0:T(8,128)S(1)} %bitcast.279, f32[80,128,128]{2,1,0:T(8,128)} %all-gather.3.cloned.1.call-done.refs_4_), custom_call_target="tpu_custom_call" | custom-call | bytes 8388608 | tf_op jit(solution)/shard_map/pallas_call | solution.py:416
  56.9 17.7 %all_to_all.66.refs_1_ = f32[16,8,8,128]{3,2,1,0:T(8,128)S(1)} all-to-all(f32[16,8,8,128]{3,2,1,0:T(8,128)S(1)} %shard_map.98), channel_id=1, replica_groups=mesh['prow'=16,'pcol'=8] {'prow'}, dimensions={0} | all-to-all | bytes 1048576 | tf_op jit(solution)/shard_map/all_to_all | solution.py:477
  74.6 4.8 %shard_map.99 = f32[16,8,8,128]{3,2,1,0:T(8,128)S(1)} custom-call(s32[16,128]{1,0:T(8,128)S(1)} %copy-done.1, f32[16,8,8,128]{3,2,1,0:T(8,128)S(1)} %all_to_all.66.refs_1_, f32[8,64,128]{2,1,0:T(8,128)S(1)} %bitcast.294, f32[8,128,128]{2,1,0:T(8,128)S(1)} %bitcast.280, f32[80,128,128]{2,1,0:T(8,128)} %all-gather.3.cloned.1.call-done.refs_4_), custom_call_target="tpu_custom_call" | custom-call | bytes 8388608 | tf_op jit(solution)/shard_map/pallas_call | solution.py:416
  79.4 13.4 %all_to_all.67.refs_1_ = f32[16,8,8,128]{3,2,1,0:T(8,128)S(1)} all-to-all(f32[16,8,8,128]{3,2,1,0:T(8,128)S(1)} %shard_map.99), channel_id=1, replica_groups=mesh['prow'=16,'pcol'=8] {'prow'}, dimensions={0} | all-to-all | bytes 1048576 | tf_op jit(solution)/shard_map/all_to_all | solution.py:477
  92.8 20.3 %all_to_all.68.known = f32[8,2,8,8,128]{4,3,2,1,0:T(8,128)S(1)} all-to-all(f32[8,2,8,8,128]{4,3,2,1,0:T(8,128)S(1)} %bitcast.311), channel_id=1, replica_groups=mesh['prow'=16,'pcol'=8] {'pcol'}, dimensions={0} | all-to-all | bytes 1048576 | tf_op jit(solution)/shard_map/all_to_all | solution.py:488
  113.2 4.2 %shard_map.100 = f32[8,8,8,128]{3,2,1,0:T(8,128)S(1)} custom-call(s32[16,128]{1,0:T(8,128)S(1)} %copy-done.1, f32[8,2,8,8,128]{4,3,2,1,0:T(8,128)S(1)} %all_to_all.68.known, f32[8,16,128,128]{3,2,1,0:T(8,128)} %bitcast.274), custom_call_target="tpu_custom_call" | custom-call | bytes 8388608 | tf_op jit(solution)/shard_map/pallas_call | solution.py:459
  117.4 13.1 %all_to_all.69.refs_5_ = f32[8,8,8,128]{3,2,1,0:T(8,128)S(1)} all-to-all(f32[8,8,8,128]{3,2,1,0:T(8,128)S(1)} %shard_map.100), channel_id=1, replica_groups=mesh['prow'=16,'pcol'=8] {'pcol'}, dimensions={0} | all-to-all | bytes 524288 | tf_op jit(solution)/shard_map/all_to_all | solution.py:489
  130.4 0.0 copy-start.4
  130.4 1.5 shard_map.101
  131.9 15.2 %all_to_all.70.refs_1_ = f32[16,8,8,128]{3,2,1,0:T(8,128)S(1)} all-to-all(f32[16,8,8,128]{3,2,1,0:T(8,128)S(1)} %shard_map.101), channel_id=1, replica_groups=mesh['prow'=16,'pcol'=8] {'prow'}, dimensions={0} | all-to-all | bytes 1048576 | tf_op jit(solution)/shard_map/all_to_all | solution.py:477
  147.1 1.5 shard_map.102
  148.6 13.7 %all_to_all.71.refs_1_ = f32[16,8,8,128]{3,2,1,0:T(8,128)S(1)} all-to-all(f32[16,8,8,128]{3,2,1,0:T(8,128)S(1)} %shard_map.102), channel_id=1, replica_groups=mesh['prow'=16,'pcol'=8] {'prow'}, dimensions={0} | all-to-all | bytes 1048576 | tf_op jit(solution)/shard_map/all_to_all | solution.py:477
  162.3 0.0 copy-done.4
  162.3 4.3 %shard_map.103 = (f32[16,8,8,128]{3,2,1,0:T(8,128)S(1)}, f32[8,8,128]{2,1,0:T(8,128)S(1)}) custom-call(s32[16,128]{1,0:T(8,128)S(1)} %copy-done.1, f32[16,8,8,128]{3,2,1,0:T(8,128)S(1)} %all_to_all.71.refs_1_, f32[8,64,128]{2,1,0:T(8,128)S(1)} %bitcast.297, f32[8,128,128]{2,1,0:T(8,128)S(1)} %bitcast.283, ...), custom_call_target="tpu_custom_call" | custom-call | bytes 8388608 | tf_op jit(solution)/shard_map/pallas_call | solution.py:416
  166.6 11.6 %all_to_all.72.refs_1_ = f32[16,8,8,128]{3,2,1,0:T(8,128)S(1)} all-to-all(f32[16,8,8,128]{3,2,1,0:T(8,128)S(1)} %get-tuple-element.64), channel_id=1, replica_groups=mesh['prow'=16,'pcol'=8] {'prow'}, dimensions={0} | all-to-all | bytes 1048576 | tf_op jit(solution)/shard_map/all_to_all | solution.py:477
  178.2 0.0 all-gather.5.cloned.1.call-done.refs_4_
  178.2 1.5 shard_map.105
  179.7 13.9 %all_to_all.73.refs_1_ = f32[16,8,8,128]{3,2,1,0:T(8,128)S(1)} all-to-all(f32[16,8,8,128]{3,2,1,0:T(8,128)S(1)} %shard_map.105), channel_id=1, replica_groups=mesh['prow'=16,'pcol'=8] {'prow'}, dimensions={0} | all-to-all | bytes 1048576 | tf_op jit(solution)/shard_map/all_to_all | solution.py:477
  193.6 1.5 shard_map.106
  195.0 13.4 %all_to_all.74.refs_1_ = f32[16,8,8,128]{3,2,1,0:T(8,128)S(1)} all-to-all(f32[16,8,8,128]{3,2,1,0:T(8,128)S(1)} %shard_map.106), channel_id=1, replica_groups=mesh['prow'=16,'pcol'=8] {'prow'}, dimensions={0} | all-to-all | bytes 1048576 | tf_op jit(solution)/shard_map/all_to_all | solution.py:477
  208.5 4.1 %shard_map.107 = f32[16,8,8,128]{3,2,1,0:T(8,128)S(1)} custom-call(s32[16,128]{1,0:T(8,128)S(1)} %copy-done.1, f32[16,8,8,128]{3,2,1,0:T(8,128)S(1)} %all_to_all.74.refs_1_, f32[8,8,128]{2,1,0:T(8,128)S(1)} %get-tuple-element.65.refs_2_, f32[8,128,128]{2,1,0:T(8,128)S(1)} %bitcast.288, f32[224,128,128]{2,1,0:T(8,128)} %all-gather.5.cloned.1.call-done.refs_4_), custom_call_target="tpu_custom_call" | custom-call | bytes 8388608 | tf_op jit(solution)/shard_map/pallas_call | solution.py:416
  212.6 11.7 %all_to_all.75.refs_1_ = f32[16,8,8,128]{3,2,1,0:T(8,128)S(1)} all-to-all(f32[16,8,8,128]{3,2,1,0:T(8,128)S(1)} %shard_map.107), channel_id=1, replica_groups=mesh['prow'=16,'pcol'=8] {'prow'}, dimensions={0} | all-to-all | bytes 1048576 | tf_op jit(solution)/shard_map/all_to_all | solution.py:477
  224.3 4.8 %shard_map.108 = f32[16,8,8,128]{3,2,1,0:T(8,128)S(1)} custom-call(s32[16,128]{1,0:T(8,128)S(1)} %copy-done.1, f32[16,8,8,128]{3,2,1,0:T(8,128)S(1)} %all_to_all.75.refs_1_, f32[8,8,128]{2,1,0:T(8,128)S(1)} %get-tuple-element.65.refs_2_, f32[8,128,128]{2,1,0:T(8,128)S(1)} %bitcast.289, f32[224,128,128]{2,1,0:T(8,128)} %all-gather.5.cloned.1.call-done.refs_4_), custom_call_target="tpu_custom_call" | custom-call | bytes 8388608 | tf_op jit(solution)/shard_map/pallas_call | solution.py:416
  229.0 13.9 %all_to_all.76.refs_1_ = f32[16,8,8,128]{3,2,1,0:T(8,128)S(1)} all-to-all(f32[16,8,8,128]{3,2,1,0:T(8,128)S(1)} %shard_map.108), channel_id=1, replica_groups=mesh['prow'=16,'pcol'=8] {'prow'}, dimensions={0} | all-to-all | bytes 1048576 | tf_op jit(solution)/shard_map/all_to_all | solution.py:477
  242.9 0.0 copy-start.7
  242.9 0.0 copy-start.8
  242.9 0.0 copy-start.9
  242.9 6.9 %shard_map.109 = f32[8,2,8,8,128]{4,3,2,1,0:T(8,128)} custom-call(s32[16,128]{1,0:T(8,128)S(1)} %copy-done.1, f32[16,8,8,128]{3,2,1,0:T(8,128)S(1)} %all_to_all.76.refs_1_, f32[8,8,128]{2,1,0:T(8,128)S(1)} %get-tuple-element.65.refs_2_, f32[8,128,128]{2,1,0:T(8,128)S(1)} %bitcast.290, f32[224,128,128]{2,1,0:T(8,128)} %all-gather.5.cloned.1.call-done.refs_4_), custom_call_target="tpu_custom_call" | custom-call | bytes 8388608 | tf_op jit(solution)/shard_map/pallas_call | solution.py:416
  249.8 13.5 %all-to-all-start.12 = ((f32[8,2,8,8,128]{4,3,2,1,0:T(8,128)}), f32[8,2,8,8,128]{4,3,2,1,0:T(8,128)S(1)}, u32[]{:S(2)}, u32[]{:S(2)}) async-start(f32[8,2,8,8,128]{4,3,2,1,0:T(8,128)} %shard_map.109), calls=%async_computation.12 | async-start | bytes 1048576 | tf_op jit(solution)/shard_map/all_to_all | solution.py:500
  263.3 0.6 slice.19
  263.9 0.0 copy-done.7
  263.9 0.1 copy.74
  264.0 8.8 %all-to-all-done.12 = f32[8,2,8,8,128]{4,3,2,1,0:T(8,128)S(1)} async-done(((f32[8,2,8,8,128]{4,3,2,1,0:T(8,128)}), f32[8,2,8,8,128]{4,3,2,1,0:T(8,128)S(1)}, u32[]{:S(2)}, u32[]{:S(2)}) %all-to-all-start.12) | async-done | bytes 524320 | tf_op jit(solution)/shard_map/all_to_all | solution.py:500
  272.9 0.8 copy_bitcast_fusion.1
  273.7 0.0 copy-done.8
  273.7 0.0 copy-done.9
  273.7 0.9 while.11
  (2 shorter events, 0.1 us)
Async XLA Ops:
  7.2 6.0 %copy-start.5 = (f32[8,1,64,128]{3,2,1,0:T(8,128)S(1)}, f32[8,1,64,128]{3,2,1,0:T(8,128)}, u32[]{:S(2)}) copy-start(f32[8,1,64,128]{3,2,1,0:T(8,128)} %param.10) | copy-start | bytes 786436
  7.2 6.0 %copy-start.3 = (f32[8,1,128,128]{3,2,1,0:T(8,128)S(1)}, f32[8,1,128,128]{3,2,1,0:T(8,128)}, u32[]{:S(2)}) copy-start(f32[8,1,128,128]{3,2,1,0:T(8,128)} %param.13) | copy-start | bytes 1572868
  7.2 46.2 %all-gather.3.cloned.1.call-start = ((), (), s32[]{:S(2)}) async-start(), calls=%async_computation.34 | async-start | bytes 5898240 | tf_op jit(solution)/shard_map/all_gather | solution.py:480
  9.8 3.3 %copy-start = (s32[16,128]{1,0:T(8,128)S(1)}, s32[16,128]{1,0:T(8,128)}, u32[]{:S(2)}) copy-start(s32[16,128]{1,0:T(8,128)} %shard_map.95.refs_0_.refs_2_.table) | copy-start | bytes 24580
  13.0 40.3 %copy-start.1 = (s32[16,128]{1,0:T(8,128)S(1)}, s32[16,128]{1,0:T(8,128)}, u32[]{:S(2)}) copy-start(s32[16,128]{1,0:T(8,128)} %shard_map.95.refs_0_.refs_2_.table) | copy-start | bytes 24580
  13.1 165.1 %all-gather.5.cloned.1.call-start = ((), (), s32[]{:S(2)}) async-start(), calls=%async_computation.35 | async-start | bytes 16515072 | tf_op jit(solution)/shard_map/all_gather | solution.py:484
  13.1 0.7 copy-start.2
  130.4 31.9 %copy-start.4 = (f32[8,1,128,128]{3,2,1,0:T(8,128)S(1)}, f32[8,1,128,128]{3,2,1,0:T(8,128)}, u32[]{:S(2)}) copy-start(f32[8,1,128,128]{3,2,1,0:T(8,128)} %param.14) | copy-start | bytes 1572868
  242.9 21.0 %copy-start.7 = (s32[128,128]{1,0:T(8,128)S(1)}, s32[128,128]{1,0:T(8,128)}, u32[]{:S(2)}) copy-start(s32[128,128]{1,0:T(8,128)} %pattern.1) | copy-start | bytes 196612
  242.9 30.8 %copy-start.8 = (s32[128]{0:T(128)S(1)}, s32[128]{0:T(128)}, u32[]{:S(2)}) copy-start(s32[128]{0:T(128)} %param.16) | copy-start | bytes 1540
  242.9 30.8 %copy-start.9 = (s32[128]{0:T(128)S(1)}, s32[128]{0:T(128)}, u32[]{:S(2)}) copy-start(s32[128]{0:T(128)} %param.17) | copy-start | bytes 1540
  249.8 23.0 %all-to-all-start.12 = ((f32[8,2,8,8,128]{4,3,2,1,0:T(8,128)}), f32[8,2,8,8,128]{4,3,2,1,0:T(8,128)S(1)}, u32[]{:S(2)}, u32[]{:S(2)}) async-start(f32[8,2,8,8,128]{4,3,2,1,0:T(8,128)} %shard_map.109), calls=%async_computation.12 | async-start | bytes 1048576 | tf_op jit(solution)/shard_map/all_to_all | solution.py:500
Sparse Core Ops, SparseCore 0:
  13.2 40.1 all-gather.2
  55.2 84.6 all-gather.4

commit v4 on v3

--- a/solution.py
+++ b/solution.py
@@ -167,14 +167,14 @@
             total = total + sel[a : a + 1]
         return dot(jnp.concatenate(rows, axis=0), same) + dot(sel, same_ahead)
 
-    def ordered(size):
+    def ordered():
         start = jnp.zeros((RB, 1), jnp.float32)
         below = jnp.zeros((1, NB), jnp.float32)
         index = iota((RB, 1), 0)
         for a in range(RB):
             first = (row_lev[a : a + 1] < row_lev) | ((row_lev[a : a + 1] == row_lev) & (index > a))
-            start = start + flag(first) * size[a : a + 1]
-            below = below + flag(row_lev[a : a + 1] < node[:1]) * size[a : a + 1]
+            start = start + flag(first)
+            below = below + flag(row_lev[a : a + 1] < node[:1])
         return start, below
 
     def listing(sel, place, value, size):
@@ -192,10 +192,22 @@
     def count(sel):
         return jnp.sum(jnp.sum(sel, axis=1, keepdims=True), axis=0, keepdims=True)
 
-    def panel(sel, cap):
+    def by_step(sel, step):
+        parts = jnp.concatenate([sel * flag(step == k) for k in range(LEVELS)], axis=0)
+        size = RB * LEVELS
+        earlier = flag(iota((size, size), 0) > iota((size, size), 1))
+        base = jnp.sum(dot(earlier, parts), axis=1, keepdims=True)
+        spread = parts * (dot(parts, ahead) + base)
+        place = jnp.zeros((RB, NB), jnp.float32)
+        below = jnp.zeros((1, NB), jnp.float32)
+        for k in range(LEVELS):
+            place = place + spread[RB * k : RB * (k + 1)]
+            below = below + flag(node[:1] == k) * base[RB * k : RB * k + 1]
+        return place, below + flag(node[:1] == LEVELS) * count(sel)
+
+    def panel(sel, cap, step):
         rank = ranks(sel)
-        start, below = ordered(jnp.sum(sel, axis=1, keepdims=True))
-        place = start + dot(sel, ahead)
+        place, below = by_step(sel, step)
         slot = (col * cap).astype(jnp.float32) + jnp.minimum(rank, cap - 1.0)
         listed = listing(sel, place, slot, LIST) * (NB * RB) + listing(sel, place, node, LIST) * RB
         listed = listed + listing(sel, place, sub.astype(jnp.float32), LIST)
@@ -205,15 +217,19 @@
     near_p = dot(mine, near)
     high_p = dot(mine, high)
     far_p = dot(mine, far)
-    below_l, list_l, pack_l, count_l = panel(near_p, CAP_L)
-    below_u, list_u, pack_u, count_u = panel(high_p, CAP_U)
+    top = jnp.where(row_lev > 2.5, row_lev, jnp.where(row_lev > 0.5, 4.0, 3.0))
+    fourth = jnp.minimum(jnp.maximum(row_lev, 2.0), 3.0)
+    third = jnp.minimum(jnp.maximum(row_lev, 1.0), 2.0)
+    down = jnp.where(lev > 4.5, top, jnp.where(lev > 3.5, fourth, jnp.where(lev > 2.5, third, row_lev)))
+    below_l, list_l, pack_l, count_l = panel(near_p, CAP_L, row_lev + 0.0 * node)
+    below_u, list_u, pack_u, count_u = panel(high_p, CAP_U, down)
     list_t = listing(far_p * own, ranks(far_p), spot, NB)
     count_t = count(far_p * own)
     rows = flag(lane == WIDTH) * row_wid
     counts = jnp.zeros((1, NB), jnp.float32)
     for k, value in enumerate([count_l, count_u, count_t, full]):
         counts = counts + flag(lane[:1] == k) * value
-    spot_of, below_r = ordered(jnp.ones((RB, 1), jnp.float32))
+    spot_of, below_r = ordered()
     order = jnp.zeros((1, NB), jnp.float32)
     for a in range(RB):
         order = order + flag(spot_of[a : a + 1] == node[:1]) * a
@@ -278,7 +294,7 @@
     )(table, blocks, after)
 
 
-def level_kernel(level, copies, kind, turn, both, sliced, table, known, right, inverse, panel, less, *rest):
+def level_kernel(level, copies, kind, turn, both, sliced, group, table, known, right, inverse, panel, less, *rest):
     if turn:
         inverse_2, out, out_2, sums, blocks, inv, inv_2, sems, isems = rest
     else:
@@ -309,7 +325,7 @@
     shift = lax.axis_index("pcol") * HS
     for a in range(RB):
         mine = right[a, pl.ds(shift, HS)] if sliced else right[a]
-        if less is not None:
+        if less is not None and not both:
             parts = [less[k, a] for k in range(PC)]
             while len(parts) > 1:
                 parts = [x + y for x, y in zip(parts[::2], parts[1::2])]
@@ -318,7 +334,7 @@
         old = known[p, a] if known is not None else jnp.zeros((HS, W), jnp.float32)
         for r in range(copies):
             if both:
-                out[r, 0, a] = mine
+                out[r, 0, a] = less[a]
                 out[r, 1, a] = old
             else:
                 out[r, a] = old if not turn else jnp.zeros((HS, W), jnp.float32)
@@ -326,11 +342,11 @@
             out_2[a] = old
 
     if panel is not None:
-        @pl.loop(0, (e1 - e0 + GROUP - 1) >> 2)
+        @pl.loop(0, (e1 - e0 + group - 1) // group)
         def _(g):
             terms = []
-            for u in range(GROUP):
-                t = e0 + g * GROUP + u
+            for u in range(group):
+                t = e0 + g * group + u
                 there = t < e1
 
                 @pl.when(there)
@@ -376,7 +392,7 @@
                         out[r, a] = x
 
 
-def level_step(level, copies, kind, table, known, right, inverse, panel, turn=None, both=False, sliced=False, after=None, less=None):
+def level_step(level, copies, kind, table, known, right, inverse, panel, turn=None, both=False, sliced=False, after=None, less=None, group=GROUP):
     ins, specs = [table], [SMEM]
     for x, spec in ((known, VMEM), (right, VMEM), (inverse, HBM)):
         if x is not None:
@@ -404,11 +420,15 @@
         given += [refs.pop(0), refs.pop(0)]
         given.append(refs.pop(0) if panel is not None else None)
         given.append(refs.pop(0) if less is not None else None)
-        level_kernel(level, copies, kind, turn is not None, both, sliced, *given, *refs)
+        level_kernel(level, copies, kind, turn is not None, both, sliced, group, *given, *refs)
 
     shape = (copies, 2, RB, HS, W) if both else (copies, RB, HS, W)
     out_shape = [jax.ShapeDtypeStruct(shape, jnp.float32)]
-    scratch = [pltpu.VMEM((RB, HS, W), jnp.float32), pltpu.VMEM((LIST, W, W), jnp.float32), pltpu.VMEM((RB, W, W), jnp.float32)]
+    carry = kind == 1 and not both
+    sums = [] if carry else [pltpu.VMEM((RB, HS, W), jnp.float32)]
+    if carry:
+        out_shape.append(jax.ShapeDtypeStruct((RB, HS, W), jnp.float32))
+    scratch = sums + [pltpu.VMEM((LIST, W, W), jnp.float32), pltpu.VMEM((RB, W, W), jnp.float32)]
     if turn is not None:
         out_shape.append(jax.ShapeDtypeStruct((RB, HS, W), jnp.float32))
         scratch.append(pltpu.VMEM((RB, W, W), jnp.float32))
@@ -422,7 +442,7 @@
         compiler_params=pltpu.CompilerParams(vmem_limit_bytes=ROOM),
         cost_estimate=cost(8),
     )(*ins)
-    return out if turn is not None else out[0]
+    return out if len(out) > 1 else out[0]
 
 
 def across_kernel(table, known, lower, out, blocks, sems):
@@ -482,8 +502,8 @@
     known = swap(leaves)
     packed_u, _ = pack(1, CAP_U, table, upper_blocks, known[0, 0])
     panel_u = lax.all_gather(packed_u, "pcol", tiled=True)
-    known = swap(level_step(1, PR, 0, table, known, right, lower_inv, panel_l, sliced=True))
-    known = swap(level_step(2, PR, 0, table, known, right, lower_inv, panel_l, sliced=True))
+    known = swap(level_step(1, PR, 0, table, known, right, lower_inv, panel_l, sliced=True, group=8))
+    known = swap(level_step(2, PR, 0, table, known, right, lower_inv, panel_l, sliced=True, group=8))
     split = known.reshape(2, PC, RB, HS, W).transpose(1, 0, 2, 3, 4)
     columns = lax.all_to_all(split, "pcol", 0, 0)
     sums = lax.all_to_all(across(table, columns, lower_blocks), "pcol", 0, 0)
@@ -494,9 +514,11 @@
         known = swap(step(level, PR))
     state, forward = step(LEVELS - 1, PR, upper_inv)
     known = swap(state)
+    left = forward
     for level in range(LEVELS - 2, 0, -1):
-        known = swap(level_step(level, PR, 1, table, known, forward, upper_inv, panel_u))
-    state = level_step(0, PC, 1, table, known, forward, upper_inv, panel_u, both=True)
+        state, left = level_step(level, PR, 1, table, known, left, upper_inv, panel_u, group=8)
+        known = swap(state)
+    state = level_step(0, PC, 1, table, known, left, upper_inv, panel_u, both=True, less=forward, group=8)
     full = lax.all_to_all(state, "pcol", 0, 0)
     shape = rhs.shape
     whole = lambda x: x.transpose(1, 0, 2, 3).reshape(shape)

time: 284 us -> 286 us (level)
  blocking collectives: 177 us -> 181 us
    pallas_call x11, Pallas kernels: 36.5 us -> 41.7 us  [level_step(): pl.pallas_call(kernel, out_shape=out_shape, in_specs=specs, out_specs=[VM...]
    all_to_all x10, blocking collectives: 143 us -> 147 us  [local(): swap = lambda x: lax.all_to_all(x, 'prow', 0, 0)]
  transfers between devices with their start and end apart: 3 -> 3, of which waited for: 2 -> 2; matrix products, arithmetic and copies ran while one was open for 0% -> 0% of each run, Pallas kernels for 9% -> 8%
where the time goes in v4:
time: 286 us; the launch traced here: 285 us
  blocking collectives  181 us (63%)
  Pallas kernels  51.4 us (18%)
  waiting for transfers between devices  21.1 us (7%)
  between operations  14.3 us (5%)
  starting transfers between devices  13.9 us (5%)
  local copies, waits for them, and re-layouts  2.92 us (1%)
    all_to_all x10, blocking collectives, local(): swap = lambda x: lax.all_to_all(x, 'prow', 0, 0)  147 us
    pallas_call x11, Pallas kernels, level_step(): pl.pallas_call(kernel, out_shape=out_shape, in_specs=specs, out_specs=[VM...  41.7 us
    all_to_all x1, blocking collectives, local(): columns = lax.all_to_all(split, 'pcol', 0, 0)  20.6 us
    all_to_all x1, starting transfers between devices, local(): full = lax.all_to_all(state, 'pcol', 0, 0)  13.8 us
    all_to_all x1, blocking collectives, local(): sums = lax.all_to_all(across(table, columns, lower_blocks), 'pcol', 0, 0)  13.1 us
    all_gather x1, waiting for transfers between devices, local(): panel_l = lax.all_gather(packed_l, 'pcol', tiled=True)  12.3 us
    all_to_all x1, waiting for transfers between devices, local(): full = lax.all_to_all(state, 'pcol', 0, 0)  8.81 us
  transfers between devices with their start and end apart: 3, of which 2 were waited for; matrix products, arithmetic and copies ran while one was open for 0% of the time, Pallas kernels for 8%

profile of v4, /device:TPU:1, one launch (start us, length us, event | category | flops | bytes accessed | tf_op | source)
XLA Modules:
  0.0 285.4 jit_solution(855636712080771558)
XLA Ops:
  7.2 0.0 copy-start.5
  7.2 0.0 copy-start.3
  7.2 0.0 all-gather.3.cloned.1.call-start
  7.2 2.7 shard_map.95.refs_0_.refs_2_.table
  9.9 0.0 copy-start
  9.9 1.7 shard_map.96
  11.7 0.0 copy-start.1
  11.7 0.0 all-gather.3.cloned.1.call-update
  11.7 0.0 all-gather.5.cloned.1.call-start
  11.7 0.0 copy-done.5
  11.7 0.0 copy-done.3
  11.8 0.0 copy-done
  11.8 0.0 copy-start.2
  11.8 0.7 copy-done.2
  12.5 3.2 %shard_map.97 = f32[16,8,8,128]{3,2,1,0:T(8,128)S(1)} custom-call(s32[16,128]{1,0:T(8,128)S(1)} %copy-done, f32[8,64,128]{2,1,0:T(8,128)S(1)} %bitcast.292, f32[8,128,128]{2,1,0:T(8,128)S(1)} %bitcast.278, f32[8,128]{1,0:T(8,128)S(1)} %copy-done.2), custom_call_target="tpu_custom_call" | custom-call | bytes 8388608 | tf_op jit(solution)/shard_map/pallas_call | solution.py:436
  15.7 21.2 %all_to_all.65.refs_1_ = f32[16,8,8,128]{3,2,1,0:T(8,128)S(1)} all-to-all(f32[16,8,8,128]{3,2,1,0:T(8,128)S(1)} %shard_map.97), channel_id=1, replica_groups=mesh['prow'=16,'pcol'=8] {'prow'}, dimensions={0} | all-to-all | bytes 1048576 | tf_op jit(solution)/shard_map/all_to_all | solution.py:497
  36.9 0.6 slice_bitcast_fusion.2.refs_2_
  37.5 3.5 %shard_map.104 = (f32[28,128,128]{2,1,0:T(8,128)}, f32[8,128]{1,0:T(8,128)}) custom-call(s32[16,128]{1,0:T(8,128)} %shard_map.95.refs_0_.refs_2_.table, f32[8,16,128,128]{3,2,1,0:T(8,128)} %bitcast.276, f32[8,128]{1,0:T(8,128)} %slice_bitcast_fusion.2.refs_2_), custom_call_target="tpu_custom_call" | custom-call | bytes 4194304 | tf_op jit(solution)/shard_map/pallas_call | solution.py:280
  41.0 0.0 all-gather.5.cloned.1.call-update
  41.0 12.3 %all-gather.3.cloned.1.call-done.refs_4_ = f32[80,128,128]{2,1,0:T(8,128)} async-done(((f32[10,128,128]{2,1,0:T(8,128)}), f32[80,128,128]{2,1,0:T(8,128)}) %all-gather.3.cloned.1.call-update) | async-done | bytes 5242896 | tf_op jit(solution)/shard_map/all_gather | solution.py:500
  53.3 0.0 copy-done.1
  53.3 4.1 %shard_map.98 = f32[16,8,8,128]{3,2,1,0:T(8,128)S(1)} custom-call(s32[16,128]{1,0:T(8,128)S(1)} %copy-done.1, f32[16,8,8,128]{3,2,1,0:T(8,128)S(1)} %all_to_all.65.refs_1_, f32[8,64,128]{2,1,0:T(8,128)S(1)} %bitcast.293, f32[8,128,128]{2,1,0:T(8,128)S(1)} %bitcast.279, f32[80,128,128]{2,1,0:T(8,128)} %all-gather.3.cloned.1.call-done.refs_4_), custom_call_target="tpu_custom_call" | custom-call | bytes 8388608 | tf_op jit(solution)/shard_map/pallas_call | solution.py:436
  57.4 17.7 %all_to_all.66.refs_1_ = f32[16,8,8,128]{3,2,1,0:T(8,128)S(1)} all-to-all(f32[16,8,8,128]{3,2,1,0:T(8,128)S(1)} %shard_map.98), channel_id=1, replica_groups=mesh['prow'=16,'pcol'=8] {'prow'}, dimensions={0} | all-to-all | bytes 1048576 | tf_op jit(solution)/shard_map/all_to_all | solution.py:497
  75.2 5.4 %shard_map.99 = f32[16,8,8,128]{3,2,1,0:T(8,128)S(1)} custom-call(s32[16,128]{1,0:T(8,128)S(1)} %copy-done.1, f32[16,8,8,128]{3,2,1,0:T(8,128)S(1)} %all_to_all.66.refs_1_, f32[8,64,128]{2,1,0:T(8,128)S(1)} %bitcast.294, f32[8,128,128]{2,1,0:T(8,128)S(1)} %bitcast.280, f32[80,128,128]{2,1,0:T(8,128)} %all-gather.3.cloned.1.call-done.refs_4_), custom_call_target="tpu_custom_call" | custom-call | bytes 8388608 | tf_op jit(solution)/shard_map/pallas_call | solution.py:436
  80.6 12.7 %all_to_all.67.refs_1_ = f32[16,8,8,128]{3,2,1,0:T(8,128)S(1)} all-to-all(f32[16,8,8,128]{3,2,1,0:T(8,128)S(1)} %shard_map.99), channel_id=1, replica_groups=mesh['prow'=16,'pcol'=8] {'prow'}, dimensions={0} | all-to-all | bytes 1048576 | tf_op jit(solution)/shard_map/all_to_all | solution.py:497
  93.3 20.6 %all_to_all.68.known = f32[8,2,8,8,128]{4,3,2,1,0:T(8,128)S(1)} all-to-all(f32[8,2,8,8,128]{4,3,2,1,0:T(8,128)S(1)} %bitcast.311), channel_id=1, replica_groups=mesh['prow'=16,'pcol'=8] {'pcol'}, dimensions={0} | all-to-all | bytes 1048576 | tf_op jit(solution)/shard_map/all_to_all | solution.py:508
  113.9 1.8 shard_map.100
  115.7 13.1 %all_to_all.69.refs_5_ = f32[8,8,8,128]{3,2,1,0:T(8,128)S(1)} all-to-all(f32[8,8,8,128]{3,2,1,0:T(8,128)S(1)} %shard_map.100), channel_id=1, replica_groups=mesh['prow'=16,'pcol'=8] {'pcol'}, dimensions={0} | all-to-all | bytes 524288 | tf_op jit(solution)/shard_map/all_to_all | solution.py:509
  128.8 0.0 copy-start.4
  128.8 1.5 shard_map.101
  130.3 16.9 %all_to_all.70.refs_1_ = f32[16,8,8,128]{3,2,1,0:T(8,128)S(1)} all-to-all(f32[16,8,8,128]{3,2,1,0:T(8,128)S(1)} %shard_map.101), channel_id=1, replica_groups=mesh['prow'=16,'pcol'=8] {'prow'}, dimensions={0} | all-to-all | bytes 1048576 | tf_op jit(solution)/shard_map/all_to_all | solution.py:497
  147.2 1.5 shard_map.102
  148.6 13.1 %all_to_all.71.refs_1_ = f32[16,8,8,128]{3,2,1,0:T(8,128)S(1)} all-to-all(f32[16,8,8,128]{3,2,1,0:T(8,128)S(1)} %shard_map.102), channel_id=1, replica_groups=mesh['prow'=16,'pcol'=8] {'prow'}, dimensions={0} | all-to-all | bytes 1048576 | tf_op jit(solution)/shard_map/all_to_all | solution.py:497
  161.8 0.0 copy-done.4
  161.8 1.5 shard_map.103
  163.2 15.1 %all_to_all.72.refs_1_ = f32[16,8,8,128]{3,2,1,0:T(8,128)S(1)} all-to-all(f32[16,8,8,128]{3,2,1,0:T(8,128)S(1)} %get-tuple-element.72), channel_id=1, replica_groups=mesh['prow'=16,'pcol'=8] {'prow'}, dimensions={0} | all-to-all | bytes 1048576 | tf_op jit(solution)/shard_map/all_to_all | solution.py:497
  178.3 0.0 all-gather.5.cloned.1.call-done.refs_4_
  178.3 3.5 %shard_map.105 = (f32[16,8,8,128]{3,2,1,0:T(8,128)S(1)}, f32[8,8,128]{2,1,0:T(8,128)S(1)}) custom-call(s32[16,128]{1,0:T(8,128)S(1)} %copy-done.1, f32[16,8,8,128]{3,2,1,0:T(8,128)S(1)} %all_to_all.72.refs_1_, f32[8,8,128]{2,1,0:T(8,128)S(1)} %get-tuple-element.73.refs_2_.refs_5_, f32[8,128,128]{2,1,0:T(8,128)S(1)} %bitcast.286, ...), custom_call_target="tpu_custom_call" | custom-call | bytes 8388608 | tf_op jit(solution)/shard_map/pallas_call | solution.py:436
  181.8 12.7 %all_to_all.73.refs_1_ = f32[16,8,8,128]{3,2,1,0:T(8,128)S(1)} all-to-all(f32[16,8,8,128]{3,2,1,0:T(8,128)S(1)} %get-tuple-element.75), channel_id=1, replica_groups=mesh['prow'=16,'pcol'=8] {'prow'}, dimensions={0} | all-to-all | bytes 1048576 | tf_op jit(solution)/shard_map/all_to_all | solution.py:497
  194.6 4.8 %shard_map.106 = (f32[16,8,8,128]{3,2,1,0:T(8,128)S(1)}, f32[8,8,128]{2,1,0:T(8,128)S(1)}) custom-call(s32[16,128]{1,0:T(8,128)S(1)} %copy-done.1, f32[16,8,8,128]{3,2,1,0:T(8,128)S(1)} %all_to_all.73.refs_1_, f32[8,8,128]{2,1,0:T(8,128)S(1)} %get-tuple-element.76.refs_2_, f32[8,128,128]{2,1,0:T(8,128)S(1)} %bitcast.287, ...), custom_call_target="tpu_custom_call" | custom-call | bytes 8388608 | tf_op jit(solution)/shard_map/pallas_call | solution.py:436
  199.3 13.3 %all_to_all.74.refs_1_ = f32[16,8,8,128]{3,2,1,0:T(8,128)S(1)} all-to-all(f32[16,8,8,128]{3,2,1,0:T(8,128)S(1)} %get-tuple-element.77), channel_id=1, replica_groups=mesh['prow'=16,'pcol'=8] {'prow'}, dimensions={0} | all-to-all | bytes 1048576 | tf_op jit(solution)/shard_map/all_to_all | solution.py:497
  212.6 5.4 %shard_map.107 = (f32[16,8,8,128]{3,2,1,0:T(8,128)S(1)}, f32[8,8,128]{2,1,0:T(8,128)S(1)}) custom-call(s32[16,128]{1,0:T(8,128)S(1)} %copy-done.1, f32[16,8,8,128]{3,2,1,0:T(8,128)S(1)} %all_to_all.74.refs_1_, f32[8,8,128]{2,1,0:T(8,128)S(1)} %get-tuple-element.78.refs_2_, f32[8,128,128]{2,1,0:T(8,128)S(1)} %bitcast.288, ...), custom_call_target="tpu_custom_call" | custom-call | bytes 8388608 | tf_op jit(solution)/shard_map/pallas_call | solution.py:436
  218.0 11.6 %all_to_all.75.refs_1_ = f32[16,8,8,128]{3,2,1,0:T(8,128)S(1)} all-to-all(f32[16,8,8,128]{3,2,1,0:T(8,128)S(1)} %get-tuple-element.79), channel_id=1, replica_groups=mesh['prow'=16,'pcol'=8] {'prow'}, dimensions={0} | all-to-all | bytes 1048576 | tf_op jit(solution)/shard_map/all_to_all | solution.py:497
  229.6 4.1 %shard_map.108 = (f32[16,8,8,128]{3,2,1,0:T(8,128)S(1)}, f32[8,8,128]{2,1,0:T(8,128)S(1)}) custom-call(s32[16,128]{1,0:T(8,128)S(1)} %copy-done.1, f32[16,8,8,128]{3,2,1,0:T(8,128)S(1)} %all_to_all.75.refs_1_, f32[8,8,128]{2,1,0:T(8,128)S(1)} %get-tuple-element.80.refs_2_, f32[8,128,128]{2,1,0:T(8,128)S(1)} %bitcast.289, ...), custom_call_target="tpu_custom_call" | custom-call | bytes 8388608 | tf_op jit(solution)/shard_map/pallas_call | solution.py:436
  233.7 12.9 %all_to_all.76.refs_1_ = f32[16,8,8,128]{3,2,1,0:T(8,128)S(1)} all-to-all(f32[16,8,8,128]{3,2,1,0:T(8,128)S(1)} %get-tuple-element.81), channel_id=1, replica_groups=mesh['prow'=16,'pcol'=8] {'prow'}, dimensions={0} | all-to-all | bytes 1048576 | tf_op jit(solution)/shard_map/all_to_all | solution.py:497
  246.7 0.0 copy-start.7
  246.7 0.0 copy-start.8
  246.7 0.0 copy-start.9
  246.7 6.8 %shard_map.109 = f32[8,2,8,8,128]{4,3,2,1,0:T(8,128)} custom-call(s32[16,128]{1,0:T(8,128)S(1)} %copy-done.1, f32[16,8,8,128]{3,2,1,0:T(8,128)S(1)} %all_to_all.76.refs_1_, f32[8,8,128]{2,1,0:T(8,128)S(1)} %get-tuple-element.82.refs_2_, f32[8,128,128]{2,1,0:T(8,128)S(1)} %bitcast.290, f32[224,128,128]{2,1,0:T(8,128)} %all-gather.5.cloned.1.call-done.refs_4_, ...), custom_call_target="tpu_custom_call" | custom-call | bytes 8388608 | tf_op jit(solution)/shard_map/pallas_call | solution.py:436
  253.5 13.8 %all-to-all-start.12 = ((f32[8,2,8,8,128]{4,3,2,1,0:T(8,128)}), f32[8,2,8,8,128]{4,3,2,1,0:T(8,128)S(1)}, u32[]{:S(2)}, u32[]{:S(2)}) async-start(f32[8,2,8,8,128]{4,3,2,1,0:T(8,128)} %shard_map.109), calls=%async_computation.12 | async-start | bytes 1048576 | tf_op jit(solution)/shard_map/all_to_all | solution.py:522
  267.3 0.6 slice.19
  267.9 0.0 copy-done.7
  267.9 0.1 copy.74
  268.0 8.8 %all-to-all-done.12 = f32[8,2,8,8,128]{4,3,2,1,0:T(8,128)S(1)} async-done(((f32[8,2,8,8,128]{4,3,2,1,0:T(8,128)}), f32[8,2,8,8,128]{4,3,2,1,0:T(8,128)S(1)}, u32[]{:S(2)}, u32[]{:S(2)}) %all-to-all-start.12) | async-done | bytes 524320 | tf_op jit(solution)/shard_map/all_to_all | solution.py:522
  276.8 0.8 copy_bitcast_fusion.1
  277.7 0.0 copy-done.8
  277.7 0.0 copy-done.9
  277.7 0.8 while.11
  (2 shorter events, 0.1 us)
Async XLA Ops:
  7.2 4.6 %copy-start.5 = (f32[8,1,64,128]{3,2,1,0:T(8,128)S(1)}, f32[8,1,64,128]{3,2,1,0:T(8,128)}, u32[]{:S(2)}) copy-start(f32[8,1,64,128]{3,2,1,0:T(8,128)} %param.10) | copy-start | bytes 786436
  7.2 4.6 %copy-start.3 = (f32[8,1,128,128]{3,2,1,0:T(8,128)S(1)}, f32[8,1,128,128]{3,2,1,0:T(8,128)}, u32[]{:S(2)}) copy-start(f32[8,1,128,128]{3,2,1,0:T(8,128)} %param.13) | copy-start | bytes 1572868
  7.2 46.1 %all-gather.3.cloned.1.call-start = ((), (), s32[]{:S(2)}) async-start(), calls=%async_computation.34 | async-start | bytes 5898240 | tf_op jit(solution)/shard_map/all_gather | solution.py:500
  9.9 1.8 copy-start
  11.7 41.7 %copy-start.1 = (s32[16,128]{1,0:T(8,128)S(1)}, s32[16,128]{1,0:T(8,128)}, u32[]{:S(2)}) copy-start(s32[16,128]{1,0:T(8,128)} %shard_map.95.refs_0_.refs_2_.table) | copy-start | bytes 24580
  11.7 166.7 %all-gather.5.cloned.1.call-start = ((), (), s32[]{:S(2)}) async-start(), calls=%async_computation.35 | async-start | bytes 16515072 | tf_op jit(solution)/shard_map/all_gather | solution.py:504
  11.8 0.7 copy-start.2
  128.8 32.9 %copy-start.4 = (f32[8,1,128,128]{3,2,1,0:T(8,128)S(1)}, f32[8,1,128,128]{3,2,1,0:T(8,128)}, u32[]{:S(2)}) copy-start(f32[8,1,128,128]{3,2,1,0:T(8,128)} %param.14) | copy-start | bytes 1572868
  246.7 21.2 %copy-start.7 = (s32[128,128]{1,0:T(8,128)S(1)}, s32[128,128]{1,0:T(8,128)}, u32[]{:S(2)}) copy-start(s32[128,128]{1,0:T(8,128)} %pattern.1) | copy-start | bytes 196612
  246.7 31.0 %copy-start.8 = (s32[128]{0:T(128)S(1)}, s32[128]{0:T(128)}, u32[]{:S(2)}) copy-start(s32[128]{0:T(128)} %param.16) | copy-start | bytes 1540
  246.7 31.0 %copy-start.9 = (s32[128]{0:T(128)S(1)}, s32[128]{0:T(128)}, u32[]{:S(2)}) copy-start(s32[128]{0:T(128)} %param.17) | copy-start | bytes 1540
  253.5 23.3 %all-to-all-start.12 = ((f32[8,2,8,8,128]{4,3,2,1,0:T(8,128)}), f32[8,2,8,8,128]{4,3,2,1,0:T(8,128)S(1)}, u32[]{:S(2)}, u32[]{:S(2)}) async-start(f32[8,2,8,8,128]{4,3,2,1,0:T(8,128)} %shard_map.109), calls=%async_computation.12 | async-start | bytes 1048576 | tf_op jit(solution)/shard_map/all_to_all | solution.py:522
Sparse Core Ops, SparseCore 0:
  11.8 41.4 all-gather.2
  55.1 84.6 all-gather.4

commit v5 on v4

--- a/solution.py
+++ b/solution.py
@@ -19,7 +19,7 @@
 LIST = 64
 GROUP = 4
 HBM = pl.BlockSpec(memory_space=pl.ANY)
-ROOM = 52 * 1024 * 1024
+ROOM = 44 * 1024 * 1024
 SMEM = pl.BlockSpec(memory_space=pltpu.SMEM)
 VMEM = pl.BlockSpec(memory_space=pltpu.VMEM)
 WIDTH = 0
@@ -147,7 +147,11 @@
         listed = jnp.max(jnp.sum(rows, axis=1, keepdims=True), axis=0, keepdims=True)
         return flag((most > cap) | (listed > LIST))
 
-    full = jnp.maximum(over(near, CAP_L), over(high, CAP_U))
+    def over_far():
+        rows = dot(dot(by_row, far), same)
+        return flag(jnp.max(jnp.max(rows, axis=1, keepdims=True), axis=0, keepdims=True) > LIST)
+
+    full = jnp.maximum(jnp.maximum(over(near, CAP_L), over(high, CAP_U)), over_far())
 
     lane = iota((RB, NB), 1)
     sub = iota((RB, NB), 0)
@@ -224,7 +228,7 @@
     below_l, list_l, pack_l, count_l = panel(near_p, CAP_L, row_lev + 0.0 * node)
     below_u, list_u, pack_u, count_u = panel(high_p, CAP_U, down)
     list_t = listing(far_p * own, ranks(far_p), spot, NB)
-    count_t = count(far_p * own)
+    count_t = jnp.minimum(count(far_p * own), LIST)
     rows = flag(lane == WIDTH) * row_wid
     counts = jnp.zeros((1, NB), jnp.float32)
     for k, value in enumerate([count_l, count_u, count_t, full]):
@@ -254,7 +258,10 @@
     )(pattern, levels.reshape(1, NB), widths.reshape(1, NB))
 
 
-def pack_kernel(where, cap, table, blocks, _, out, token, held, sems_in, sems_out):
+def pack_kernel(where, cap, with_far, table, blocks, _, *rest):
+    rest = list(rest)
+    lower = rest.pop(0) if with_far else None
+    out, extra, held, sems_in, sems_out = rest[:5]
     count = table[COUNTS, where]
     row = PACK_L + where
 
@@ -265,8 +272,15 @@
     def store(t):
         return pltpu.make_async_copy(held.at[t], out.at[t], sems_out.at[t])
 
+    def load_far(t):
+        n = table[LIST_T, t]
+        return pltpu.make_async_copy(lower.at[n >> 4, n & (CB - 1)], extra.at[t], rest[5].at[t])
+
     pl.loop(0, count)(lambda t: load(t).start())
-    token[...] = jnp.zeros_like(token)
+    if with_far:
+        pl.loop(0, table[COUNTS, 2])(lambda t: load_far(t).start())
+    else:
+        extra[...] = jnp.zeros_like(extra)
 
     @pl.loop(0, count)
     def _(t):
@@ -274,53 +288,55 @@
         store(t).start()
 
     pl.loop(0, count)(lambda t: store(t).wait())
-
-
-def pack(where, cap, table, blocks, after):
+    if with_far:
+        pl.loop(0, table[COUNTS, 2])(lambda t: load_far(t).wait())
+
+
+def pack(where, cap, table, blocks, after, lower=None):
+    with_far = lower is not None
+    extra = (LIST, W, W) if with_far else (HS, W)
+    scratch = [
+        pltpu.VMEM((cap, W, W), jnp.float32),
+        pltpu.SemaphoreType.DMA((cap,)),
+        pltpu.SemaphoreType.DMA((cap,)),
+    ]
+    if with_far:
+        scratch.append(pltpu.SemaphoreType.DMA((LIST,)))
     return pl.pallas_call(
-        lambda *refs: pack_kernel(where, cap, *refs),
+        lambda *refs: pack_kernel(where, cap, with_far, *refs),
         out_shape=(
             jax.ShapeDtypeStruct((cap, W, W), jnp.float32),
-            jax.ShapeDtypeStruct((HS, W), jnp.float32),
+            jax.ShapeDtypeStruct(extra, jnp.float32),
         ),
-        in_specs=[SMEM, HBM, HBM],
+        in_specs=[SMEM, HBM, HBM] + ([HBM] if with_far else []),
         out_specs=(HBM, VMEM),
-        scratch_shapes=[
-            pltpu.VMEM((cap, W, W), jnp.float32),
-            pltpu.SemaphoreType.DMA((cap,)),
-            pltpu.SemaphoreType.DMA((cap,)),
-        ],
+        scratch_shapes=scratch,
+        compiler_params=pltpu.CompilerParams(vmem_limit_bytes=ROOM),
         cost_estimate=cost(4),
-    )(table, blocks, after)
-
-
-def level_kernel(level, copies, kind, turn, both, sliced, group, table, known, right, inverse, panel, less, *rest):
-    if turn:
-        inverse_2, out, out_2, sums, blocks, inv, inv_2, sems, isems = rest
-    else:
-        out, sums, blocks, inv, sems, isems = rest
+    )(table, blocks, after, *([lower] if with_far else []))
+
+
+def level_kernel(level, copies, kind, turn, both, sliced, group, fetch, table, known, right, inverse, panel, less, *rest):
+    rest = list(rest)
+    inverse_2 = rest.pop(0) if turn else None
+    out = rest.pop(0)
+    out_2 = rest.pop(0) if turn else None
+    blocks = rest.pop(0) if fetch else panel
+    sums = rest.pop(0)
+    sems = rest.pop(0) if fetch else None
     p = lax.axis_index("prow")
     row = LIST_U if kind else LIST_L
     e0, e1 = table[STARTS, kind * HALF + level], table[STARTS, kind * HALF + level + 1]
     r0, r1 = table[ROWS, HALF + level], table[ROWS, HALF + level + 1]
+    whole = table[STARTS, kind * HALF + LEVELS]
 
     def copy(t):
         return pltpu.make_async_copy(panel.at[table[row, t] >> 10], blocks.at[t], sems.at[t])
 
-    def icopy(a):
-        return pltpu.make_async_copy(inverse.at[a], inv.at[a], isems.at[a])
-
-    def icopy_2(a):
-        return pltpu.make_async_copy(inverse_2.at[a], inv_2.at[a], isems.at[RB + a])
-
-    if panel is not None:
+    if fetch:
         pl.loop(e0, e1)(lambda t: copy(t).start())
-
-    @pl.loop(r0, r1)
-    def _(r):
-        icopy(table[ROWS, r]).start()
-        if turn:
-            icopy_2(table[ROWS, r]).start()
+        pl.loop(0, e0)(lambda t: copy(t).start())
+        pl.loop(e1, whole)(lambda t: copy(t).start())
 
     shift = lax.axis_index("pcol") * HS
     for a in range(RB):
@@ -349,9 +365,10 @@
                 t = e0 + g * group + u
                 there = t < e1
 
-                @pl.when(there)
-                def _():
-                    copy(t).wait()
+                if fetch:
+                    @pl.when(there)
+                    def _():
+                        copy(t).wait()
 
                 t = jnp.minimum(t, e1 - 1)
                 node = (table[row, t] >> 3) & (NB - 1)
@@ -370,15 +387,9 @@
             there = r < r1
             a = table[ROWS, jnp.minimum(r, r1 - 1)]
 
-            @pl.when(there)
-            def _():
-                icopy(a).wait()
-                if turn:
-                    icopy_2(a).wait()
-
-            fresh.append((there, a, jnp.where(lane < table[a, WIDTH], dot3(sums[a], inv[a]), 0.0)))
+            fresh.append((there, a, jnp.where(lane < table[a, WIDTH], dot3(sums[a], inverse[a]), 0.0)))
         if turn:
-            later = [jnp.where(lane < table[a, WIDTH], dot3(x, inv_2[a]), 0.0) for _, a, x in fresh]
+            later = [jnp.where(lane < table[a, WIDTH], dot3(x, inverse_2[a]), 0.0) for _, a, x in fresh]
             for there, a, x in fresh:
                 out_2[a] = x
             fresh = [(there, a, x) for (there, a, _), x in zip(fresh, later)]
@@ -391,53 +402,47 @@
                     else:
                         out[r, a] = x
 
-
-def level_step(level, copies, kind, table, known, right, inverse, panel, turn=None, both=False, sliced=False, after=None, less=None, group=GROUP):
+    if fetch:
+        pl.loop(0, e0)(lambda t: copy(t).wait())
+        pl.loop(e1, whole)(lambda t: copy(t).wait())
+
+
+def level_step(
+    level, copies, kind, table, known, right, inverse, panel, *,
+    turn=None, both=False, sliced=False, after=None, less=None, group=GROUP, fetch=False,
+):
     ins, specs = [table], [SMEM]
-    for x, spec in ((known, VMEM), (right, VMEM), (inverse, HBM)):
+    given = ((known, VMEM), (right, VMEM), (inverse, VMEM), (panel, HBM if fetch else VMEM), (less, VMEM))
+    for x, spec in given + ((turn, VMEM), (after, HBM)):
         if x is not None:
             ins.append(x)
             specs.append(spec)
-    if panel is not None:
-        ins.append(panel)
-        specs.append(HBM)
-    if less is not None:
-        ins.append(less)
-        specs.append(VMEM)
-    if turn is not None:
-        ins.append(turn)
-        specs.append(HBM)
-    if after is not None:
-        ins.append(after)
-        specs.append(HBM)
 
     def kernel(*refs):
         refs = list(refs)
         if after is not None:
             refs.pop(len(ins) - 1)
-        given = [refs.pop(0)]
-        given.append(refs.pop(0) if known is not None else None)
-        given += [refs.pop(0), refs.pop(0)]
-        given.append(refs.pop(0) if panel is not None else None)
-        given.append(refs.pop(0) if less is not None else None)
-        level_kernel(level, copies, kind, turn is not None, both, sliced, group, *given, *refs)
-
-    shape = (copies, 2, RB, HS, W) if both else (copies, RB, HS, W)
-    out_shape = [jax.ShapeDtypeStruct(shape, jnp.float32)]
-    carry = kind == 1 and not both
-    sums = [] if carry else [pltpu.VMEM((RB, HS, W), jnp.float32)]
-    if carry:
-        out_shape.append(jax.ShapeDtypeStruct((RB, HS, W), jnp.float32))
-    scratch = sums + [pltpu.VMEM((LIST, W, W), jnp.float32), pltpu.VMEM((RB, W, W), jnp.float32)]
+        args = [refs.pop(0)] + [refs.pop(0) if x is not None else None for x, _ in given]
+        level_kernel(level, copies, kind, turn is not None, both, sliced, group, fetch, *args, *refs)
+
+    small = (RB, HS, W)
+    shapes = [(copies, 2) + small if both else (copies,) + small]
     if turn is not None:
-        out_shape.append(jax.ShapeDtypeStruct((RB, HS, W), jnp.float32))
-        scratch.append(pltpu.VMEM((RB, W, W), jnp.float32))
-    scratch += [pltpu.SemaphoreType.DMA((LIST,)), pltpu.SemaphoreType.DMA((2 * RB,))]
+        shapes.append(small)
+    if fetch:
+        shapes.append((LIST, W, W))
+    scratch = []
+    if kind == 1 and not both:
+        shapes.append(small)
+    else:
+        scratch.append(pltpu.VMEM(small, jnp.float32))
+    if fetch:
+        scratch.append(pltpu.SemaphoreType.DMA((LIST,)))
     out = pl.pallas_call(
         kernel,
-        out_shape=out_shape,
+        out_shape=[jax.ShapeDtypeStruct(x, jnp.float32) for x in shapes],
         in_specs=specs,
-        out_specs=[VMEM] * len(out_shape),
+        out_specs=[VMEM] * len(shapes),
         scratch_shapes=scratch,
         compiler_params=pltpu.CompilerParams(vmem_limit_bytes=ROOM),
         cost_estimate=cost(8),
@@ -445,14 +450,8 @@
     return out if len(out) > 1 else out[0]
 
 
-def across_kernel(table, known, lower, out, blocks, sems):
+def across_kernel(table, known, blocks, out):
     count = table[COUNTS, 2]
-
-    def copy(t):
-        n = table[LIST_T, t]
-        return pltpu.make_async_copy(lower.at[n >> 4, n & (CB - 1)], blocks.at[t], sems.at[t])
-
-    pl.loop(0, count)(lambda t: copy(t).start())
     out[...] = jnp.zeros_like(out)
 
     @pl.loop(0, (count + GROUP - 1) >> 2)
@@ -461,11 +460,6 @@
         for u in range(GROUP):
             t = g * GROUP + u
             there = t < count
-
-            @pl.when(there)
-            def _():
-                copy(t).wait()
-
             t = jnp.minimum(t, count - 1)
             n = table[LIST_T, t]
             c = n & (CB - 1)
@@ -475,16 +469,15 @@
             out[:, a] += term
 
 
-def across(table, known, lower):
+def across(table, known, blocks):
     return pl.pallas_call(
         across_kernel,
         out_shape=jax.ShapeDtypeStruct((PC, RB, HS, W), jnp.float32),
-        in_specs=[SMEM, VMEM, HBM],
+        in_specs=[SMEM, VMEM, VMEM],
         out_specs=VMEM,
-        scratch_shapes=[pltpu.VMEM((NB, W, W), jnp.float32), pltpu.SemaphoreType.DMA((NB,))],
         compiler_params=pltpu.CompilerParams(vmem_limit_bytes=ROOM),
         cost_estimate=cost(8),
-    )(table, known, lower)
+    )(table, known, blocks)
 
 
 def local(rhs, lower, upper, lower_inverse, upper_inverse, pattern, levels, widths):
@@ -500,25 +493,27 @@
     panel_l = lax.all_gather(packed_l, "pcol", tiled=True)
     leaves = level_step(0, PR, 0, table, None, right, lower_inv, None, sliced=True, after=token)
     known = swap(leaves)
-    packed_u, _ = pack(1, CAP_U, table, upper_blocks, known[0, 0])
+    packed_u, far_blocks = pack(1, CAP_U, table, upper_blocks, known[0, 0], lower_blocks)
     panel_u = lax.all_gather(packed_u, "pcol", tiled=True)
-    known = swap(level_step(1, PR, 0, table, known, right, lower_inv, panel_l, sliced=True, group=8))
-    known = swap(level_step(2, PR, 0, table, known, right, lower_inv, panel_l, sliced=True, group=8))
+    state, held = level_step(1, PR, 0, table, known, right, lower_inv, panel_l, sliced=True, group=8, fetch=True)
+    known = swap(state)
+    known = swap(level_step(2, PR, 0, table, known, right, lower_inv, held, sliced=True, group=8))
     split = known.reshape(2, PC, RB, HS, W).transpose(1, 0, 2, 3, 4)
     columns = lax.all_to_all(split, "pcol", 0, 0)
-    sums = lax.all_to_all(across(table, columns, lower_blocks), "pcol", 0, 0)
-    step = lambda level, copies, *turn: level_step(
-        level, copies, 0, table, known, right, lower_inv, panel_l, *turn, sliced=True, less=sums
+    sums = lax.all_to_all(across(table, columns, far_blocks), "pcol", 0, 0)
+    step = lambda level, turn=None: level_step(
+        level, PR, 0, table, known, right, lower_inv, held, turn=turn, sliced=True, less=sums
     )
     for level in range(3, LEVELS - 1):
-        known = swap(step(level, PR))
-    state, forward = step(LEVELS - 1, PR, upper_inv)
+        known = swap(step(level))
+    state, forward = step(LEVELS - 1, upper_inv)
     known = swap(state)
-    left = forward
-    for level in range(LEVELS - 2, 0, -1):
-        state, left = level_step(level, PR, 1, table, known, left, upper_inv, panel_u, group=8)
+    state, held, left = level_step(4, PR, 1, table, known, forward, upper_inv, panel_u, group=8, fetch=True)
+    for level in range(3, 0, -1):
         known = swap(state)
-    state = level_step(0, PC, 1, table, known, left, upper_inv, panel_u, both=True, less=forward, group=8)
+        state, left = level_step(level, PR, 1, table, known, left, upper_inv, held, group=8)
+    known = swap(state)
+    state = level_step(0, PC, 1, table, known, left, upper_inv, held, both=True, less=forward, group=8)
     full = lax.all_to_all(state, "pcol", 0, 0)
     shape = rhs.shape
     whole = lambda x: x.transpose(1, 0, 2, 3).reshape(shape)

time: 286 us -> 255 us (0.89)
  Pallas kernels: 51.4 us -> 27.9 us
  blocking collectives: 181 us -> 170 us
    pallas_call x13, Pallas kernels: 46.9 us -> 24.6 us  [the longest x11 18.9 us: level_step(): pl.pallas_call(kernel, out_shape=[jax.ShapeDtypeStruct(x, jnp.float32) fo...]
    all_to_all x10, blocking collectives: 147 us -> 137 us  [local(): swap = lambda x: lax.all_to_all(x, 'prow', 0, 0)]
  transfers between devices with their start and end apart: 3 -> 3, of which waited for: 2 -> 2; matrix products, arithmetic and copies ran while one was open for 0% -> 0% of each run, Pallas kernels for 8% -> 5%
where the time goes in v5:
time: 255 us
  blocking collectives  170 us (67%)
  Pallas kernels  27.9 us (11%)
  waiting for transfers between devices  23.8 us (9%)
  between operations  14.3 us (6%)
  starting transfers between devices  13.6 us (5%)
  local copies, waits for them, and re-layouts  4.3 us (2%)
    all_to_all x10, blocking collectives, local(): swap = lambda x: lax.all_to_all(x, 'prow', 0, 0)  137 us
    all_to_all x1, blocking collectives, local(): columns = lax.all_to_all(split, 'pcol', 0, 0)  20.2 us
    pallas_call x11, Pallas kernels, level_step(): pl.pallas_call(kernel, out_shape=[jax.ShapeDtypeStruct(x, jnp.float32) fo...  18.9 us
    all_gather x1, waiting for transfers between devices, local(): panel_l = lax.all_gather(packed_l, 'pcol', tiled=True)  15 us
    all_to_all x1, starting transfers between devices, local(): full = lax.all_to_all(state, 'pcol', 0, 0)  13.5 us
    all_to_all x1, blocking collectives, local(): sums = lax.all_to_all(across(table, columns, far_blocks), 'pcol', 0, 0)  13.2 us
    all_to_all x1, waiting for transfers between devices, local(): full = lax.all_to_all(state, 'pcol', 0, 0)  8.79 us
    pallas_call x2, Pallas kernels, pack(): pl.pallas_call(lambda *refs: pack_kernel(where, cap, with_far, *refs), ou...  5.71 us
  transfers between devices with their start and end apart: 3, of which 2 were waited for; matrix products, arithmetic and copies ran while one was open for 0% of the time, Pallas kernels for 5%

profile of v5, /device:TPU:1, one launch (start us, length us, event | category | flops | bytes accessed | tf_op | source)
XLA Modules:
  0.0 255.2 jit_solution(15040655981785499688)
XLA Ops:
  7.2 0.0 all-gather.3.cloned.1.call-start
  7.2 2.7 %shard_map.95.refs_0_.refs_2_.table = s32[16,128]{1,0:T(8,128)} custom-call(s32[128,128]{1,0:T(8,128)} %pattern.1, s32[1,128]{1,0:T(1,128)} %bitcast.313, s32[1,128]{1,0:T(1,128)} %bitcast.314), custom_call_target="tpu_custom_call" | custom-call | bytes 4194304 | tf_op jit(solution)/shard_map/pallas_call | solution.py:252
  9.9 0.0 copy-start.2
  9.9 0.7 copy-done.2
  10.6 0.0 copy-start.3
  10.6 0.0 copy-start.4
  10.6 0.0 copy-start.6
  10.6 2.4 shard_map.96
  13.0 0.0 all-gather.3.cloned.1.call-update
  13.0 0.0 all-gather.5.cloned.1.call-start
  13.0 0.0 copy-done.3
  13.0 0.0 copy-done.4
  13.1 0.0 copy-done.6
  13.1 0.9 shard_map.97
  14.0 18.9 %all_to_all.65.refs_1_ = f32[16,8,8,128]{3,2,1,0:T(8,128)S(1)} all-to-all(f32[16,8,8,128]{3,2,1,0:T(8,128)S(1)} %shard_map.97), channel_id=1, replica_groups=mesh['prow'=16,'pcol'=8] {'prow'}, dimensions={0} | all-to-all | bytes 1048576 | tf_op jit(solution)/shard_map/all_to_all | solution.py:490
  32.9 3.3 %shard_map.100 = (f32[28,128,128]{2,1,0:T(8,128)}, f32[64,128,128]{2,1,0:T(8,128)S(1)}) custom-call(s32[16,128]{1,0:T(8,128)S(1)} %copy-done.3, f32[8,16,128,128]{3,2,1,0:T(8,128)} %bitcast.276, f32[8,128]{1,0:T(8,128)S(1)} %slice_bitcast_fusion.2.refs_2_, f32[8,16,128,128]{3,2,1,0:T(8,128)} %bitcast.274), custom_call_target="tpu_custom_call" | custom-call | bytes 4194304 | tf_op jit(solution)/shard_map/pallas_call | solution.py:305
  36.2 0.0 copy-start
  36.2 1.9 copy-done
  38.2 0.0 all-gather.5.cloned.1.call-update
  38.2 15.0 %all-gather.3.cloned.1.call-done.refs_4_ = f32[80,128,128]{2,1,0:T(8,128)} async-done(((f32[10,128,128]{2,1,0:T(8,128)}), f32[80,128,128]{2,1,0:T(8,128)}) %all-gather.3.cloned.1.call-update) | async-done | bytes 5242896 | tf_op jit(solution)/shard_map/all_gather | solution.py:493
  53.2 0.0 copy-start.1
  53.2 3.9 %shard_map.98 = (f32[16,8,8,128]{3,2,1,0:T(8,128)S(1)}, f32[64,128,128]{2,1,0:T(8,128)S(1)}) custom-call(s32[16,128]{1,0:T(8,128)S(1)} %copy-done.3, f32[16,8,8,128]{3,2,1,0:T(8,128)S(1)} %all_to_all.65.refs_1_, f32[8,64,128]{2,1,0:T(8,128)S(1)} %bitcast.293, f32[8,128,128]{2,1,0:T(8,128)S(1)} %bitcast.279, f32[80,128,128]{2,1,0:T(8,128)} %all-gather.3.cloned.1.call-done.refs_4_), custom_call_target="tpu_custom_call" | custom-call | bytes 8388608 | tf_op jit(solution)/shard_map/pallas_call | solution.py:441
  57.1 18.9 %all_to_all.66.refs_1_ = f32[16,8,8,128]{3,2,1,0:T(8,128)S(1)} all-to-all(f32[16,8,8,128]{3,2,1,0:T(8,128)S(1)} %get-tuple-element.76), channel_id=1, replica_groups=mesh['prow'=16,'pcol'=8] {'prow'}, dimensions={0} | all-to-all | bytes 1048576 | tf_op jit(solution)/shard_map/all_to_all | solution.py:490
  76.0 1.2 shard_map.99
  77.2 13.6 %all_to_all.67.refs_1_ = f32[16,8,8,128]{3,2,1,0:T(8,128)S(1)} all-to-all(f32[16,8,8,128]{3,2,1,0:T(8,128)S(1)} %shard_map.99), channel_id=1, replica_groups=mesh['prow'=16,'pcol'=8] {'prow'}, dimensions={0} | all-to-all | bytes 1048576 | tf_op jit(solution)/shard_map/all_to_all | solution.py:490
  90.8 20.2 %all_to_all.68.known = f32[8,2,8,8,128]{4,3,2,1,0:T(8,128)S(1)} all-to-all(f32[8,2,8,8,128]{4,3,2,1,0:T(8,128)S(1)} %bitcast.311), channel_id=1, replica_groups=mesh['prow'=16,'pcol'=8] {'pcol'}, dimensions={0} | all-to-all | bytes 1048576 | tf_op jit(solution)/shard_map/all_to_all | solution.py:502
  111.0 0.0 copy-done.1
  111.0 0.7 shard_map.101
  111.7 0.0 copy-start.5
  111.7 13.2 %all_to_all.69.refs_5_ = f32[8,8,8,128]{3,2,1,0:T(8,128)S(1)} all-to-all(f32[8,8,8,128]{3,2,1,0:T(8,128)S(1)} %shard_map.101), channel_id=1, replica_groups=mesh['prow'=16,'pcol'=8] {'pcol'}, dimensions={0} | all-to-all | bytes 524288 | tf_op jit(solution)/shard_map/all_to_all | solution.py:503
  124.9 0.7 shard_map.102
  125.7 13.9 %all_to_all.70.refs_1_ = f32[16,8,8,128]{3,2,1,0:T(8,128)S(1)} all-to-all(f32[16,8,8,128]{3,2,1,0:T(8,128)S(1)} %shard_map.102), channel_id=1, replica_groups=mesh['prow'=16,'pcol'=8] {'prow'}, dimensions={0} | all-to-all | bytes 1048576 | tf_op jit(solution)/shard_map/all_to_all | solution.py:490
  139.6 0.7 shard_map.103
  140.3 12.8 %all_to_all.71.refs_1_ = f32[16,8,8,128]{3,2,1,0:T(8,128)S(1)} all-to-all(f32[16,8,8,128]{3,2,1,0:T(8,128)S(1)} %shard_map.103), channel_id=1, replica_groups=mesh['prow'=16,'pcol'=8] {'prow'}, dimensions={0} | all-to-all | bytes 1048576 | tf_op jit(solution)/shard_map/all_to_all | solution.py:490
  153.1 0.0 copy-done.5
  153.1 0.7 shard_map.104
  153.9 12.1 %all_to_all.72.refs_1_ = f32[16,8,8,128]{3,2,1,0:T(8,128)S(1)} all-to-all(f32[16,8,8,128]{3,2,1,0:T(8,128)S(1)} %get-tuple-element.79), channel_id=1, replica_groups=mesh['prow'=16,'pcol'=8] {'prow'}, dimensions={0} | all-to-all | bytes 1048576 | tf_op jit(solution)/shard_map/all_to_all | solution.py:490
  166.0 0.0 all-gather.5.cloned.1.call-done.refs_4_
  166.0 4.8 %shard_map.105 = (f32[16,8,8,128]{3,2,1,0:T(8,128)S(1)}, f32[64,128,128]{2,1,0:T(8,128)S(1)}, f32[8,8,128]{2,1,0:T(8,128)S(1)}) custom-call(s32[16,128]{1,0:T(8,128)S(1)} %copy-done.3, f32[16,8,8,128]{3,2,1,0:T(8,128)S(1)} %all_to_all.72.refs_1_, f32[8,8,128]{2,1,0:T(8,128)S(1)} %get-tuple-element.80.refs_2_.refs_5_, f32[8,128,128]{2,1,0:T(8,128)S(1)} %bitcast.286, ...), custom_call_target="tpu_custom_call" | custom-call | bytes 8388608 | tf_op jit(solution)/shard_map/pallas_call | solution.py:441
  170.8 11.6 %all_to_all.73.refs_1_ = f32[16,8,8,128]{3,2,1,0:T(8,128)S(1)} all-to-all(f32[16,8,8,128]{3,2,1,0:T(8,128)S(1)} %get-tuple-element.82), channel_id=1, replica_groups=mesh['prow'=16,'pcol'=8] {'prow'}, dimensions={0} | all-to-all | bytes 1048576 | tf_op jit(solution)/shard_map/all_to_all | solution.py:490
  182.4 1.2 shard_map.106
  183.7 11.6 %all_to_all.74.refs_1_ = f32[16,8,8,128]{3,2,1,0:T(8,128)S(1)} all-to-all(f32[16,8,8,128]{3,2,1,0:T(8,128)S(1)} %get-tuple-element.85), channel_id=1, replica_groups=mesh['prow'=16,'pcol'=8] {'prow'}, dimensions={0} | all-to-all | bytes 1048576 | tf_op jit(solution)/shard_map/all_to_all | solution.py:490
  195.3 1.2 shard_map.107
  196.5 0.0 copy-start.8
  196.5 0.0 copy-start.9
  196.5 0.0 copy-start.10
  196.5 11.8 %all_to_all.75.refs_1_ = f32[16,8,8,128]{3,2,1,0:T(8,128)S(1)} all-to-all(f32[16,8,8,128]{3,2,1,0:T(8,128)S(1)} %get-tuple-element.87), channel_id=1, replica_groups=mesh['prow'=16,'pcol'=8] {'prow'}, dimensions={0} | all-to-all | bytes 1048576 | tf_op jit(solution)/shard_map/all_to_all | solution.py:490
  208.3 1.5 shard_map.108
  209.8 11.9 %all_to_all.76.refs_1_ = f32[16,8,8,128]{3,2,1,0:T(8,128)S(1)} all-to-all(f32[16,8,8,128]{3,2,1,0:T(8,128)S(1)} %get-tuple-element.89), channel_id=1, replica_groups=mesh['prow'=16,'pcol'=8] {'prow'}, dimensions={0} | all-to-all | bytes 1048576 | tf_op jit(solution)/shard_map/all_to_all | solution.py:490
  221.6 2.0 shard_map.109
  223.6 13.5 %all-to-all-start.12 = ((f32[8,2,8,8,128]{4,3,2,1,0:T(8,128)}), f32[8,2,8,8,128]{4,3,2,1,0:T(8,128)S(1)}, u32[]{:S(2)}, u32[]{:S(2)}) async-start(f32[8,2,8,8,128]{4,3,2,1,0:T(8,128)} %shard_map.109), calls=%async_computation.12 | async-start | bytes 1048576 | tf_op jit(solution)/shard_map/all_to_all | solution.py:517
  237.1 0.6 slice.19
  237.7 0.0 copy-done.8
  237.7 0.1 copy.74
  237.8 8.8 %all-to-all-done.12 = f32[8,2,8,8,128]{4,3,2,1,0:T(8,128)S(1)} async-done(((f32[8,2,8,8,128]{4,3,2,1,0:T(8,128)}), f32[8,2,8,8,128]{4,3,2,1,0:T(8,128)S(1)}, u32[]{:S(2)}, u32[]{:S(2)}) %all-to-all-start.12) | async-done | bytes 524320 | tf_op jit(solution)/shard_map/all_to_all | solution.py:517
  246.6 0.8 copy_bitcast_fusion.1
  247.5 0.0 copy-done.9
  247.5 0.0 copy-done.10
  247.5 0.9 while.11
  (3 shorter events, 0.1 us)
Async XLA Ops:
  7.2 46.0 %all-gather.3.cloned.1.call-start = ((), (), s32[]{:S(2)}) async-start(), calls=%async_computation.34 | async-start | bytes 5898240 | tf_op jit(solution)/shard_map/all_gather | solution.py:493
  9.9 0.7 copy-start.2
  10.6 2.5 copy-start.3
  10.6 2.5 copy-start.4
  10.6 2.5 copy-start.6
  13.0 153.0 %all-gather.5.cloned.1.call-start = ((), (), s32[]{:S(2)}) async-start(), calls=%async_computation.35 | async-start | bytes 16515072 | tf_op jit(solution)/shard_map/all_gather | solution.py:497
  36.2 2.0 copy-start
  53.2 57.9 %copy-start.1 = (f32[64,128,128]{2,1,0:T(8,128)S(1)}, f32[64,128,128]{2,1,0:T(8,128)}, u32[]{:S(2)}) copy-start(f32[64,128,128]{2,1,0:T(8,128)} %copy-done) | copy-start | bytes 12582916
  111.7 41.4 %copy-start.5 = (f32[8,1,128,128]{3,2,1,0:T(8,128)S(1)}, f32[8,1,128,128]{3,2,1,0:T(8,128)}, u32[]{:S(2)}) copy-start(f32[8,1,128,128]{3,2,1,0:T(8,128)} %param.14) | copy-start | bytes 1572868
  196.5 41.2 %copy-start.8 = (s32[128,128]{1,0:T(8,128)S(1)}, s32[128,128]{1,0:T(8,128)}, u32[]{:S(2)}) copy-start(s32[128,128]{1,0:T(8,128)} %pattern.1) | copy-start | bytes 196612
  196.5 51.0 %copy-start.9 = (s32[128]{0:T(128)S(1)}, s32[128]{0:T(128)}, u32[]{:S(2)}) copy-start(s32[128]{0:T(128)} %param.16) | copy-start | bytes 1540
  196.5 51.0 %copy-start.10 = (s32[128]{0:T(128)S(1)}, s32[128]{0:T(128)}, u32[]{:S(2)}) copy-start(s32[128]{0:T(128)} %param.17) | copy-start | bytes 1540
  223.6 23.0 %all-to-all-start.12 = ((f32[8,2,8,8,128]{4,3,2,1,0:T(8,128)}), f32[8,2,8,8,128]{4,3,2,1,0:T(8,128)S(1)}, u32[]{:S(2)}, u32[]{:S(2)}) async-start(f32[8,2,8,8,128]{4,3,2,1,0:T(8,128)} %shard_map.109), calls=%async_computation.12 | async-start | bytes 1048576 | tf_op jit(solution)/shard_map/all_to_all | solution.py:517
Sparse Core Ops, SparseCore 0:
  13.1 40.0 all-gather.2
  55.0 84.6 all-gather.4

commit v6 on v5

--- a/solution.py
+++ b/solution.py
@@ -18,6 +18,7 @@
 CAP_U = 28
 LIST = 64
 GROUP = 4
+ORDER = [[PC * (k & 1) + (k >> 1) for k in range(PR)]]
 HBM = pl.BlockSpec(memory_space=pl.ANY)
 ROOM = 44 * 1024 * 1024
 SMEM = pl.BlockSpec(memory_space=pltpu.SMEM)
@@ -119,7 +120,39 @@
     return jnp.where(cond, 1.0, 0.0)
 
 
-def table_kernel(pattern, levels, widths, out):
+def dot(x, y):
+    return jnp.dot(x, y, preferred_element_type=jnp.float32)
+
+
+def ranks(sel):
+    i, j = iota((NB, NB), 0), iota((NB, NB), 1)
+    same = flag((i & (PC - 1)) == (j & (PC - 1)))
+    total = jnp.zeros((1, NB), jnp.float32)
+    rows = []
+    for a in range(RB):
+        rows.append(total)
+        total = total + sel[a : a + 1]
+    return dot(jnp.concatenate(rows, axis=0), same) + dot(sel, same * flag(i < j))
+
+
+def listing(sel, place, value, size):
+    t = iota((size, NB), 0).astype(jnp.float32)
+    held = jnp.zeros((size, NB), jnp.float32)
+    for a in range(RB):
+        hit = flag(t == place[a : a + 1]) * sel[a : a + 1]
+        held = held + hit * value[a : a + 1]
+    ones = jnp.ones((RB, NB), jnp.float32)
+    row = lax.dot_general(ones, held, (((1,), (1,)), ((), ())), preferred_element_type=jnp.float32)[:1]
+    if size < NB:
+        row = jnp.concatenate([row, jnp.zeros((1, NB - size), jnp.float32)], axis=1)
+    return row
+
+
+def count(sel):
+    return jnp.sum(jnp.sum(sel, axis=1, keepdims=True), axis=0, keepdims=True)
+
+
+def table_kernel(pattern, levels, widths, _, out):
     p = lax.axis_index("prow")
     q = lax.axis_index("pcol")
     lev = levels[...].astype(jnp.float32)
@@ -134,10 +167,6 @@
     far = low - near
     same = flag((i & (PC - 1)) == (j & (PC - 1)))
     ahead = flag(i < j)
-    same_ahead = same * ahead
-
-    def dot(x, y):
-        return jnp.dot(x, y, preferred_element_type=jnp.float32)
 
     by_row = flag((iota((PR, NB), 1) & (PR - 1)) == iota((PR, NB), 0))
 
@@ -163,14 +192,6 @@
     node = lane.astype(jnp.float32)
     spot = (sub * CB + (lane >> 3)).astype(jnp.float32)
 
-    def ranks(sel):
-        total = jnp.zeros((1, NB), jnp.float32)
-        rows = []
-        for a in range(RB):
-            rows.append(total)
-            total = total + sel[a : a + 1]
-        return dot(jnp.concatenate(rows, axis=0), same) + dot(sel, same_ahead)
-
     def ordered():
         start = jnp.zeros((RB, 1), jnp.float32)
         below = jnp.zeros((1, NB), jnp.float32)
@@ -180,21 +201,6 @@
             start = start + flag(first)
             below = below + flag(row_lev[a : a + 1] < node[:1])
         return start, below
-
-    def listing(sel, place, value, size):
-        t = iota((size, NB), 0).astype(jnp.float32)
-        held = jnp.zeros((size, NB), jnp.float32)
-        for a in range(RB):
-            hit = flag(t == place[a : a + 1]) * sel[a : a + 1]
-            held = held + hit * value[a : a + 1]
-        ones = jnp.ones((RB, NB), jnp.float32)
-        row = lax.dot_general(ones, held, (((1,), (1,)), ((), ())), preferred_element_type=jnp.float32)[:1]
-        if size < NB:
-            row = jnp.concatenate([row, jnp.zeros((1, NB - size), jnp.float32)], axis=1)
-        return row
-
-    def count(sel):
-        return jnp.sum(jnp.sum(sel, axis=1, keepdims=True), axis=0, keepdims=True)
 
     def by_step(sel, step):
         parts = jnp.concatenate([sel * flag(step == k) for k in range(LEVELS)], axis=0)
@@ -248,14 +254,73 @@
     out[8:16, :] = lists.astype(jnp.int32)
 
 
-def tables(pattern, levels, widths):
+def tables(pattern, levels, widths, after):
     return pl.pallas_call(
         table_kernel,
         out_shape=jax.ShapeDtypeStruct((16, NB), jnp.int32),
-        in_specs=[VMEM, VMEM, VMEM],
+        in_specs=[VMEM, VMEM, VMEM, VMEM],
         out_specs=VMEM,
         cost_estimate=cost(4),
-    )(pattern, levels.reshape(1, NB), widths.reshape(1, NB))
+    )(pattern, levels.reshape(1, NB), widths.reshape(1, NB), after)
+
+
+def first_kernel(pattern, levels, blocks, out, token, lists, places, held, sem, sems_in, sems_out):
+    p = lax.axis_index("prow")
+    q = lax.axis_index("pcol")
+    lev = levels[...].astype(jnp.float32)
+    i, j = iota((NB, NB), 0), iota((NB, NB), 1)
+    lev_col = jnp.sum(jnp.where(i == j, lev, 0.0), axis=1, keepdims=True)
+    near = flag(pattern[...] > 0) * flag(lev < lev_col) * flag((lev_col < 2.5) | (lev > 2.5))
+    lane, sub = iota((RB, NB), 1), iota((RB, NB), 0)
+    sel = dot(flag(lane == sub * PR + p), near) * flag((lane & (PC - 1)) == q)
+    spot = (sub * CB + (lane >> 3)).astype(jnp.float32)
+    found = listing(sel, ranks(sel), spot, 32)
+    number = jnp.minimum(count(sel), CAP_L)
+    rows = jnp.where(sub == 0, found, number + 0.0 * spot)
+    lists[...] = rows.astype(jnp.int32)
+    move = pltpu.make_async_copy(lists, places, sem)
+    move.start()
+    token[...] = jnp.zeros_like(token)
+    move.wait()
+    total = places[1, 0]
+
+    def load(t):
+        n = places[0, t]
+        return pltpu.make_async_copy(blocks.at[n >> 4, n & (CB - 1)], held.at[t], sems_in.at[t])
+
+    def store(t):
+        return pltpu.make_async_copy(held.at[t], out.at[t], sems_out.at[t])
+
+    pl.loop(0, total)(lambda t: load(t).start())
+
+    @pl.loop(0, total)
+    def _(t):
+        load(t).wait()
+        store(t).start()
+
+    pl.loop(0, total)(lambda t: store(t).wait())
+
+
+def first(pattern, levels, blocks):
+    return pl.pallas_call(
+        first_kernel,
+        out_shape=(
+            jax.ShapeDtypeStruct((CAP_L, W, W), jnp.float32),
+            jax.ShapeDtypeStruct((1, NB), jnp.int32),
+        ),
+        in_specs=[VMEM, VMEM, HBM],
+        out_specs=(HBM, VMEM),
+        scratch_shapes=[
+            pltpu.VMEM((RB, NB), jnp.int32),
+            pltpu.SMEM((RB, NB), jnp.int32),
+            pltpu.VMEM((CAP_L, W, W), jnp.float32),
+            pltpu.SemaphoreType.DMA,
+            pltpu.SemaphoreType.DMA((CAP_L,)),
+            pltpu.SemaphoreType.DMA((CAP_L,)),
+        ],
+        compiler_params=pltpu.CompilerParams(vmem_limit_bytes=ROOM),
+        cost_estimate=cost(4),
+    )(pattern, levels.reshape(1, NB), blocks)
 
 
 def pack_kernel(where, cap, with_far, table, blocks, _, *rest):
@@ -347,7 +412,7 @@
                 parts = [x + y for x, y in zip(parts[::2], parts[1::2])]
             mine = mine - parts[0]
         sums[a] = mine
-        old = known[p, a] if known is not None else jnp.zeros((HS, W), jnp.float32)
+        old = known[((p & (PC - 1)) << 1) + (p >> 3), a] if known is not None else jnp.zeros((HS, W), jnp.float32)
         for r in range(copies):
             if both:
                 out[r, 0, a] = less[a]
@@ -372,7 +437,7 @@
 
                 t = jnp.minimum(t, e1 - 1)
                 node = (table[row, t] >> 3) & (NB - 1)
-                x = known[node & (PR - 1), node >> 4] * jnp.where(there, 1.0, 0.0)
+                x = known[((node & (PC - 1)) << 1) + ((node >> 3) & 1), node >> 4] * jnp.where(there, 1.0, 0.0)
                 terms.append((table[row, t] & (RB - 1), dot3(x, blocks[t])))
             for a, term in terms:
                 sums[a] -= term
@@ -486,20 +551,19 @@
     upper_blocks = upper.reshape(RB, CB, W, W)
     lower_inv = lower_inverse.reshape(RB, W, W)
     upper_inv = upper_inverse.reshape(RB, W, W)
-    table = tables(pattern, levels, widths)
-    swap = lambda x: lax.all_to_all(x, "prow", 0, 0)
-
-    packed_l, token = pack(0, CAP_L, table, lower_blocks, table)
+    packed_l, token = first(pattern, levels, lower_blocks)
+    table = tables(pattern, levels, widths, token)
+    swap = lambda x: lax.all_to_all(x, "prow", 0, 0, axis_index_groups=ORDER)
+
     panel_l = lax.all_gather(packed_l, "pcol", tiled=True)
-    leaves = level_step(0, PR, 0, table, None, right, lower_inv, None, sliced=True, after=token)
+    leaves = level_step(0, PR, 0, table, None, right, lower_inv, None, sliced=True)
     known = swap(leaves)
     packed_u, far_blocks = pack(1, CAP_U, table, upper_blocks, known[0, 0], lower_blocks)
     panel_u = lax.all_gather(packed_u, "pcol", tiled=True)
     state, held = level_step(1, PR, 0, table, known, right, lower_inv, panel_l, sliced=True, group=8, fetch=True)
     known = swap(state)
     known = swap(level_step(2, PR, 0, table, known, right, lower_inv, held, sliced=True, group=8))
-    split = known.reshape(2, PC, RB, HS, W).transpose(1, 0, 2, 3, 4)
-    columns = lax.all_to_all(split, "pcol", 0, 0)
+    columns = lax.all_to_all(known.reshape(PC, 2, RB, HS, W), "pcol", 0, 0)
     sums = lax.all_to_all(across(table, columns, far_blocks), "pcol", 0, 0)
     step = lambda level, turn=None: level_step(
         level, PR, 0, table, known, right, lower_inv, held, turn=turn, sliced=True, less=sums

time: 255 us -> 257 us (level)
  Pallas kernels: 27.9 us -> 30.9 us
  waiting for transfers between devices: 23.8 us -> 21 us
    pallas_call x0 -> x1, Pallas kernels: none -> 3.48 us  [first(): pl.pallas_call(first_kernel, out_shape=(jax.ShapeDtypeStruct((CAP_L, W, W...]
    all_gather x1, waiting for transfers between devices: 15 us -> 12.2 us  [local(): panel_l = lax.all_gather(packed_l, 'pcol', tiled=True)]
    pallas_call x2 -> x1, Pallas kernels: 5.71 us -> 3.37 us  [pack(): pl.pallas_call(lambda *refs: pack_kernel(where, cap, with_far, *refs), ou...]
  transfers between devices with their start and end apart: 3 -> 3, of which waited for: 2 -> 2; matrix products, arithmetic and copies ran while one was open for 0% -> 0% of each run, Pallas kernels for 5% -> 7%
where the time goes in v6:
time: 257 us
  blocking collectives  171 us (67%)
  Pallas kernels  30.9 us (12%)
  waiting for transfers between devices  21 us (8%)
  between operations  14.3 us (6%)
  starting transfers between devices  13.3 us (5%)
  local copies, waits for them, and re-layouts  5.64 us (2%)
    all_to_all x10, blocking collectives, local(): swap = lambda x: lax.all_to_all(x, 'prow', 0, 0, axis_index_groups=ORDER)  137 us
    all_to_all x1, blocking collectives, local(): columns = lax.all_to_all(known.reshape(PC, 2, RB, HS, W), 'pcol', 0, 0)  20.9 us
    pallas_call x11, Pallas kernels, level_step(): pl.pallas_call(kernel, out_shape=[jax.ShapeDtypeStruct(x, jnp.float32) fo...  18.9 us
    all_to_all x1, starting transfers between devices, local(): full = lax.all_to_all(state, 'pcol', 0, 0)  13.3 us
    all_to_all x1, blocking collectives, local(): sums = lax.all_to_all(across(table, columns, far_blocks), 'pcol', 0, 0)  13 us
    all_gather x1, waiting for transfers between devices, local(): panel_l = lax.all_gather(packed_l, 'pcol', tiled=True)  12.2 us
    all_to_all x1, waiting for transfers between devices, local(): full = lax.all_to_all(state, 'pcol', 0, 0)  8.76 us
  transfers between devices with their start and end apart: 3, of which 2 were waited for; matrix products, arithmetic and copies ran while one was open for 0% of the time, Pallas kernels for 7%

profile of v6, /device:TPU:1, one launch (start us, length us, event | category | flops | bytes accessed | tf_op | source)
XLA Modules:
  0.0 257.1 jit_solution(15797062105276471043)
XLA Ops:
  7.2 0.0 copy-start.11
  7.2 0.0 copy-start.12
  7.2 0.0 all-gather.3.cloned.1.call-start
  7.2 0.0 copy-start.4
  7.2 0.8 copy-done.4
  8.1 0.0 copy-start.7
  8.1 0.0 copy-start.9
  8.1 3.5 %shard_map.95 = (f32[10,128,128]{2,1,0:T(8,128)}, s32[1,128]{1,0:T(1,128)S(1)}) custom-call(s32[128,128]{1,0:T(8,128)S(1)} %copy-done.4, s32[1,128]{1,0:T(1,128)} %bitcast.309, f32[8,16,128,128]{3,2,1,0:T(8,128)} %bitcast.270), custom_call_target="tpu_custom_call" | custom-call | bytes 4194304 | tf_op jit(solution)/shard_map/pallas_call | solution.py:305
  11.6 0.0 copy-start.6
  11.6 0.5 copy-done.6
  12.1 0.0 all-gather.3.cloned.1.call-update
  12.1 0.0 all-gather.5.cloned.1.call-start
  12.2 0.0 copy-done.11
  12.2 0.0 copy-done.12
  12.2 2.6 %shard_map.96.refs_0_.table = s32[16,128]{1,0:T(8,128)} custom-call(s32[128,128]{1,0:T(8,128)} %pattern.3, s32[1,128]{1,0:T(1,128)S(1)} %bitcast.310, s32[1,128]{1,0:T(1,128)S(1)} %bitcast.311, s32[1,128]{1,0:T(1,128)} %copy-done.6), custom_call_target="tpu_custom_call" | custom-call | bytes 4194304 | tf_op jit(solution)/shard_map/pallas_call | solution.py:258
  14.8 0.0 copy-done.7
  14.8 0.0 copy-done.9
  14.8 0.0 copy-start.2
  14.8 0.7 copy-done.2
  15.5 0.9 shard_map.97
  16.4 18.4 %all_to_all.65.refs_1_ = f32[16,8,8,128]{3,2,1,0:T(8,128)S(1)} all-to-all(f32[16,8,8,128]{3,2,1,0:T(8,128)S(1)} %shard_map.97), channel_id=1, replica_groups={{0,64,8,72,16,80,24,88,32,96,40,104,48,112,56,120},{1,65,9,73,17,81,25,..., dimensions={0} | all-to-all | bytes 1048576 | tf_op jit(solution)/shard_map/all_to_all | solution.py:556
  34.8 0.0 copy-start.3
  34.8 3.4 %shard_map.100 = (f32[28,128,128]{2,1,0:T(8,128)}, f32[64,128,128]{2,1,0:T(8,128)S(1)}) custom-call(s32[16,128]{1,0:T(8,128)S(1)} %copy-done.2, f32[8,16,128,128]{3,2,1,0:T(8,128)} %bitcast.273, f32[8,128]{1,0:T(8,128)S(1)} %slice_bitcast_fusion.2.refs_2_, f32[8,16,128,128]{3,2,1,0:T(8,128)} %bitcast.271), custom_call_target="tpu_custom_call" | custom-call | bytes 4194304 | tf_op jit(solution)/shard_map/pallas_call | solution.py:370
  38.2 0.0 copy-start
  38.2 2.0 copy-done
  40.2 0.0 all-gather.5.cloned.1.call-update
  40.2 12.2 %all-gather.3.cloned.1.call-done.refs_4_ = f32[80,128,128]{2,1,0:T(8,128)} async-done(((f32[10,128,128]{2,1,0:T(8,128)}), f32[80,128,128]{2,1,0:T(8,128)}) %all-gather.3.cloned.1.call-update) | async-done | bytes 5242896 | tf_op jit(solution)/shard_map/all_gather | solution.py:558
  52.4 0.0 copy-done.3
  52.4 0.0 copy-start.1
  52.4 4.1 %shard_map.98 = (f32[16,8,8,128]{3,2,1,0:T(8,128)S(1)}, f32[64,128,128]{2,1,0:T(8,128)S(1)}) custom-call(s32[16,128]{1,0:T(8,128)S(1)} %copy-done.3, f32[16,8,8,128]{3,2,1,0:T(8,128)S(1)} %all_to_all.65.refs_1_, f32[8,64,128]{2,1,0:T(8,128)S(1)} %bitcast.290, f32[8,128,128]{2,1,0:T(8,128)S(1)} %bitcast.276, f32[80,128,128]{2,1,0:T(8,128)} %all-gather.3.cloned.1.call-done.refs_4_), custom_call_target="tpu_custom_call" | custom-call | bytes 8388608 | tf_op jit(solution)/shard_map/pallas_call | solution.py:506
  56.5 18.3 %all_to_all.66.refs_1_ = f32[16,8,8,128]{3,2,1,0:T(8,128)S(1)} all-to-all(f32[16,8,8,128]{3,2,1,0:T(8,128)S(1)} %get-tuple-element.76), channel_id=1, replica_groups={{0,64,8,72,16,80,24,88,32,96,40,104,48,112,56,120},{1,65,9,73,17,81,25,..., dimensions={0} | all-to-all | bytes 1048576 | tf_op jit(solution)/shard_map/all_to_all | solution.py:556
  74.7 1.2 shard_map.99
  75.9 13.3 %all_to_all.67.refs_1_ = f32[16,8,8,128]{3,2,1,0:T(8,128)S(1)} all-to-all(f32[16,8,8,128]{3,2,1,0:T(8,128)S(1)} %shard_map.99), channel_id=1, replica_groups={{0,64,8,72,16,80,24,88,32,96,40,104,48,112,56,120},{1,65,9,73,17,81,25,..., dimensions={0} | all-to-all | bytes 1048576 | tf_op jit(solution)/shard_map/all_to_all | solution.py:556
  89.3 20.9 %all_to_all.68.known = f32[8,2,8,8,128]{4,3,2,1,0:T(8,128)S(1)} all-to-all(f32[8,2,8,8,128]{4,3,2,1,0:T(8,128)S(1)} %bitcast.269), channel_id=1, replica_groups=mesh['prow'=16,'pcol'=8] {'pcol'}, dimensions={0} | all-to-all | bytes 1048576 | tf_op jit(solution)/shard_map/all_to_all | solution.py:566
  110.2 0.0 copy-done.1
  110.2 2.4 shard_map.101
  112.6 0.0 copy-start.8
  112.7 13.0 %all_to_all.69.refs_5_ = f32[8,8,8,128]{3,2,1,0:T(8,128)S(1)} all-to-all(f32[8,8,8,128]{3,2,1,0:T(8,128)S(1)} %shard_map.101), channel_id=1, replica_groups=mesh['prow'=16,'pcol'=8] {'pcol'}, dimensions={0} | all-to-all | bytes 524288 | tf_op jit(solution)/shard_map/all_to_all | solution.py:567
  125.7 0.9 shard_map.102
  126.6 12.6 %all_to_all.70.refs_1_ = f32[16,8,8,128]{3,2,1,0:T(8,128)S(1)} all-to-all(f32[16,8,8,128]{3,2,1,0:T(8,128)S(1)} %shard_map.102), channel_id=1, replica_groups={{0,64,8,72,16,80,24,88,32,96,40,104,48,112,56,120},{1,65,9,73,17,81,25,..., dimensions={0} | all-to-all | bytes 1048576 | tf_op jit(solution)/shard_map/all_to_all | solution.py:556
  139.2 0.7 shard_map.103
  139.9 13.5 %all_to_all.71.refs_1_ = f32[16,8,8,128]{3,2,1,0:T(8,128)S(1)} all-to-all(f32[16,8,8,128]{3,2,1,0:T(8,128)S(1)} %shard_map.103), channel_id=1, replica_groups={{0,64,8,72,16,80,24,88,32,96,40,104,48,112,56,120},{1,65,9,73,17,81,25,..., dimensions={0} | all-to-all | bytes 1048576 | tf_op jit(solution)/shard_map/all_to_all | solution.py:556
  153.5 0.0 copy-done.8
  153.5 2.0 shard_map.104
  155.5 11.7 %all_to_all.72.refs_1_ = f32[16,8,8,128]{3,2,1,0:T(8,128)S(1)} all-to-all(f32[16,8,8,128]{3,2,1,0:T(8,128)S(1)} %get-tuple-element.79), channel_id=1, replica_groups={{0,64,8,72,16,80,24,88,32,96,40,104,48,112,56,120},{1,65,9,73,17,81,25,..., dimensions={0} | all-to-all | bytes 1048576 | tf_op jit(solution)/shard_map/all_to_all | solution.py:556
  167.2 0.0 all-gather.5.cloned.1.call-done.refs_4_
  167.2 3.5 %shard_map.105 = (f32[16,8,8,128]{3,2,1,0:T(8,128)S(1)}, f32[64,128,128]{2,1,0:T(8,128)S(1)}, f32[8,8,128]{2,1,0:T(8,128)S(1)}) custom-call(s32[16,128]{1,0:T(8,128)S(1)} %copy-done.3, f32[16,8,8,128]{3,2,1,0:T(8,128)S(1)} %all_to_all.72.refs_1_, f32[8,8,128]{2,1,0:T(8,128)S(1)} %get-tuple-element.80.refs_2_.refs_5_, f32[8,128,128]{2,1,0:T(8,128)S(1)} %bitcast.283, ...), custom_call_target="tpu_custom_call" | custom-call | bytes 8388608 | tf_op jit(solution)/shard_map/pallas_call | solution.py:506
  170.7 13.1 %all_to_all.73.refs_1_ = f32[16,8,8,128]{3,2,1,0:T(8,128)S(1)} all-to-all(f32[16,8,8,128]{3,2,1,0:T(8,128)S(1)} %get-tuple-element.82), channel_id=1, replica_groups={{0,64,8,72,16,80,24,88,32,96,40,104,48,112,56,120},{1,65,9,73,17,81,25,..., dimensions={0} | all-to-all | bytes 1048576 | tf_op jit(solution)/shard_map/all_to_all | solution.py:556
  183.8 1.2 shard_map.106
  185.0 11.9 %all_to_all.74.refs_1_ = f32[16,8,8,128]{3,2,1,0:T(8,128)S(1)} all-to-all(f32[16,8,8,128]{3,2,1,0:T(8,128)S(1)} %get-tuple-element.85), channel_id=1, replica_groups={{0,64,8,72,16,80,24,88,32,96,40,104,48,112,56,120},{1,65,9,73,17,81,25,..., dimensions={0} | all-to-all | bytes 1048576 | tf_op jit(solution)/shard_map/all_to_all | solution.py:556
  196.9 1.2 shard_map.107
  198.1 0.0 copy-start.5
  198.1 12.0 %all_to_all.75.refs_1_ = f32[16,8,8,128]{3,2,1,0:T(8,128)S(1)} all-to-all(f32[16,8,8,128]{3,2,1,0:T(8,128)S(1)} %get-tuple-element.87), channel_id=1, replica_groups={{0,64,8,72,16,80,24,88,32,96,40,104,48,112,56,120},{1,65,9,73,17,81,25,..., dimensions={0} | all-to-all | bytes 1048576 | tf_op jit(solution)/shard_map/all_to_all | solution.py:556
  210.2 1.2 shard_map.108
  211.4 12.4 %all_to_all.76.refs_1_ = f32[16,8,8,128]{3,2,1,0:T(8,128)S(1)} all-to-all(f32[16,8,8,128]{3,2,1,0:T(8,128)S(1)} %get-tuple-element.89), channel_id=1, replica_groups={{0,64,8,72,16,80,24,88,32,96,40,104,48,112,56,120},{1,65,9,73,17,81,25,..., dimensions={0} | all-to-all | bytes 1048576 | tf_op jit(solution)/shard_map/all_to_all | solution.py:556
  223.8 2.0 shard_map.109
  225.7 13.3 %all-to-all-start.12 = ((f32[8,2,8,8,128]{4,3,2,1,0:T(8,128)}), f32[8,2,8,8,128]{4,3,2,1,0:T(8,128)S(1)}, u32[]{:S(2)}, u32[]{:S(2)}) async-start(f32[8,2,8,8,128]{4,3,2,1,0:T(8,128)} %shard_map.109), calls=%async_computation.12 | async-start | bytes 1048576 | tf_op jit(solution)/shard_map/all_to_all | solution.py:581
  239.0 0.6 slice.19
  239.6 0.0 copy-done.5
  239.6 0.1 copy.70
  239.7 8.8 %all-to-all-done.12 = f32[8,2,8,8,128]{4,3,2,1,0:T(8,128)S(1)} async-done(((f32[8,2,8,8,128]{4,3,2,1,0:T(8,128)}), f32[8,2,8,8,128]{4,3,2,1,0:T(8,128)S(1)}, u32[]{:S(2)}, u32[]{:S(2)}) %all-to-all-start.12) | async-done | bytes 524320 | tf_op jit(solution)/shard_map/all_to_all | solution.py:581
  248.5 0.8 copy_bitcast_fusion
  249.4 0.9 while.11
  (2 shorter events, 0.0 us)
Async XLA Ops:
  7.2 5.0 %copy-start.11 = (s32[128]{0:T(128)S(1)}, s32[128]{0:T(128)}, u32[]{:S(2)}) copy-start(s32[128]{0:T(128)} %param.16) | copy-start | bytes 1540
  7.2 5.0 %copy-start.12 = (s32[128]{0:T(128)S(1)}, s32[128]{0:T(128)}, u32[]{:S(2)}) copy-start(s32[128]{0:T(128)} %param.17) | copy-start | bytes 1540
  7.2 45.2 %all-gather.3.cloned.1.call-start = ((), (), s32[]{:S(2)}) async-start(), calls=%async_computation.34 | async-start | bytes 5898240 | tf_op jit(solution)/shard_map/all_gather | solution.py:558
  7.2 0.8 copy-start.4
  8.1 6.7 %copy-start.7 = (f32[8,1,128,128]{3,2,1,0:T(8,128)S(1)}, f32[8,1,128,128]{3,2,1,0:T(8,128)}, u32[]{:S(2)}) copy-start(f32[8,1,128,128]{3,2,1,0:T(8,128)} %param.13) | copy-start | bytes 1572868
  8.1 6.7 %copy-start.9 = (f32[8,1,64,128]{3,2,1,0:T(8,128)S(1)}, f32[8,1,64,128]{3,2,1,0:T(8,128)}, u32[]{:S(2)}) copy-start(f32[8,1,64,128]{3,2,1,0:T(8,128)} %param.10) | copy-start | bytes 786436
  11.6 0.5 copy-start.6
  12.1 155.1 %all-gather.5.cloned.1.call-start = ((), (), s32[]{:S(2)}) async-start(), calls=%async_computation.35 | async-start | bytes 16515072 | tf_op jit(solution)/shard_map/all_gather | solution.py:562
  14.8 0.7 copy-start.2
  34.8 17.5 %copy-start.3 = (s32[16,128]{1,0:T(8,128)S(1)}, s32[16,128]{1,0:T(8,128)}, u32[]{:S(2)}) copy-start(s32[16,128]{1,0:T(8,128)} %shard_map.96.refs_0_.table) | copy-start | bytes 24580
  38.2 2.0 copy-start
  52.4 57.8 %copy-start.1 = (f32[64,128,128]{2,1,0:T(8,128)S(1)}, f32[64,128,128]{2,1,0:T(8,128)}, u32[]{:S(2)}) copy-start(f32[64,128,128]{2,1,0:T(8,128)} %copy-done) | copy-start | bytes 12582916
  112.6 40.8 %copy-start.8 = (f32[8,1,128,128]{3,2,1,0:T(8,128)S(1)}, f32[8,1,128,128]{3,2,1,0:T(8,128)}, u32[]{:S(2)}) copy-start(f32[8,1,128,128]{3,2,1,0:T(8,128)} %param.14) | copy-start | bytes 1572868
  198.1 41.5 %copy-start.5 = (s32[128,128]{1,0:T(8,128)S(1)}, s32[128,128]{1,0:T(8,128)}, u32[]{:S(2)}) copy-start(s32[128,128]{1,0:T(8,128)} %pattern.3) | copy-start | bytes 196612
  225.7 22.8 %all-to-all-start.12 = ((f32[8,2,8,8,128]{4,3,2,1,0:T(8,128)}), f32[8,2,8,8,128]{4,3,2,1,0:T(8,128)S(1)}, u32[]{:S(2)}, u32[]{:S(2)}) async-start(f32[8,2,8,8,128]{4,3,2,1,0:T(8,128)} %shard_map.109), calls=%async_computation.12 | async-start | bytes 1048576 | tf_op jit(solution)/shard_map/all_to_all | solution.py:581
Sparse Core Ops, SparseCore 0:
  12.2 40.0 all-gather.2
  54.2 84.6 all-gather.4

commit v7 on v6

--- a/solution.py
+++ b/solution.py
@@ -18,7 +18,6 @@
 CAP_U = 28
 LIST = 64
 GROUP = 4
-ORDER = [[PC * (k & 1) + (k >> 1) for k in range(PR)]]
 HBM = pl.BlockSpec(memory_space=pl.ANY)
 ROOM = 44 * 1024 * 1024
 SMEM = pl.BlockSpec(memory_space=pltpu.SMEM)
@@ -412,7 +411,7 @@
                 parts = [x + y for x, y in zip(parts[::2], parts[1::2])]
             mine = mine - parts[0]
         sums[a] = mine
-        old = known[((p & (PC - 1)) << 1) + (p >> 3), a] if known is not None else jnp.zeros((HS, W), jnp.float32)
+        old = known[p, a] if known is not None else jnp.zeros((HS, W), jnp.float32)
         for r in range(copies):
             if both:
                 out[r, 0, a] = less[a]
@@ -437,8 +436,8 @@
 
                 t = jnp.minimum(t, e1 - 1)
                 node = (table[row, t] >> 3) & (NB - 1)
-                x = known[((node & (PC - 1)) << 1) + ((node >> 3) & 1), node >> 4] * jnp.where(there, 1.0, 0.0)
-                terms.append((table[row, t] & (RB - 1), dot3(x, blocks[t])))
+                x = known[node & (PR - 1), node >> 4] * jnp.where(there, 1.0, 0.0)
+                terms.append((table[row, t] & (RB - 1), dot3(x, blocks[t if kind else table[row, t] >> 10])))
             for a, term in terms:
                 sums[a] -= term
 
@@ -553,20 +552,20 @@
     upper_inv = upper_inverse.reshape(RB, W, W)
     packed_l, token = first(pattern, levels, lower_blocks)
     table = tables(pattern, levels, widths, token)
-    swap = lambda x: lax.all_to_all(x, "prow", 0, 0, axis_index_groups=ORDER)
+    swap = lambda x: lax.all_to_all(x, "prow", 0, 0)
 
     panel_l = lax.all_gather(packed_l, "pcol", tiled=True)
     leaves = level_step(0, PR, 0, table, None, right, lower_inv, None, sliced=True)
     known = swap(leaves)
     packed_u, far_blocks = pack(1, CAP_U, table, upper_blocks, known[0, 0], lower_blocks)
     panel_u = lax.all_gather(packed_u, "pcol", tiled=True)
-    state, held = level_step(1, PR, 0, table, known, right, lower_inv, panel_l, sliced=True, group=8, fetch=True)
-    known = swap(state)
-    known = swap(level_step(2, PR, 0, table, known, right, lower_inv, held, sliced=True, group=8))
-    columns = lax.all_to_all(known.reshape(PC, 2, RB, HS, W), "pcol", 0, 0)
+    for level in (1, 2):
+        known = swap(level_step(level, PR, 0, table, known, right, lower_inv, panel_l, sliced=True, group=8))
+    split = known.reshape(2, PC, RB, HS, W).transpose(1, 0, 2, 3, 4)
+    columns = lax.all_to_all(split, "pcol", 0, 0)
     sums = lax.all_to_all(across(table, columns, far_blocks), "pcol", 0, 0)
     step = lambda level, turn=None: level_step(
-        level, PR, 0, table, known, right, lower_inv, held, turn=turn, sliced=True, less=sums
+        level, PR, 0, table, known, right, lower_inv, panel_l, turn=turn, sliced=True, less=sums
     )
     for level in range(3, LEVELS - 1):
         known = swap(step(level))

time: 257 us -> 253 us (0.984)
  Pallas kernels: 30.9 us -> 25.3 us
    pallas_call x11, Pallas kernels: 18.9 us -> 14.9 us  [level_step(): pl.pallas_call(kernel, out_shape=[jax.ShapeDtypeStruct(x, jnp.float32) fo...]
    unnamed x24 -> x28, local copies, waits for them, and re-layouts: 4.02 us -> 6.51 us
  transfers between devices with their start and end apart: 3 -> 3, of which waited for: 2 -> 2; matrix products, arithmetic and copies ran while one was open for 0% -> 0% of each run, Pallas kernels for 7% -> 5%
where the time goes in v7:
time: 253 us; the launch traced here: 251 us
  blocking collectives  169 us (67%)
  Pallas kernels  25.3 us (10%)
  waiting for transfers between devices  20.2 us (8%)
  between operations  14.3 us (6%)
  starting transfers between devices  13.5 us (5%)
  local copies, waits for them, and re-layouts  8.07 us (3%)
    all_to_all x10, blocking collectives, local(): swap = lambda x: lax.all_to_all(x, 'prow', 0, 0)  136 us
    all_to_all x1, blocking collectives, local(): columns = lax.all_to_all(split, 'pcol', 0, 0)  20.2 us
    pallas_call x11, Pallas kernels, level_step(): pl.pallas_call(kernel, out_shape=[jax.ShapeDtypeStruct(x, jnp.float32) fo...  14.9 us
    all_to_all x1, starting transfers between devices, local(): full = lax.all_to_all(state, 'pcol', 0, 0)  13.4 us
    all_to_all x1, blocking collectives, local(): sums = lax.all_to_all(across(table, columns, far_blocks), 'pcol', 0, 0)  13.1 us
    all_gather x1, waiting for transfers between devices, local(): panel_l = lax.all_gather(packed_l, 'pcol', tiled=True)  11.3 us
    all_to_all x1, waiting for transfers between devices, local(): full = lax.all_to_all(state, 'pcol', 0, 0)  8.85 us
    unnamed x28, local copies, waits for them, and re-layouts  6.51 us
  transfers between devices with their start and end apart: 3, of which 2 were waited for; matrix products, arithmetic and copies ran while one was open for 0% of the time, Pallas kernels for 5%

profile of v7, /device:TPU:1, one launch (start us, length us, event | category | flops | bytes accessed | tf_op | source)
XLA Modules:
  0.0 251.5 jit_solution(8049313904407756004)
XLA Ops:
  7.2 0.0 copy-start.13
  7.2 0.0 copy-start.14
  7.2 0.0 all-gather.3.cloned.1.call-start
  7.2 0.0 copy-start.6
  7.2 0.8 copy-done.6
  8.1 0.0 copy-start.9
  8.1 0.0 copy-start.11
  8.1 3.5 %shard_map.95 = (f32[10,128,128]{2,1,0:T(8,128)}, s32[1,128]{1,0:T(1,128)S(1)}) custom-call(s32[128,128]{1,0:T(8,128)S(1)} %copy-done.6, s32[1,128]{1,0:T(1,128)} %bitcast.313, f32[8,16,128,128]{3,2,1,0:T(8,128)} %bitcast.273), custom_call_target="tpu_custom_call" | custom-call | bytes 4194304 | tf_op jit(solution)/shard_map/pallas_call | solution.py:304
  11.6 0.0 copy-start.8
  11.6 0.5 copy-done.8
  12.1 0.0 all-gather.3.cloned.1.call-update
  12.1 0.0 all-gather.5.cloned.1.call-start
  12.1 0.0 copy-done.13
  12.2 0.0 copy-done.14
  12.2 2.6 %shard_map.96.refs_0_.table = s32[16,128]{1,0:T(8,128)} custom-call(s32[128,128]{1,0:T(8,128)} %pattern.3, s32[1,128]{1,0:T(1,128)S(1)} %bitcast.314, s32[1,128]{1,0:T(1,128)S(1)} %bitcast.315, s32[1,128]{1,0:T(1,128)} %copy-done.8), custom_call_target="tpu_custom_call" | custom-call | bytes 4194304 | tf_op jit(solution)/shard_map/pallas_call | solution.py:257
  14.8 0.0 copy-done.9
  14.8 0.0 copy-done.11
  14.8 0.0 copy-start.4
  14.8 0.7 copy-done.4
  15.5 0.9 shard_map.97
  16.5 19.0 %all_to_all.65.refs_1_ = f32[16,8,8,128]{3,2,1,0:T(8,128)S(1)} all-to-all(f32[16,8,8,128]{3,2,1,0:T(8,128)S(1)} %shard_map.97), channel_id=1, replica_groups=mesh['prow'=16,'pcol'=8] {'prow'}, dimensions={0} | all-to-all | bytes 1048576 | tf_op jit(solution)/shard_map/all_to_all | solution.py:555
  35.5 0.0 copy-start.5
  35.5 3.6 %shard_map.100 = (f32[28,128,128]{2,1,0:T(8,128)}, f32[64,128,128]{2,1,0:T(8,128)S(1)}) custom-call(s32[16,128]{1,0:T(8,128)S(1)} %copy-done.4, f32[8,16,128,128]{3,2,1,0:T(8,128)} %bitcast.276, f32[8,128]{1,0:T(8,128)S(1)} %slice_bitcast_fusion.2.refs_2_, f32[8,16,128,128]{3,2,1,0:T(8,128)} %bitcast.274), custom_call_target="tpu_custom_call" | custom-call | bytes 4194304 | tf_op jit(solution)/shard_map/pallas_call | solution.py:369
  39.1 0.0 copy-start.2
  39.1 1.9 copy-done.2
  41.0 0.0 all-gather.5.cloned.1.call-update
  41.0 11.3 %all-gather.3.cloned.1.call-done.refs_4_ = f32[80,128,128]{2,1,0:T(8,128)} async-done(((f32[10,128,128]{2,1,0:T(8,128)}), f32[80,128,128]{2,1,0:T(8,128)}) %all-gather.3.cloned.1.call-update) | async-done | bytes 5242896 | tf_op jit(solution)/shard_map/all_gather | solution.py:557
  52.4 0.0 copy-done.5
  52.4 0.0 copy-start
  52.4 2.5 copy-done
  54.8 0.0 copy-start.1
  54.9 1.2 shard_map.98
  56.1 17.6 %all_to_all.66.refs_1_ = f32[16,8,8,128]{3,2,1,0:T(8,128)S(1)} all-to-all(f32[16,8,8,128]{3,2,1,0:T(8,128)S(1)} %shard_map.98), channel_id=1, replica_groups=mesh['prow'=16,'pcol'=8] {'prow'}, dimensions={0} | all-to-all | bytes 1048576 | tf_op jit(solution)/shard_map/all_to_all | solution.py:555
  73.6 0.0 copy-done.1
  73.6 1.2 shard_map.99
  74.8 13.6 %all_to_all.67.refs_1_ = f32[16,8,8,128]{3,2,1,0:T(8,128)S(1)} all-to-all(f32[16,8,8,128]{3,2,1,0:T(8,128)S(1)} %shard_map.99), channel_id=1, replica_groups=mesh['prow'=16,'pcol'=8] {'prow'}, dimensions={0} | all-to-all | bytes 1048576 | tf_op jit(solution)/shard_map/all_to_all | solution.py:555
  88.5 20.2 %all_to_all.68.known = f32[8,2,8,8,128]{4,3,2,1,0:T(8,128)S(1)} all-to-all(f32[8,2,8,8,128]{4,3,2,1,0:T(8,128)S(1)} %bitcast.311), channel_id=1, replica_groups=mesh['prow'=16,'pcol'=8] {'pcol'}, dimensions={0} | all-to-all | bytes 1048576 | tf_op jit(solution)/shard_map/all_to_all | solution.py:565
  108.7 0.0 copy-done.3
  108.7 0.7 shard_map.101
  109.4 13.1 %all_to_all.69.refs_5_ = f32[8,8,8,128]{3,2,1,0:T(8,128)S(1)} all-to-all(f32[8,8,8,128]{3,2,1,0:T(8,128)S(1)} %shard_map.101), channel_id=1, replica_groups=mesh['prow'=16,'pcol'=8] {'pcol'}, dimensions={0} | all-to-all | bytes 524288 | tf_op jit(solution)/shard_map/all_to_all | solution.py:566
  122.5 0.7 shard_map.102
  123.2 13.5 %all_to_all.70.refs_1_ = f32[16,8,8,128]{3,2,1,0:T(8,128)S(1)} all-to-all(f32[16,8,8,128]{3,2,1,0:T(8,128)S(1)} %shard_map.102), channel_id=1, replica_groups=mesh['prow'=16,'pcol'=8] {'prow'}, dimensions={0} | all-to-all | bytes 1048576 | tf_op jit(solution)/shard_map/all_to_all | solution.py:555
  136.7 0.7 shard_map.103
  137.5 12.8 %all_to_all.71.refs_1_ = f32[16,8,8,128]{3,2,1,0:T(8,128)S(1)} all-to-all(f32[16,8,8,128]{3,2,1,0:T(8,128)S(1)} %shard_map.103), channel_id=1, replica_groups=mesh['prow'=16,'pcol'=8] {'prow'}, dimensions={0} | all-to-all | bytes 1048576 | tf_op jit(solution)/shard_map/all_to_all | solution.py:555
  150.3 0.0 copy-done.10
  150.3 0.7 shard_map.104
  151.0 12.0 %all_to_all.72.refs_1_ = f32[16,8,8,128]{3,2,1,0:T(8,128)S(1)} all-to-all(f32[16,8,8,128]{3,2,1,0:T(8,128)S(1)} %get-tuple-element.75), channel_id=1, replica_groups=mesh['prow'=16,'pcol'=8] {'prow'}, dimensions={0} | all-to-all | bytes 1048576 | tf_op jit(solution)/shard_map/all_to_all | solution.py:555
  163.0 3.5 %shard_map.105 = (f32[16,8,8,128]{3,2,1,0:T(8,128)S(1)}, f32[64,128,128]{2,1,0:T(8,128)S(1)}, f32[8,8,128]{2,1,0:T(8,128)S(1)}) custom-call(s32[16,128]{1,0:T(8,128)S(1)} %copy-done.5, f32[16,8,8,128]{3,2,1,0:T(8,128)S(1)} %all_to_all.72.refs_1_, f32[8,8,128]{2,1,0:T(8,128)S(1)} %get-tuple-element.76.refs_2_.refs_5_, f32[8,128,128]{2,1,0:T(8,128)S(1)} %bitcast.286, ...), custom_call_target="tpu_custom_call" | custom-call | bytes 8388608 | tf_op jit(solution)/shard_map/pallas_call | solution.py:505
  166.6 12.5 %all_to_all.73.refs_1_ = f32[16,8,8,128]{3,2,1,0:T(8,128)S(1)} all-to-all(f32[16,8,8,128]{3,2,1,0:T(8,128)S(1)} %get-tuple-element.78), channel_id=1, replica_groups=mesh['prow'=16,'pcol'=8] {'prow'}, dimensions={0} | all-to-all | bytes 1048576 | tf_op jit(solution)/shard_map/all_to_all | solution.py:555
  179.0 1.2 shard_map.106
  180.3 11.7 %all_to_all.74.refs_1_ = f32[16,8,8,128]{3,2,1,0:T(8,128)S(1)} all-to-all(f32[16,8,8,128]{3,2,1,0:T(8,128)S(1)} %get-tuple-element.81), channel_id=1, replica_groups=mesh['prow'=16,'pcol'=8] {'prow'}, dimensions={0} | all-to-all | bytes 1048576 | tf_op jit(solution)/shard_map/all_to_all | solution.py:555
  191.9 1.2 shard_map.107
  193.1 0.0 copy-start.7
  193.1 11.8 %all_to_all.75.refs_1_ = f32[16,8,8,128]{3,2,1,0:T(8,128)S(1)} all-to-all(f32[16,8,8,128]{3,2,1,0:T(8,128)S(1)} %get-tuple-element.83), channel_id=1, replica_groups=mesh['prow'=16,'pcol'=8] {'prow'}, dimensions={0} | all-to-all | bytes 1048576 | tf_op jit(solution)/shard_map/all_to_all | solution.py:555
  204.9 1.5 shard_map.108
  206.4 11.6 %all_to_all.76.refs_1_ = f32[16,8,8,128]{3,2,1,0:T(8,128)S(1)} all-to-all(f32[16,8,8,128]{3,2,1,0:T(8,128)S(1)} %get-tuple-element.85), channel_id=1, replica_groups=mesh['prow'=16,'pcol'=8] {'prow'}, dimensions={0} | all-to-all | bytes 1048576 | tf_op jit(solution)/shard_map/all_to_all | solution.py:555
  218.0 2.0 shard_map.109
  220.0 13.4 %all-to-all-start.12 = ((f32[8,2,8,8,128]{4,3,2,1,0:T(8,128)}), f32[8,2,8,8,128]{4,3,2,1,0:T(8,128)S(1)}, u32[]{:S(2)}, u32[]{:S(2)}) async-start(f32[8,2,8,8,128]{4,3,2,1,0:T(8,128)} %shard_map.109), calls=%async_computation.12 | async-start | bytes 1048576 | tf_op jit(solution)/shard_map/all_to_all | solution.py:580
  233.4 0.6 slice.19
  234.0 0.0 copy-done.7
  234.0 0.1 copy.74
  234.1 8.8 %all-to-all-done.12 = f32[8,2,8,8,128]{4,3,2,1,0:T(8,128)S(1)} async-done(((f32[8,2,8,8,128]{4,3,2,1,0:T(8,128)}), f32[8,2,8,8,128]{4,3,2,1,0:T(8,128)S(1)}, u32[]{:S(2)}, u32[]{:S(2)}) %all-to-all-start.12) | async-done | bytes 524320 | tf_op jit(solution)/shard_map/all_to_all | solution.py:580
  243.0 0.8 copy_bitcast_fusion.1
  243.8 0.8 while.11
  (6 shorter events, 0.1 us)
Async XLA Ops:
  7.2 5.0 %copy-start.13 = (s32[128]{0:T(128)S(1)}, s32[128]{0:T(128)}, u32[]{:S(2)}) copy-start(s32[128]{0:T(128)} %param.16) | copy-start | bytes 1540
  7.2 5.0 %copy-start.14 = (s32[128]{0:T(128)S(1)}, s32[128]{0:T(128)}, u32[]{:S(2)}) copy-start(s32[128]{0:T(128)} %param.17) | copy-start | bytes 1540
  7.2 45.2 %all-gather.3.cloned.1.call-start = ((), (), s32[]{:S(2)}) async-start(), calls=%async_computation.34 | async-start | bytes 5898240 | tf_op jit(solution)/shard_map/all_gather | solution.py:557
  7.2 0.8 copy-start.6
  8.1 6.7 %copy-start.9 = (f32[8,1,128,128]{3,2,1,0:T(8,128)S(1)}, f32[8,1,128,128]{3,2,1,0:T(8,128)}, u32[]{:S(2)}) copy-start(f32[8,1,128,128]{3,2,1,0:T(8,128)} %param.13) | copy-start | bytes 1572868
  8.1 6.7 %copy-start.11 = (f32[8,1,64,128]{3,2,1,0:T(8,128)S(1)}, f32[8,1,64,128]{3,2,1,0:T(8,128)}, u32[]{:S(2)}) copy-start(f32[8,1,64,128]{3,2,1,0:T(8,128)} %param.10) | copy-start | bytes 786436
  11.6 0.5 copy-start.8
  12.1 150.9 %all-gather.5.cloned.1.call-start = ((), (), s32[]{:S(2)}) async-start(), calls=%async_computation.35 | async-start | bytes 16515072 | tf_op jit(solution)/shard_map/all_gather | solution.py:561
  14.8 0.7 copy-start.4
  35.5 16.9 %copy-start.5 = (s32[16,128]{1,0:T(8,128)S(1)}, s32[16,128]{1,0:T(8,128)}, u32[]{:S(2)}) copy-start(s32[16,128]{1,0:T(8,128)} %shard_map.96.refs_0_.table) | copy-start | bytes 24580
  39.1 2.0 copy-start.2
  52.4 2.5 copy-start
  54.8 18.8 %copy-start.1 = (f32[80,128,128]{2,1,0:T(8,128)S(1)}, f32[80,128,128]{2,1,0:T(8,128)}, u32[]{:S(2)}) copy-start(f32[80,128,128]{2,1,0:T(8,128)} %all-gather.3.cloned.1.call-done.refs_4_) | copy-start | bytes 15728644
  54.8 53.8 %copy-start.3 = (f32[64,128,128]{2,1,0:T(8,128)S(1)}, f32[64,128,128]{2,1,0:T(8,128)}, u32[]{:S(2)}) copy-start(f32[64,128,128]{2,1,0:T(8,128)} %copy-done.2) | copy-start | bytes 12582916
  122.5 27.8 %copy-start.10 = (f32[8,1,128,128]{3,2,1,0:T(8,128)S(1)}, f32[8,1,128,128]{3,2,1,0:T(8,128)}, u32[]{:S(2)}) copy-start(f32[8,1,128,128]{3,2,1,0:T(8,128)} %param.14) | copy-start | bytes 1572868
  193.1 40.9 %copy-start.7 = (s32[128,128]{1,0:T(8,128)S(1)}, s32[128,128]{1,0:T(8,128)}, u32[]{:S(2)}) copy-start(s32[128,128]{1,0:T(8,128)} %pattern.3) | copy-start | bytes 196612
  220.0 22.9 %all-to-all-start.12 = ((f32[8,2,8,8,128]{4,3,2,1,0:T(8,128)}), f32[8,2,8,8,128]{4,3,2,1,0:T(8,128)S(1)}, u32[]{:S(2)}, u32[]{:S(2)}) async-start(f32[8,2,8,8,128]{4,3,2,1,0:T(8,128)} %shard_map.109), calls=%async_computation.12 | async-start | bytes 1048576 | tf_op jit(solution)/shard_map/all_to_all | solution.py:580
Sparse Core Ops, SparseCore 0:
  12.2 40.0 all-gather.2
  54.2 84.5 all-gather.4

commit v8 on v7

--- a/solution.py
+++ b/solution.py
@@ -267,11 +267,11 @@
     p = lax.axis_index("prow")
     q = lax.axis_index("pcol")
     lev = levels[...].astype(jnp.float32)
-    i, j = iota((NB, NB), 0), iota((NB, NB), 1)
-    lev_col = jnp.sum(jnp.where(i == j, lev, 0.0), axis=1, keepdims=True)
-    near = flag(pattern[...] > 0) * flag(lev < lev_col) * flag((lev_col < 2.5) | (lev > 2.5))
     lane, sub = iota((RB, NB), 1), iota((RB, NB), 0)
-    sel = dot(flag(lane == sub * PR + p), near) * flag((lane & (PC - 1)) == q)
+    mine = flag(lane == sub * PR + p)
+    row_lev = jnp.sum(mine * lev, axis=1, keepdims=True)
+    wanted = flag(lev < row_lev) * flag((row_lev < 2.5) | (lev > 2.5)) * flag((lane & (PC - 1)) == q)
+    sel = dot(mine, flag(pattern[...] > 0)) * wanted
     spot = (sub * CB + (lane >> 3)).astype(jnp.float32)
     found = listing(sel, ranks(sel), spot, 32)
     number = jnp.minimum(count(sel), CAP_L)

time: 253 us -> 253 us (level)
  no operation moved by 1% of the time
where the time goes in v8:
time: 253 us; the launch traced here: 252 us
  blocking collectives  168 us (66%)
  Pallas kernels  26.3 us (10%)
  waiting for transfers between devices  21.1 us (8%)
  between operations  14.3 us (6%)
  starting transfers between devices  13.4 us (5%)
  local copies, waits for them, and re-layouts  8.07 us (3%)
    all_to_all x10, blocking collectives, local(): swap = lambda x: lax.all_to_all(x, 'prow', 0, 0)  135 us
    all_to_all x1, blocking collectives, local(): columns = lax.all_to_all(split, 'pcol', 0, 0)  20.4 us
    pallas_call x11, Pallas kernels, level_step(): pl.pallas_call(kernel, out_shape=[jax.ShapeDtypeStruct(x, jnp.float32) fo...  15.3 us
    all_to_all x1, starting transfers between devices, local(): full = lax.all_to_all(state, 'pcol', 0, 0)  13.3 us
    all_to_all x1, blocking collectives, local(): sums = lax.all_to_all(across(table, columns, far_blocks), 'pcol', 0, 0)  12.8 us
    all_gather x1, waiting for transfers between devices, local(): panel_l = lax.all_gather(packed_l, 'pcol', tiled=True)  12.2 us
    all_to_all x1, waiting for transfers between devices, local(): full = lax.all_to_all(state, 'pcol', 0, 0)  8.85 us
    unnamed x28, local copies, waits for them, and re-layouts  6.51 us
  transfers between devices with their start and end apart: 3, of which 2 were waited for; matrix products, arithmetic and copies ran while one was open for 0% of the time, Pallas kernels for 5%

profile of v8, /device:TPU:1, one launch (start us, length us, event | category | flops | bytes accessed | tf_op | source)
XLA Modules:
  0.0 252.0 jit_solution(16391340027619170398)
XLA Ops:
  7.2 0.0 copy-start.13
  7.2 0.0 copy-start.14
  7.2 0.0 all-gather.3.cloned.1.call-start
  7.2 0.0 copy-start.6
  7.2 0.8 copy-done.6
  8.1 0.0 copy-start.9
  8.1 0.0 copy-start.11
  8.1 3.4 %shard_map.95 = (f32[10,128,128]{2,1,0:T(8,128)}, s32[1,128]{1,0:T(1,128)S(1)}) custom-call(s32[128,128]{1,0:T(8,128)S(1)} %copy-done.6, s32[1,128]{1,0:T(1,128)} %bitcast.313, f32[8,16,128,128]{3,2,1,0:T(8,128)} %bitcast.273), custom_call_target="tpu_custom_call" | custom-call | bytes 4194304 | tf_op jit(solution)/shard_map/pallas_call | solution.py:304
  11.5 0.0 copy-start.8
  11.5 0.5 copy-done.8
  12.0 0.0 all-gather.3.cloned.1.call-update
  12.0 0.0 all-gather.5.cloned.1.call-start
  12.1 0.0 copy-done.13
  12.1 0.0 copy-done.14
  12.1 2.6 %shard_map.96.refs_0_.table = s32[16,128]{1,0:T(8,128)} custom-call(s32[128,128]{1,0:T(8,128)} %pattern.3, s32[1,128]{1,0:T(1,128)S(1)} %bitcast.314, s32[1,128]{1,0:T(1,128)S(1)} %bitcast.315, s32[1,128]{1,0:T(1,128)} %copy-done.8), custom_call_target="tpu_custom_call" | custom-call | bytes 4194304 | tf_op jit(solution)/shard_map/pallas_call | solution.py:257
  14.7 0.0 copy-done.9
  14.7 0.0 copy-done.11
  14.7 0.0 copy-start.4
  14.7 0.7 copy-done.4
  15.4 1.1 shard_map.97
  16.6 18.0 %all_to_all.65.refs_1_ = f32[16,8,8,128]{3,2,1,0:T(8,128)S(1)} all-to-all(f32[16,8,8,128]{3,2,1,0:T(8,128)S(1)} %shard_map.97), channel_id=1, replica_groups=mesh['prow'=16,'pcol'=8] {'prow'}, dimensions={0} | all-to-all | bytes 1048576 | tf_op jit(solution)/shard_map/all_to_all | solution.py:555
  34.6 0.0 copy-start.5
  34.6 3.5 %shard_map.100 = (f32[28,128,128]{2,1,0:T(8,128)}, f32[64,128,128]{2,1,0:T(8,128)S(1)}) custom-call(s32[16,128]{1,0:T(8,128)S(1)} %copy-done.4, f32[8,16,128,128]{3,2,1,0:T(8,128)} %bitcast.276, f32[8,128]{1,0:T(8,128)S(1)} %slice_bitcast_fusion.2.refs_2_, f32[8,16,128,128]{3,2,1,0:T(8,128)} %bitcast.274), custom_call_target="tpu_custom_call" | custom-call | bytes 4194304 | tf_op jit(solution)/shard_map/pallas_call | solution.py:369
  38.1 0.0 copy-start.2
  38.1 1.9 copy-done.2
  40.0 0.0 all-gather.5.cloned.1.call-update
  40.1 12.2 %all-gather.3.cloned.1.call-done.refs_4_ = f32[80,128,128]{2,1,0:T(8,128)} async-done(((f32[10,128,128]{2,1,0:T(8,128)}), f32[80,128,128]{2,1,0:T(8,128)}) %all-gather.3.cloned.1.call-update) | async-done | bytes 5242896 | tf_op jit(solution)/shard_map/all_gather | solution.py:557
  52.3 0.0 copy-done.5
  52.3 0.0 copy-start
  52.3 2.5 copy-done
  54.8 0.0 copy-start.1
  54.8 1.2 shard_map.98
  56.0 17.6 %all_to_all.66.refs_1_ = f32[16,8,8,128]{3,2,1,0:T(8,128)S(1)} all-to-all(f32[16,8,8,128]{3,2,1,0:T(8,128)S(1)} %shard_map.98), channel_id=1, replica_groups=mesh['prow'=16,'pcol'=8] {'prow'}, dimensions={0} | all-to-all | bytes 1048576 | tf_op jit(solution)/shard_map/all_to_all | solution.py:555
  73.6 0.0 copy-done.1
  73.6 0.7 shard_map.99
  74.3 13.4 %all_to_all.67.refs_1_ = f32[16,8,8,128]{3,2,1,0:T(8,128)S(1)} all-to-all(f32[16,8,8,128]{3,2,1,0:T(8,128)S(1)} %shard_map.99), channel_id=1, replica_groups=mesh['prow'=16,'pcol'=8] {'prow'}, dimensions={0} | all-to-all | bytes 1048576 | tf_op jit(solution)/shard_map/all_to_all | solution.py:555
  87.7 20.4 %all_to_all.68.known = f32[8,2,8,8,128]{4,3,2,1,0:T(8,128)S(1)} all-to-all(f32[8,2,8,8,128]{4,3,2,1,0:T(8,128)S(1)} %bitcast.311), channel_id=1, replica_groups=mesh['prow'=16,'pcol'=8] {'pcol'}, dimensions={0} | all-to-all | bytes 1048576 | tf_op jit(solution)/shard_map/all_to_all | solution.py:565
  108.2 0.0 copy-done.3
  108.2 1.4 shard_map.101
  109.6 12.8 %all_to_all.69.refs_5_ = f32[8,8,8,128]{3,2,1,0:T(8,128)S(1)} all-to-all(f32[8,8,8,128]{3,2,1,0:T(8,128)S(1)} %shard_map.101), channel_id=1, replica_groups=mesh['prow'=16,'pcol'=8] {'pcol'}, dimensions={0} | all-to-all | bytes 524288 | tf_op jit(solution)/shard_map/all_to_all | solution.py:566
  122.4 0.7 shard_map.102
  123.2 13.1 %all_to_all.70.refs_1_ = f32[16,8,8,128]{3,2,1,0:T(8,128)S(1)} all-to-all(f32[16,8,8,128]{3,2,1,0:T(8,128)S(1)} %shard_map.102), channel_id=1, replica_groups=mesh['prow'=16,'pcol'=8] {'prow'}, dimensions={0} | all-to-all | bytes 1048576 | tf_op jit(solution)/shard_map/all_to_all | solution.py:555
  136.3 0.7 shard_map.103
  137.0 12.9 %all_to_all.71.refs_1_ = f32[16,8,8,128]{3,2,1,0:T(8,128)S(1)} all-to-all(f32[16,8,8,128]{3,2,1,0:T(8,128)S(1)} %shard_map.103), channel_id=1, replica_groups=mesh['prow'=16,'pcol'=8] {'prow'}, dimensions={0} | all-to-all | bytes 1048576 | tf_op jit(solution)/shard_map/all_to_all | solution.py:555
  149.9 0.0 copy-done.10
  149.9 1.4 shard_map.104
  151.3 11.7 %all_to_all.72.refs_1_ = f32[16,8,8,128]{3,2,1,0:T(8,128)S(1)} all-to-all(f32[16,8,8,128]{3,2,1,0:T(8,128)S(1)} %get-tuple-element.75), channel_id=1, replica_groups=mesh['prow'=16,'pcol'=8] {'prow'}, dimensions={0} | all-to-all | bytes 1048576 | tf_op jit(solution)/shard_map/all_to_all | solution.py:555
  163.0 3.6 %shard_map.105 = (f32[16,8,8,128]{3,2,1,0:T(8,128)S(1)}, f32[64,128,128]{2,1,0:T(8,128)S(1)}, f32[8,8,128]{2,1,0:T(8,128)S(1)}) custom-call(s32[16,128]{1,0:T(8,128)S(1)} %copy-done.5, f32[16,8,8,128]{3,2,1,0:T(8,128)S(1)} %all_to_all.72.refs_1_, f32[8,8,128]{2,1,0:T(8,128)S(1)} %get-tuple-element.76.refs_2_.refs_5_, f32[8,128,128]{2,1,0:T(8,128)S(1)} %bitcast.286, ...), custom_call_target="tpu_custom_call" | custom-call | bytes 8388608 | tf_op jit(solution)/shard_map/pallas_call | solution.py:505
  166.6 12.8 %all_to_all.73.refs_1_ = f32[16,8,8,128]{3,2,1,0:T(8,128)S(1)} all-to-all(f32[16,8,8,128]{3,2,1,0:T(8,128)S(1)} %get-tuple-element.78), channel_id=1, replica_groups=mesh['prow'=16,'pcol'=8] {'prow'}, dimensions={0} | all-to-all | bytes 1048576 | tf_op jit(solution)/shard_map/all_to_all | solution.py:555
  179.4 1.2 shard_map.106
  180.6 11.6 %all_to_all.74.refs_1_ = f32[16,8,8,128]{3,2,1,0:T(8,128)S(1)} all-to-all(f32[16,8,8,128]{3,2,1,0:T(8,128)S(1)} %get-tuple-element.81), channel_id=1, replica_groups=mesh['prow'=16,'pcol'=8] {'prow'}, dimensions={0} | all-to-all | bytes 1048576 | tf_op jit(solution)/shard_map/all_to_all | solution.py:555
  192.3 1.0 shard_map.107
  193.2 0.0 copy-start.7
  193.3 11.8 %all_to_all.75.refs_1_ = f32[16,8,8,128]{3,2,1,0:T(8,128)S(1)} all-to-all(f32[16,8,8,128]{3,2,1,0:T(8,128)S(1)} %get-tuple-element.83), channel_id=1, replica_groups=mesh['prow'=16,'pcol'=8] {'prow'}, dimensions={0} | all-to-all | bytes 1048576 | tf_op jit(solution)/shard_map/all_to_all | solution.py:555
  205.1 1.2 shard_map.108
  206.2 11.9 %all_to_all.76.refs_1_ = f32[16,8,8,128]{3,2,1,0:T(8,128)S(1)} all-to-all(f32[16,8,8,128]{3,2,1,0:T(8,128)S(1)} %get-tuple-element.85), channel_id=1, replica_groups=mesh['prow'=16,'pcol'=8] {'prow'}, dimensions={0} | all-to-all | bytes 1048576 | tf_op jit(solution)/shard_map/all_to_all | solution.py:555
  218.2 2.4 shard_map.109
  220.6 13.3 %all-to-all-start.12 = ((f32[8,2,8,8,128]{4,3,2,1,0:T(8,128)}), f32[8,2,8,8,128]{4,3,2,1,0:T(8,128)S(1)}, u32[]{:S(2)}, u32[]{:S(2)}) async-start(f32[8,2,8,8,128]{4,3,2,1,0:T(8,128)} %shard_map.109), calls=%async_computation.12 | async-start | bytes 1048576 | tf_op jit(solution)/shard_map/all_to_all | solution.py:580
  233.9 0.6 slice.19
  234.5 0.0 copy-done.7
  234.5 0.1 copy.74
  234.6 8.8 %all-to-all-done.12 = f32[8,2,8,8,128]{4,3,2,1,0:T(8,128)S(1)} async-done(((f32[8,2,8,8,128]{4,3,2,1,0:T(8,128)}), f32[8,2,8,8,128]{4,3,2,1,0:T(8,128)S(1)}, u32[]{:S(2)}, u32[]{:S(2)}) %all-to-all-start.12) | async-done | bytes 524320 | tf_op jit(solution)/shard_map/all_to_all | solution.py:580
  243.5 0.8 copy_bitcast_fusion.1
  244.3 0.8 while.11
  (6 shorter events, 0.1 us)
Async XLA Ops:
  7.2 4.9 %copy-start.13 = (s32[128]{0:T(128)S(1)}, s32[128]{0:T(128)}, u32[]{:S(2)}) copy-start(s32[128]{0:T(128)} %param.16) | copy-start | bytes 1540
  7.2 4.9 %copy-start.14 = (s32[128]{0:T(128)S(1)}, s32[128]{0:T(128)}, u32[]{:S(2)}) copy-start(s32[128]{0:T(128)} %param.17) | copy-start | bytes 1540
  7.2 45.1 %all-gather.3.cloned.1.call-start = ((), (), s32[]{:S(2)}) async-start(), calls=%async_computation.34 | async-start | bytes 5898240 | tf_op jit(solution)/shard_map/all_gather | solution.py:557
  7.2 0.8 copy-start.6
  8.1 6.7 %copy-start.9 = (f32[8,1,128,128]{3,2,1,0:T(8,128)S(1)}, f32[8,1,128,128]{3,2,1,0:T(8,128)}, u32[]{:S(2)}) copy-start(f32[8,1,128,128]{3,2,1,0:T(8,128)} %param.13) | copy-start | bytes 1572868
  8.1 6.7 %copy-start.11 = (f32[8,1,64,128]{3,2,1,0:T(8,128)S(1)}, f32[8,1,64,128]{3,2,1,0:T(8,128)}, u32[]{:S(2)}) copy-start(f32[8,1,64,128]{3,2,1,0:T(8,128)} %param.10) | copy-start | bytes 786436
  11.5 0.5 copy-start.8
  12.0 151.0 %all-gather.5.cloned.1.call-start = ((), (), s32[]{:S(2)}) async-start(), calls=%async_computation.35 | async-start | bytes 16515072 | tf_op jit(solution)/shard_map/all_gather | solution.py:561
  14.7 0.7 copy-start.4
  34.6 17.7 %copy-start.5 = (s32[16,128]{1,0:T(8,128)S(1)}, s32[16,128]{1,0:T(8,128)}, u32[]{:S(2)}) copy-start(s32[16,128]{1,0:T(8,128)} %shard_map.96.refs_0_.table) | copy-start | bytes 24580
  38.1 2.0 copy-start.2
  52.3 2.5 copy-start
  54.8 18.8 %copy-start.1 = (f32[80,128,128]{2,1,0:T(8,128)S(1)}, f32[80,128,128]{2,1,0:T(8,128)}, u32[]{:S(2)}) copy-start(f32[80,128,128]{2,1,0:T(8,128)} %all-gather.3.cloned.1.call-done.refs_4_) | copy-start | bytes 15728644
  54.8 53.4 %copy-start.3 = (f32[64,128,128]{2,1,0:T(8,128)S(1)}, f32[64,128,128]{2,1,0:T(8,128)}, u32[]{:S(2)}) copy-start(f32[64,128,128]{2,1,0:T(8,128)} %copy-done.2) | copy-start | bytes 12582916
  122.4 27.5 %copy-start.10 = (f32[8,1,128,128]{3,2,1,0:T(8,128)S(1)}, f32[8,1,128,128]{3,2,1,0:T(8,128)}, u32[]{:S(2)}) copy-start(f32[8,1,128,128]{3,2,1,0:T(8,128)} %param.14) | copy-start | bytes 1572868
  193.2 41.2 %copy-start.7 = (s32[128,128]{1,0:T(8,128)S(1)}, s32[128,128]{1,0:T(8,128)}, u32[]{:S(2)}) copy-start(s32[128,128]{1,0:T(8,128)} %pattern.3) | copy-start | bytes 196612
  220.6 22.8 %all-to-all-start.12 = ((f32[8,2,8,8,128]{4,3,2,1,0:T(8,128)}), f32[8,2,8,8,128]{4,3,2,1,0:T(8,128)S(1)}, u32[]{:S(2)}, u32[]{:S(2)}) async-start(f32[8,2,8,8,128]{4,3,2,1,0:T(8,128)} %shard_map.109), calls=%async_computation.12 | async-start | bytes 1048576 | tf_op jit(solution)/shard_map/all_to_all | solution.py:580
Sparse Core Ops, SparseCore 0:
  12.1 40.0 all-gather.2
  54.1 84.5 all-gather.4

commit v9 on v8

--- a/solution.py
+++ b/solution.py
@@ -574,7 +574,7 @@
     state, held, left = level_step(4, PR, 1, table, known, forward, upper_inv, panel_u, group=8, fetch=True)
     for level in range(3, 0, -1):
         known = swap(state)
-        state, left = level_step(level, PR, 1, table, known, left, upper_inv, held, group=8)
+        state, left = level_step(level, PR, 1, table, known, left, upper_inv, held, group=16 if level == 3 else 8)
     known = swap(state)
     state = level_step(0, PC, 1, table, known, left, upper_inv, held, both=True, less=forward, group=8)
     full = lax.all_to_all(state, "pcol", 0, 0)

time: 253 us -> 253 us (level)
  no operation moved by 1% of the time
where the time goes in v9:
time: 253 us; the launch traced here: 252 us
  blocking collectives  169 us (67%)
  Pallas kernels  26.4 us (10%)
  waiting for transfers between devices  20.3 us (8%)
  between operations  14.3 us (6%)
  starting transfers between devices  13.7 us (5%)
  local copies, waits for them, and re-layouts  8.07 us (3%)
    all_to_all x10, blocking collectives, local(): swap = lambda x: lax.all_to_all(x, 'prow', 0, 0)  135 us
    all_to_all x1, blocking collectives, local(): columns = lax.all_to_all(split, 'pcol', 0, 0)  20.6 us
    pallas_call x11, Pallas kernels, level_step(): pl.pallas_call(kernel, out_shape=[jax.ShapeDtypeStruct(x, jnp.float32) fo...  16 us
    all_to_all x1, starting transfers between devices, local(): full = lax.all_to_all(state, 'pcol', 0, 0)  13.6 us
    all_to_all x1, blocking collectives, local(): sums = lax.all_to_all(across(table, columns, far_blocks), 'pcol', 0, 0)  13.1 us
    all_gather x1, waiting for transfers between devices, local(): panel_l = lax.all_gather(packed_l, 'pcol', tiled=True)  11.4 us
    all_to_all x1, waiting for transfers between devices, local(): full = lax.all_to_all(state, 'pcol', 0, 0)  8.85 us
    unnamed x28, local copies, waits for them, and re-layouts  6.51 us
  transfers between devices with their start and end apart: 3, of which 2 were waited for; matrix products, arithmetic and copies ran while one was open for 0% of the time, Pallas kernels for 5%

profile of v9, /device:TPU:1, one launch (start us, length us, event | category | flops | bytes accessed | tf_op | source)
XLA Modules:
  0.0 252.5 jit_solution(4625060143527806541)
XLA Ops:
  7.2 0.0 copy-start.13
  7.2 0.0 copy-start.14
  7.2 0.0 all-gather.3.cloned.1.call-start
  7.2 0.0 copy-start.6
  7.2 0.8 copy-done.6
  8.1 0.0 copy-start.9
  8.1 0.0 copy-start.11
  8.1 3.5 %shard_map.95 = (f32[10,128,128]{2,1,0:T(8,128)}, s32[1,128]{1,0:T(1,128)S(1)}) custom-call(s32[128,128]{1,0:T(8,128)S(1)} %copy-done.6, s32[1,128]{1,0:T(1,128)} %bitcast.313, f32[8,16,128,128]{3,2,1,0:T(8,128)} %bitcast.273), custom_call_target="tpu_custom_call" | custom-call | bytes 4194304 | tf_op jit(solution)/shard_map/pallas_call | solution.py:304
  11.6 0.0 copy-start.8
  11.6 0.5 copy-done.8
  12.1 0.0 all-gather.3.cloned.1.call-update
  12.1 0.0 all-gather.5.cloned.1.call-start
  12.2 0.0 copy-done.13
  12.2 0.0 copy-done.14
  12.2 2.6 %shard_map.96.refs_0_.table = s32[16,128]{1,0:T(8,128)} custom-call(s32[128,128]{1,0:T(8,128)} %pattern.3, s32[1,128]{1,0:T(1,128)S(1)} %bitcast.314, s32[1,128]{1,0:T(1,128)S(1)} %bitcast.315, s32[1,128]{1,0:T(1,128)} %copy-done.8), custom_call_target="tpu_custom_call" | custom-call | bytes 4194304 | tf_op jit(solution)/shard_map/pallas_call | solution.py:257
  14.8 0.0 copy-done.9
  14.8 0.0 copy-done.11
  14.8 0.0 copy-start.4
  14.8 0.7 copy-done.4
  15.5 0.9 shard_map.97
  16.5 18.9 %all_to_all.65.refs_1_ = f32[16,8,8,128]{3,2,1,0:T(8,128)S(1)} all-to-all(f32[16,8,8,128]{3,2,1,0:T(8,128)S(1)} %shard_map.97), channel_id=1, replica_groups=mesh['prow'=16,'pcol'=8] {'prow'}, dimensions={0} | all-to-all | bytes 1048576 | tf_op jit(solution)/shard_map/all_to_all | solution.py:555
  35.4 0.0 copy-start.5
  35.4 3.6 %shard_map.100 = (f32[28,128,128]{2,1,0:T(8,128)}, f32[64,128,128]{2,1,0:T(8,128)S(1)}) custom-call(s32[16,128]{1,0:T(8,128)S(1)} %copy-done.4, f32[8,16,128,128]{3,2,1,0:T(8,128)} %bitcast.276, f32[8,128]{1,0:T(8,128)S(1)} %slice_bitcast_fusion.2.refs_2_, f32[8,16,128,128]{3,2,1,0:T(8,128)} %bitcast.274), custom_call_target="tpu_custom_call" | custom-call | bytes 4194304 | tf_op jit(solution)/shard_map/pallas_call | solution.py:369
  39.0 0.0 copy-start.2
  39.0 1.9 copy-done.2
  40.9 0.0 all-gather.5.cloned.1.call-update
  40.9 11.4 %all-gather.3.cloned.1.call-done.refs_4_ = f32[80,128,128]{2,1,0:T(8,128)} async-done(((f32[10,128,128]{2,1,0:T(8,128)}), f32[80,128,128]{2,1,0:T(8,128)}) %all-gather.3.cloned.1.call-update) | async-done | bytes 5242896 | tf_op jit(solution)/shard_map/all_gather | solution.py:557
  52.3 0.0 copy-done.5
  52.3 0.0 copy-start
  52.3 2.5 copy-done
  54.8 0.0 copy-start.1
  54.8 1.2 shard_map.98
  56.0 17.6 %all_to_all.66.refs_1_ = f32[16,8,8,128]{3,2,1,0:T(8,128)S(1)} all-to-all(f32[16,8,8,128]{3,2,1,0:T(8,128)S(1)} %shard_map.98), channel_id=1, replica_groups=mesh['prow'=16,'pcol'=8] {'prow'}, dimensions={0} | all-to-all | bytes 1048576 | tf_op jit(solution)/shard_map/all_to_all | solution.py:555
  73.7 0.0 copy-done.1
  73.7 1.2 shard_map.99
  74.8 13.2 %all_to_all.67.refs_1_ = f32[16,8,8,128]{3,2,1,0:T(8,128)S(1)} all-to-all(f32[16,8,8,128]{3,2,1,0:T(8,128)S(1)} %shard_map.99), channel_id=1, replica_groups=mesh['prow'=16,'pcol'=8] {'prow'}, dimensions={0} | all-to-all | bytes 1048576 | tf_op jit(solution)/shard_map/all_to_all | solution.py:555
  88.1 20.6 %all_to_all.68.known = f32[8,2,8,8,128]{4,3,2,1,0:T(8,128)S(1)} all-to-all(f32[8,2,8,8,128]{4,3,2,1,0:T(8,128)S(1)} %bitcast.311), channel_id=1, replica_groups=mesh['prow'=16,'pcol'=8] {'pcol'}, dimensions={0} | all-to-all | bytes 1048576 | tf_op jit(solution)/shard_map/all_to_all | solution.py:565
  108.8 0.0 copy-done.3
  108.8 0.7 shard_map.101
  109.4 13.1 %all_to_all.69.refs_5_ = f32[8,8,8,128]{3,2,1,0:T(8,128)S(1)} all-to-all(f32[8,8,8,128]{3,2,1,0:T(8,128)S(1)} %shard_map.101), channel_id=1, replica_groups=mesh['prow'=16,'pcol'=8] {'pcol'}, dimensions={0} | all-to-all | bytes 524288 | tf_op jit(solution)/shard_map/all_to_all | solution.py:566
  122.5 0.7 shard_map.102
  123.3 13.5 %all_to_all.70.refs_1_ = f32[16,8,8,128]{3,2,1,0:T(8,128)S(1)} all-to-all(f32[16,8,8,128]{3,2,1,0:T(8,128)S(1)} %shard_map.102), channel_id=1, replica_groups=mesh['prow'=16,'pcol'=8] {'prow'}, dimensions={0} | all-to-all | bytes 1048576 | tf_op jit(solution)/shard_map/all_to_all | solution.py:555
  136.8 0.7 shard_map.103
  137.5 13.2 %all_to_all.71.refs_1_ = f32[16,8,8,128]{3,2,1,0:T(8,128)S(1)} all-to-all(f32[16,8,8,128]{3,2,1,0:T(8,128)S(1)} %shard_map.103), channel_id=1, replica_groups=mesh['prow'=16,'pcol'=8] {'prow'}, dimensions={0} | all-to-all | bytes 1048576 | tf_op jit(solution)/shard_map/all_to_all | solution.py:555
  150.7 0.0 copy-done.10
  150.7 0.7 shard_map.104
  151.5 11.8 %all_to_all.72.refs_1_ = f32[16,8,8,128]{3,2,1,0:T(8,128)S(1)} all-to-all(f32[16,8,8,128]{3,2,1,0:T(8,128)S(1)} %get-tuple-element.75), channel_id=1, replica_groups=mesh['prow'=16,'pcol'=8] {'prow'}, dimensions={0} | all-to-all | bytes 1048576 | tf_op jit(solution)/shard_map/all_to_all | solution.py:555
  163.3 4.8 %shard_map.105 = (f32[16,8,8,128]{3,2,1,0:T(8,128)S(1)}, f32[64,128,128]{2,1,0:T(8,128)S(1)}, f32[8,8,128]{2,1,0:T(8,128)S(1)}) custom-call(s32[16,128]{1,0:T(8,128)S(1)} %copy-done.5, f32[16,8,8,128]{3,2,1,0:T(8,128)S(1)} %all_to_all.72.refs_1_, f32[8,8,128]{2,1,0:T(8,128)S(1)} %get-tuple-element.76.refs_2_.refs_5_, f32[8,128,128]{2,1,0:T(8,128)S(1)} %bitcast.286, ...), custom_call_target="tpu_custom_call" | custom-call | bytes 8388608 | tf_op jit(solution)/shard_map/pallas_call | solution.py:505
  168.1 11.8 %all_to_all.73.refs_1_ = f32[16,8,8,128]{3,2,1,0:T(8,128)S(1)} all-to-all(f32[16,8,8,128]{3,2,1,0:T(8,128)S(1)} %get-tuple-element.78), channel_id=1, replica_groups=mesh['prow'=16,'pcol'=8] {'prow'}, dimensions={0} | all-to-all | bytes 1048576 | tf_op jit(solution)/shard_map/all_to_all | solution.py:555
  179.9 1.1 shard_map.106
  181.0 11.7 %all_to_all.74.refs_1_ = f32[16,8,8,128]{3,2,1,0:T(8,128)S(1)} all-to-all(f32[16,8,8,128]{3,2,1,0:T(8,128)S(1)} %get-tuple-element.81), channel_id=1, replica_groups=mesh['prow'=16,'pcol'=8] {'prow'}, dimensions={0} | all-to-all | bytes 1048576 | tf_op jit(solution)/shard_map/all_to_all | solution.py:555
  192.7 1.2 shard_map.107
  193.9 0.0 copy-start.7
  193.9 11.8 %all_to_all.75.refs_1_ = f32[16,8,8,128]{3,2,1,0:T(8,128)S(1)} all-to-all(f32[16,8,8,128]{3,2,1,0:T(8,128)S(1)} %get-tuple-element.83), channel_id=1, replica_groups=mesh['prow'=16,'pcol'=8] {'prow'}, dimensions={0} | all-to-all | bytes 1048576 | tf_op jit(solution)/shard_map/all_to_all | solution.py:555
  205.7 1.5 shard_map.108
  207.2 11.7 %all_to_all.76.refs_1_ = f32[16,8,8,128]{3,2,1,0:T(8,128)S(1)} all-to-all(f32[16,8,8,128]{3,2,1,0:T(8,128)S(1)} %get-tuple-element.85), channel_id=1, replica_groups=mesh['prow'=16,'pcol'=8] {'prow'}, dimensions={0} | all-to-all | bytes 1048576 | tf_op jit(solution)/shard_map/all_to_all | solution.py:555
  218.8 2.0 shard_map.109
  220.8 13.6 %all-to-all-start.12 = ((f32[8,2,8,8,128]{4,3,2,1,0:T(8,128)}), f32[8,2,8,8,128]{4,3,2,1,0:T(8,128)S(1)}, u32[]{:S(2)}, u32[]{:S(2)}) async-start(f32[8,2,8,8,128]{4,3,2,1,0:T(8,128)} %shard_map.109), calls=%async_computation.12 | async-start | bytes 1048576 | tf_op jit(solution)/shard_map/all_to_all | solution.py:580
  234.4 0.6 slice.19
  235.0 0.0 copy-done.7
  235.0 0.1 copy.74
  235.1 8.8 %all-to-all-done.12 = f32[8,2,8,8,128]{4,3,2,1,0:T(8,128)S(1)} async-done(((f32[8,2,8,8,128]{4,3,2,1,0:T(8,128)}), f32[8,2,8,8,128]{4,3,2,1,0:T(8,128)S(1)}, u32[]{:S(2)}, u32[]{:S(2)}) %all-to-all-start.12) | async-done | bytes 524320 | tf_op jit(solution)/shard_map/all_to_all | solution.py:580
  244.0 0.8 copy_bitcast_fusion.1
  244.8 0.8 while.11
  (6 shorter events, 0.1 us)
Async XLA Ops:
  7.2 5.0 %copy-start.13 = (s32[128]{0:T(128)S(1)}, s32[128]{0:T(128)}, u32[]{:S(2)}) copy-start(s32[128]{0:T(128)} %param.16) | copy-start | bytes 1540
  7.2 5.0 %copy-start.14 = (s32[128]{0:T(128)S(1)}, s32[128]{0:T(128)}, u32[]{:S(2)}) copy-start(s32[128]{0:T(128)} %param.17) | copy-start | bytes 1540
  7.2 45.2 %all-gather.3.cloned.1.call-start = ((), (), s32[]{:S(2)}) async-start(), calls=%async_computation.34 | async-start | bytes 5898240 | tf_op jit(solution)/shard_map/all_gather | solution.py:557
  7.2 0.8 copy-start.6
  8.1 6.8 %copy-start.9 = (f32[8,1,128,128]{3,2,1,0:T(8,128)S(1)}, f32[8,1,128,128]{3,2,1,0:T(8,128)}, u32[]{:S(2)}) copy-start(f32[8,1,128,128]{3,2,1,0:T(8,128)} %param.13) | copy-start | bytes 1572868
  8.1 6.8 %copy-start.11 = (f32[8,1,64,128]{3,2,1,0:T(8,128)S(1)}, f32[8,1,64,128]{3,2,1,0:T(8,128)}, u32[]{:S(2)}) copy-start(f32[8,1,64,128]{3,2,1,0:T(8,128)} %param.10) | copy-start | bytes 786436
  11.6 0.5 copy-start.8
  12.1 151.2 %all-gather.5.cloned.1.call-start = ((), (), s32[]{:S(2)}) async-start(), calls=%async_computation.35 | async-start | bytes 16515072 | tf_op jit(solution)/shard_map/all_gather | solution.py:561
  14.8 0.7 copy-start.4
  35.4 17.0 %copy-start.5 = (s32[16,128]{1,0:T(8,128)S(1)}, s32[16,128]{1,0:T(8,128)}, u32[]{:S(2)}) copy-start(s32[16,128]{1,0:T(8,128)} %shard_map.96.refs_0_.table) | copy-start | bytes 24580
  39.0 2.0 copy-start.2
  52.3 2.5 copy-start
  54.8 18.8 %copy-start.1 = (f32[80,128,128]{2,1,0:T(8,128)S(1)}, f32[80,128,128]{2,1,0:T(8,128)}, u32[]{:S(2)}) copy-start(f32[80,128,128]{2,1,0:T(8,128)} %all-gather.3.cloned.1.call-done.refs_4_) | copy-start | bytes 15728644
  54.8 53.9 %copy-start.3 = (f32[64,128,128]{2,1,0:T(8,128)S(1)}, f32[64,128,128]{2,1,0:T(8,128)}, u32[]{:S(2)}) copy-start(f32[64,128,128]{2,1,0:T(8,128)} %copy-done.2) | copy-start | bytes 12582916
  122.5 28.2 %copy-start.10 = (f32[8,1,128,128]{3,2,1,0:T(8,128)S(1)}, f32[8,1,128,128]{3,2,1,0:T(8,128)}, u32[]{:S(2)}) copy-start(f32[8,1,128,128]{3,2,1,0:T(8,128)} %param.14) | copy-start | bytes 1572868
  193.9 41.1 %copy-start.7 = (s32[128,128]{1,0:T(8,128)S(1)}, s32[128,128]{1,0:T(8,128)}, u32[]{:S(2)}) copy-start(s32[128,128]{1,0:T(8,128)} %pattern.3) | copy-start | bytes 196612
  220.8 23.1 %all-to-all-start.12 = ((f32[8,2,8,8,128]{4,3,2,1,0:T(8,128)}), f32[8,2,8,8,128]{4,3,2,1,0:T(8,128)S(1)}, u32[]{:S(2)}, u32[]{:S(2)}) async-start(f32[8,2,8,8,128]{4,3,2,1,0:T(8,128)} %shard_map.109), calls=%async_computation.12 | async-start | bytes 1048576 | tf_op jit(solution)/shard_map/all_to_all | solution.py:580
Sparse Core Ops, SparseCore 0:
  12.2 40.0 all-gather.2
  54.1 84.5 all-gather.4
